TPU v7x, 256 devices: a whole 4x4x8 slice. The times are simulated.
256 devices in a mesh: replica: 8 (over x_hi, y), shard: 32 (over x_lo, z, core).
Axes of the slice: x: 4 (x_hi: 2, x_lo: 2; x = x_hi * 2 + x_lo), y: 4, z: 8, core: 2. Of those that a mesh axis runs over, the one named last changes fastest.
Arguments:
- gradients: bfloat16 [8, 32, 512, 4608], P('replica', 'shard'), may hold values from -96 to 96
- master: float32 [512, 4608], P('shard'), may hold values from -0.12 to 0.12
- moment1: float32 [512, 4608], P('shard'), may hold values from -0.6 to 0.6
- moment2: float32 [512, 4608], P('shard'), may hold values from 0.1 to 2
Outputs:
- master_new: float32 [512, 4608], P('shard')
- moment1_new: float32 [512, 4608], P('shard')
- moment2_new: float32 [512, 4608], P('shard')
- params: bfloat16 [512, 4608], replicated
All inputs are finite; a program needn't handle non-finite values.
Results may differ from a plain program's by a relative error of at most 0.0004.
Values may be sent and summed in bfloat16 or wider, within the bound.
No kernel may reach another device: no remote copies, remote signals or barrier semaphores. Data moves between devices by JAX's collectives and lax.ppermute only.
A program may use at most 128 MiB of HBM per device.

v0:
```python
import jax
import jax.numpy as jnp
from jax import lax
from jax.sharding import PartitionSpec as P

STEP = 10


def per_device(gradients, master, moment1, moment2):
    local = gradients[0, 0].astype(jnp.float32)
    n_replica = lax.axis_size("replica")
    n_shard = lax.axis_size("shard")
    partial_rows = lax.psum_scatter(local, "shard", scatter_dimension=0, tiled=True)
    total = lax.psum(partial_rows, "replica")
    grad = total / (n_replica * n_shard)
    moment1_new = 0.9 * moment1 + 0.1 * grad
    moment2_new = 0.95 * moment2 + 0.05 * grad * grad
    first_fix = 1.0 - 0.9**STEP
    second_fix = 1.0 - 0.95**STEP
    update = moment1_new / first_fix / (jnp.sqrt(moment2_new / second_fix) + 1e-08)
    master_new = master * (1.0 - 0.02 * 0.1) - 0.02 * update
    params = lax.all_gather(master_new.astype(jnp.bfloat16), "shard", axis=0, tiled=True)
    return (master_new, moment1_new, moment2_new, params)


def solution(mesh):
    placed = (
        P("replica", "shard", None, None),
        P("shard", None),
        P("shard", None),
        P("shard", None),
    )
    return jax.shard_map(
        per_device,
        mesh=mesh,
        in_specs=placed,
        out_specs=(P("shard", None), P("shard", None), P("shard", None), P()),
        check_vma=False,
    )
```

profile of v0, /device:TPU:1, one launch (start us, length us, event | category | flops | bytes accessed | tf_op | source)
XLA Modules:
  0.0 317.0 jit_solution(16120985455601047730)
XLA Ops:
  7.2 0.0 reduce-scatter.2.cloned.1.call-start
  7.2 7.2 %bitcast_convert_fusion = f32[512,4608]{1,0:T(8,128)} fusion(bf16[1,1,512,4608]{3,2,1,0:T(8,128)(2,1)} %param.4), kind=kLoop, calls=%fused_computation | loop fusion | flops 2359296 | bytes 14155776 | tf_op jit(solution)/shard_map/convert_element_type | solution.py:10
  14.4 0.0 copy-start
  14.4 0.0 copy-start.1
  14.4 0.0 copy-start.2
  14.4 0.0 reduce-scatter.2.cloned.1.call-update
  14.4 0.0 all-reduce.2.cloned.1.call-start
  14.5 131.0 %reduce-scatter.2.cloned.1.call-done = f32[16,4608]{1,0:T(8,128)} async-done(((f32[512,4608]{1,0:T(8,128)}), f32[16,4608]{1,0:T(8,128)}) %reduce-scatter.2.cloned.1.call-update) | async-done | bytes 294928 | tf_op jit(solution)/shard_map/reduce_scatter | solution.py:13
  145.5 0.0 all-reduce.2.cloned.1.call-update
  145.6 0.0 all-gather.2.cloned.1.call-start
  145.6 86.5 %all-reduce.2.cloned.1.call-done = f32[16,4608]{1,0:T(8,128)} async-done(((f32[16,4608]{1,0:T(8,128)}), f32[16,4608]{1,0:T(8,128)}) %all-reduce.2.cloned.1.call-update) | async-done | bytes 294928 | tf_op jit(solution)/shard_map/psum | solution.py:14
  232.1 0.0 copy-done
  232.1 0.0 copy-done.1
  232.1 0.0 copy-done.2
  232.1 2.0 fusion
  234.1 0.0 all-gather.2.cloned.1.call-update
  234.1 71.5 %all-gather.2.cloned.1.call-done = bf16[512,4608]{1,0:T(8,128)(2,1)} async-done(((bf16[16,4608]{1,0:T(8,128)(2,1)}), bf16[512,4608]{1,0:T(8,128)(2,1)}) %all-gather.2.cloned.1.call-update) | async-done | bytes 4718608 | tf_op jit(solution)/shard_map/all_gather | solution.py:22
  305.6 4.8 %copy.10 = bf16[512,4608]{1,0:T(8,128)(2,1)} copy(bf16[512,4608]{1,0:T(8,128)(2,1)} %all-gather.2.cloned.1.call-done) | data formatting | bytes 9437184
Async XLA Ops:
  7.2 138.4 %reduce-scatter.2.cloned.1.call-start = ((), (), s32[]{:S(2)}) async-start(), calls=%async_computation.1 | async-start | bytes 9732096 | tf_op jit(solution)/shard_map/reduce_scatter | solution.py:13
  14.4 217.7 %copy-start = (f32[16,4608]{1,0:T(8,128)S(1)}, f32[16,4608]{1,0:T(8,128)}, u32[]{:S(2)}) copy-start(f32[16,4608]{1,0:T(8,128)} %param.5) | copy-start | bytes 884740
  14.4 217.7 %copy-start.1 = (f32[16,4608]{1,0:T(8,128)S(1)}, f32[16,4608]{1,0:T(8,128)}, u32[]{:S(2)}) copy-start(f32[16,4608]{1,0:T(8,128)} %param.6) | copy-start | bytes 884740
  14.4 217.7 %copy-start.2 = (f32[16,4608]{1,0:T(8,128)S(1)}, f32[16,4608]{1,0:T(8,128)}, u32[]{:S(2)}) copy-start(f32[16,4608]{1,0:T(8,128)} %param.7) | copy-start | bytes 884740
  14.4 217.6 %all-reduce.2.cloned.1.call-start = ((), (), s32[]{:S(2)}) async-start(), calls=%async_computation.2 | async-start | bytes 589824 | tf_op jit(solution)/shard_map/psum | solution.py:14
  145.6 160.0 %all-gather.2.cloned.1.call-start = ((), (), s32[]{:S(2)}) async-start(), calls=%async_computation.3 | async-start | bytes 4866048 | tf_op jit(solution)/shard_map/all_gather | solution.py:22
Sparse Core Ops, SparseCore 0:
  14.6 130.9 reduce-scatter.1
  148.2 83.8 all-reduce.1
  234.7 70.9 all-gather.1
where the time goes:
time: 317 us
  waiting for transfers between devices  289 us (91%)
  between operations  13.7 us (4%)
  other arithmetic  9.24 us (3%)
  local copies, waits for them, and re-layouts  4.84 us (2%)
    reduce_scatter x1, waiting for transfers between devices, per_device(): lax.psum_scatter(local, 'shard', scatter_dimension=0, tiled=True)  131 us
    psum x1, waiting for transfers between devices, per_device(): total = lax.psum(partial_rows, 'replica')  86.5 us
    all_gather x1, waiting for transfers between devices, per_device(): lax.all_gather(master_new.astype(jnp.bfloat16), 'shard', axis=0, tiled=True)  71.5 us
    convert_element_type x1, other arithmetic, per_device(): local = gradients[0, 0].astype(jnp.float32)  7.19 us
  transfers between devices with their start and end apart: 3, of which 3 were waited for; matrix products, arithmetic and copies ran while one was open for 0% of the time, Pallas kernels for 0%

commit v1 on v0

v1 whole, which is shorter than its diff:
```python
import jax
import jax.numpy as jnp
from jax import lax
from jax.sharding import Mesh, PartitionSpec as P

STEP = 10
PLANE = ("xh", "y", "xl")
SWAP = [(0, 1), (1, 0)]


def adam(grad, master, moment1, moment2):
    moment1_new = 0.9 * moment1 + 0.1 * grad
    moment2_new = 0.95 * moment2 + 0.05 * grad * grad
    first_fix = 1.0 - 0.9**STEP
    second_fix = 1.0 - 0.95**STEP
    update = moment1_new / first_fix / (jnp.sqrt(moment2_new / second_fix) + 1e-08)
    master_new = master * (1.0 - 0.02 * 0.1) - 0.02 * update
    return master_new, moment1_new, moment2_new


def gather(piece, axes, n):
    return lax.all_to_all(jnp.broadcast_to(piece, (n, *piece.shape)), axes, 0, 0, tiled=True)


def per_device(gradients, master, moment1, moment2):
    xh, y, core = (lax.axis_index(a) for a in ("xh", "y", "c"))
    n_xh, n_y, n_xl, n_z = (lax.axis_size(a) for a in ("xh", "y", "xl", "z"))
    rows, width = gradients.shape[2:]
    own = master.shape[0]
    low, cols = own // n_xh, width // n_y
    blocks = n_xl * n_z
    plane = n_xh * n_y * n_xl
    local = gradients.reshape(blocks, 2, own, width)

    mine = lax.dynamic_index_in_dim(local, core, 1, keepdims=False)
    theirs = lax.dynamic_index_in_dim(local, 1 - core, 1, keepdims=False)
    came = lax.ppermute(theirs, "c", SWAP)
    pair = (mine.astype(jnp.float32) + came.astype(jnp.float32)).astype(jnp.float16)
    pair = pair.reshape(n_xl, n_z, n_xh, low, n_y, cols).transpose(2, 4, 0, 1, 3, 5)
    pair = pair.reshape(plane, n_z, low, cols)

    pair = lax.all_to_all(pair, PLANE, 0, 0, tiled=True)
    column = jnp.sum(pair.astype(jnp.float32), axis=0).astype(jnp.float16)
    column = lax.all_to_all(column, "z", 0, 0, tiled=True)
    grad = jnp.sum(column.astype(jnp.float32), axis=0) / (plane * n_z * 2)

    def piece(state):
        state = state.reshape(n_xh, low, n_y, cols)
        return lax.dynamic_index_in_dim(
            lax.dynamic_index_in_dim(state, xh, 0, keepdims=False), y, 1, keepdims=False
        )

    part = adam(grad, piece(master), piece(moment1), piece(moment2))[0].astype(jnp.bfloat16)
    part = gather(part, "z", n_z)
    part = gather(part, PLANE, plane)
    part = part.reshape(n_xh, n_y, n_xl, n_z, low, cols).transpose(2, 3, 0, 4, 1, 5)
    part = part.reshape(blocks, own, width)
    other = lax.ppermute(part, "c", SWAP)
    first = core == 0
    params = jnp.stack([jnp.where(first, part, other), jnp.where(first, other, part)], axis=1)

    whole = gather(grad, ("xh", "y"), n_xh * n_y)
    whole = whole.reshape(n_xh, n_y, low, cols).transpose(0, 2, 1, 3).reshape(own, width)
    master_new, moment1_new, moment2_new = adam(whole, master, moment1, moment2)
    return master_new, moment1_new, moment2_new, params.reshape(rows, width)


def solution(mesh):
    fine = Mesh(mesh.devices.reshape(2, 4, 2, 8, 2), ("xh", "y", "xl", "z", "c"))
    replica, shard = ("xh", "y"), ("xl", "z", "c")
    state = P(shard, None)
    return jax.shard_map(
        per_device,
        mesh=fine,
        in_specs=(P(replica, shard, None, None), state, state, state),
        out_specs=(state, state, state, P()),
        check_vma=False,
    )
```

time: 317 us -> 140 us (0.44)
  waiting for transfers between devices: 289 us -> 20.7 us
  blocking collectives: 0 us -> 77 us
  starting transfers between devices: 0.12 us -> 19.4 us
  between operations: 13.7 us -> 0.74 us
  local copies, waits for them, and re-layouts: 4.84 us -> 14.1 us
    reduce_scatter x1 -> x0, waiting for transfers between devices: 131 us -> none  [per_device(): lax.psum_scatter(local, 'shard', scatter_dimension=0, tiled=True)]
    psum x1 -> x0, waiting for transfers between devices: 86.5 us -> none  [per_device(): total = lax.psum(partial_rows, 'replica')]
    all_to_all x0 -> x3, blocking collectives: none -> 77 us  [the longest x2 41.5 us: gather(): lax.all_to_all(jnp.broadcast_to(piece, (n, *piece.shape)), axes, 0, 0, ti...]
    all_gather x1 -> x0, waiting for transfers between devices: 71.5 us -> none  [per_device(): lax.all_gather(master_new.astype(jnp.bfloat16), 'shard', axis=0, tiled=True)]
    all_to_all x0 -> x2, waiting for transfers between devices: none -> 16.4 us  [the longest x1 8.28 us: gather(): lax.all_to_all(jnp.broadcast_to(piece, (n, *piece.shape)), axes, 0, 0, ti...]
    all_to_all x0 -> x2, starting transfers between devices: none -> 11.6 us  [the longest x1 8.19 us: per_device(): column = lax.all_to_all(column, 'z', 0, 0, tiled=True)]
    ppermute x0 -> x2, starting transfers between devices: none -> 7.78 us  [the longest x1 4.45 us: per_device(): other = lax.ppermute(part, 'c', SWAP)]
    convert_element_type x2 -> x3, other arithmetic: 9.24 us -> 3.8 us  [the longest x1 3.07 us: per_device(): (mine.astype(jnp.float32) + came.astype(jnp.float32)).astype(jnp.float16)]
  transfers between devices with their start and end apart: 3 -> 4, of which waited for: 3 -> 3; matrix products, arithmetic and copies ran while one was open for 0% -> 1% of each run, Pallas kernels for 0% -> 0%
where the time goes in v1:
time: 140 us; the launch traced here: 139 us
  blocking collectives  77 us (55%)
  waiting for transfers between devices  20.7 us (15%)
  starting transfers between devices  19.4 us (14%)
  local copies, waits for them, and re-layouts  14.1 us (10%)
  other arithmetic  7.57 us (5%)
    all_to_all x2, blocking collectives, gather(): lax.all_to_all(jnp.broadcast_to(piece, (n, *piece.shape)), axes, 0, 0, ti...  41.5 us
    all_to_all x1, blocking collectives, per_device(): pair = lax.all_to_all(pair, PLANE, 0, 0, tiled=True)  35.5 us
    all_to_all x1, waiting for transfers between devices, gather(): lax.all_to_all(jnp.broadcast_to(piece, (n, *piece.shape)), axes, 0, 0, ti...  8.28 us
    all_to_all x1, starting transfers between devices, per_device(): column = lax.all_to_all(column, 'z', 0, 0, tiled=True)  8.19 us
    all_to_all x1, waiting for transfers between devices, per_device(): column = lax.all_to_all(column, 'z', 0, 0, tiled=True)  8.13 us
    ppermute x1, starting transfers between devices, per_device(): other = lax.ppermute(part, 'c', SWAP)  4.45 us
    ppermute x1, waiting for transfers between devices, per_device(): came = lax.ppermute(theirs, 'c', SWAP)  4.29 us
    all_to_all x1, starting transfers between devices, gather(): lax.all_to_all(jnp.broadcast_to(piece, (n, *piece.shape)), axes, 0, 0, ti...  3.42 us
  transfers between devices with their start and end apart: 4, of which 3 were waited for; matrix products, arithmetic and copies ran while one was open for 1% of the time, Pallas kernels for 0%

profile of v1, /device:TPU:1, one launch (start us, length us, event | category | flops | bytes accessed | tf_op | source)
XLA Modules:
  0.0 139.5 jit_solution(914581075137272862)
XLA Ops:
  0.6 1.8 %dynamic-slice_bitcast_fusion = bf16[16,16,4608]{2,1,0:T(8,128)(2,1)S(1)} fusion(bf16[16,2,16,4608]{3,2,1,0:T(8,128)(2,1)} %bitcast.57, s32[]{:T(128)S(6)} %select_n.36), kind=kLoop, calls=%fused_computation.6 | loop fusion | bytes 4718596 | tf_op jit(solution)/shard_map/jit(dynamic_index_in_dim)/squeeze | solution.py:36
  2.5 3.3 %collective-permute-start = (bf16[16,16,4608]{2,1,0:T(8,128)(2,1)S(1)}, bf16[16,16,4608]{2,1,0:T(8,128)(2,1)}, u32[]{:S(2)}, u32[]{:S(2)}) collective-permute-start(bf16[16,16,4608]{2,1,0:T(8,128)(2,1)S(1)} %dynamic-slice_bitcast_fusion), channel_id=1, source_target_pairs={{0,1},{1,0},{2,3},{3,2},{4,5},{5,4},{6,7},{7,6},{8,9},{9,8},{10,11... | collective-permute-start | bytes 7077896 | tf_op jit(solution)/shard_map/ppermute | solution.py:37
  5.8 4.3 %collective-permute-done = bf16[16,16,4608]{2,1,0:T(8,128)(2,1)} collective-permute-done((bf16[16,16,4608]{2,1,0:T(8,128)(2,1)S(1)}, bf16[16,16,4608]{2,1,0:T(8,128)(2,1)}, u32[]{:S(2)}, u32[]{:S(2)}) %collective-permute-start) | collective-permute-done | bytes 2359328 | tf_op jit(solution)/shard_map/ppermute | solution.py:37
  10.1 3.1 %fusion = f16[16,16,4608]{2,1,0:T(8,128)(2,1)S(1)} fusion(bf16[16,16,4608]{2,1,0:T(8,128)(2,1)} %collective-permute-done, bf16[16,2,16,4608]{3,2,1,0:T(8,128)(2,1)} %bitcast.58, s32[]{:T(128)S(6)} %select_n.35), kind=kLoop, calls=%fused_computation.2 | loop fusion | flops 4718592 | bytes 7077892 | tf_op jit(solution)/shard_map/convert_element_type | solution.py:38
  13.2 2.3 %reshape.56 = f16[2,8,2,8,4,1152]{5,4,3,2,1,0:T(4,128)(2,1)} reshape(f16[16,16,4608]{2,1,0:T(8,128)(2,1)S(1)} %fusion) | data formatting | bytes 4718592 | tf_op jit(solution)/shard_map/reshape | solution.py:39
  15.4 2.3 %copy.18 = f16[2,4,2,8,8,1152]{5,4,3,2,1,0:T(8,128)(2,1)S(1)} copy(f16[2,4,2,8,8,1152]{5,1,4,0,3,2:T(4,128)(2,1)} %bitcast.54) | data formatting | bytes 4718592 | tf_op jit(solution)/shard_map/transpose | solution.py:39
  17.7 35.5 %all_to_all.25 = f16[16,8,8,1152]{3,2,1,0:T(8,128)(2,1)S(1)} all-to-all(f16[16,8,8,1152]{3,2,1,0:T(8,128)(2,1)S(1)} %bitcast.55), channel_id=1, replica_groups=mesh['xh'=2,'y'=4,'xl'=2,'z'=8,'c'=2] {'xh','y','xl'}, dimensions={0} | all-to-all | bytes 4718592 | tf_op jit(solution)/shard_map/all_to_all | solution.py:42
  53.2 0.3 convert_reduce_fusion
  53.5 0.7 convert_element_type.29
  54.2 8.2 %all-to-all-start.1 = ((f16[8,8,1152]{2,1,0:T(8,128)(2,1)}), f16[8,8,1152]{2,1,0:T(8,128)(2,1)S(1)}, u32[]{:S(2)}, u32[]{:S(2)}) async-start(f16[8,8,1152]{2,1,0:T(8,128)(2,1)} %convert_element_type.29), calls=%async_computation.1 | async-start | bytes 294912 | tf_op jit(solution)/shard_map/all_to_all | solution.py:44
  62.4 8.1 %all-to-all-done.1 = f16[8,8,1152]{2,1,0:T(8,128)(2,1)S(1)} async-done(((f16[8,8,1152]{2,1,0:T(8,128)(2,1)}), f16[8,8,1152]{2,1,0:T(8,128)(2,1)S(1)}, u32[]{:S(2)}, u32[]{:S(2)}) %all-to-all-start.1) | async-done | bytes 147488 | tf_op jit(solution)/shard_map/all_to_all | solution.py:44
  70.6 10.5 %all_to_all.26 = bf16[8,8,1152]{2,1,0:T(8,128)(2,1)S(1)} all-to-all(bf16[8,8,1152]{2,1,0:T(8,128)(2,1)S(1)} %broadcast_in_dim.10), channel_id=1, replica_groups=mesh['xh'=2,'y'=4,'xl'=2,'z'=8,'c'=2] {'z'}, dimensions={0} | all-to-all | bytes 294912 | tf_op jit(solution)/shard_map/all_to_all | solution.py:22
  81.1 0.3 broadcast_in_dim.11
  81.4 31.0 %all_to_all.27 = bf16[16,8,8,1152]{3,2,1,0:T(8,128)(2,1)S(1)} all-to-all(bf16[16,8,8,1152]{3,2,1,0:T(8,128)(2,1)S(1)} %broadcast_in_dim.11), channel_id=1, replica_groups=mesh['xh'=2,'y'=4,'xl'=2,'z'=8,'c'=2] {'xh','y','xl'}, dimensions={0} | all-to-all | bytes 4718592 | tf_op jit(solution)/shard_map/all_to_all | solution.py:22
  112.4 1.8 %copy.19 = bf16[2,8,2,8,4,1152]{5,4,3,2,1,0:T(4,128)(2,1)S(1)} copy(bf16[2,8,2,8,4,1152]{5,3,1,0,4,2:T(8,128)(2,1)S(1)} %bitcast.56) | data formatting | bytes 4718592 | tf_op jit(solution)/shard_map/transpose | solution.py:56
  114.3 2.4 %reshape.64 = bf16[16,16,4608]{2,1,0:T(8,128)(2,1)} reshape(bf16[2,8,2,8,4,1152]{5,4,3,2,1,0:T(4,128)(2,1)S(1)} %copy.19) | data formatting | bytes 4718592 | tf_op jit(solution)/shard_map/reshape | solution.py:57
  116.6 4.5 %collective-permute-start.1 = (bf16[16,16,4608]{2,1,0:T(8,128)(2,1)}, bf16[16,16,4608]{2,1,0:T(8,128)(2,1)}, u32[]{:S(2)}, u32[]{:S(2)}) collective-permute-start(bf16[16,16,4608]{2,1,0:T(8,128)(2,1)} %reshape.64), channel_id=1, source_target_pairs={{0,1},{1,0},{2,3},{3,2},{4,5},{5,4},{6,7},{7,6},{8,9},{9,8},{10,11... | collective-permute-start | bytes 7077896 | tf_op jit(solution)/shard_map/ppermute | solution.py:58
  121.1 0.7 broadcast_in_dim.9
  121.8 3.4 %all-to-all-start.2 = ((f32[8,8,1152]{2,1,0:T(8,128)}), f32[8,8,1152]{2,1,0:T(8,128)S(1)}, u32[]{:S(2)}, u32[]{:S(2)}) async-start(f32[8,8,1152]{2,1,0:T(8,128)} %broadcast_in_dim.9), calls=%async_computation.2 | async-start | bytes 589824 | tf_op jit(solution)/shard_map/all_to_all | solution.py:22
  125.2 8.3 %all-to-all-done.2 = f32[8,8,1152]{2,1,0:T(8,128)S(1)} async-done(((f32[8,8,1152]{2,1,0:T(8,128)}), f32[8,8,1152]{2,1,0:T(8,128)S(1)}, u32[]{:S(2)}, u32[]{:S(2)}) %all-to-all-start.2) | async-done | bytes 294944 | tf_op jit(solution)/shard_map/all_to_all | solution.py:22
  133.5 1.0 multiply_subtract_fusion
  134.6 2.0 %select_bitcast_fusion.1 = (bf16[16,1,16,4608]{3,2,0,1:T(8,128)(2,1)S(1)}, bf16[16,1,16,4608]{3,2,0,1:T(8,128)(2,1)S(1)}) fusion(bf16[16,16,4608]{2,1,0:T(8,128)(2,1)S(1)} %copy-done, bf16[16,16,4608]{2,1,0:T(8,128)(2,1)} %collective-permute-done.1, pred[]{:T(512)S(6)} %eq.3), kind=kLoop, calls=%fused_computation.5 | loop fusion | flops 2359296 | bytes 9437185 | tf_op jit(solution)/shard_map/stack | solution.py:60
  136.5 0.4 pad_maximum_fusion
  137.0 2.5 %copy.20 = bf16[16,2,16,4608]{3,2,1,0:T(8,128)(2,1)} copy(bf16[16,2,16,4608]{3,2,0,1:T(8,128)(2,1)S(1)} %pad_maximum_fusion) | data formatting | bytes 9437184 | tf_op jit(solution)/shard_map/stack | solution.py:60
  (12 shorter events, 0.1 us)
Async XLA Ops:
  2.5 7.6 %collective-permute-start = (bf16[16,16,4608]{2,1,0:T(8,128)(2,1)S(1)}, bf16[16,16,4608]{2,1,0:T(8,128)(2,1)}, u32[]{:S(2)}, u32[]{:S(2)}) collective-permute-start(bf16[16,16,4608]{2,1,0:T(8,128)(2,1)S(1)} %dynamic-slice_bitcast_fusion), channel_id=1, source_target_pairs={{0,1},{1,0},{2,3},{3,2},{4,5},{5,4},{6,7},{7,6},{8,9},{9,8},{10,11... | collective-permute-start | bytes 7077896 | tf_op jit(solution)/shard_map/ppermute | solution.py:37
  53.2 17.3 %copy-start.1 = (f32[16,4608]{1,0:T(8,128)S(1)}, f32[16,4608]{1,0:T(8,128)}, u32[]{:S(2)}) copy-start(f32[16,4608]{1,0:T(8,128)} %param.5) | copy-start | bytes 884740
  53.2 17.3 %copy-start.2 = (f32[16,4608]{1,0:T(8,128)S(1)}, f32[16,4608]{1,0:T(8,128)}, u32[]{:S(2)}) copy-start(f32[16,4608]{1,0:T(8,128)} %param.7) | copy-start | bytes 884740
  53.2 17.4 %copy-start.3 = (f32[16,4608]{1,0:T(8,128)S(1)}, f32[16,4608]{1,0:T(8,128)}, u32[]{:S(2)}) copy-start(f32[16,4608]{1,0:T(8,128)} %param.6) | copy-start | bytes 884740
  54.2 16.3 %all-to-all-start.1 = ((f16[8,8,1152]{2,1,0:T(8,128)(2,1)}), f16[8,8,1152]{2,1,0:T(8,128)(2,1)S(1)}, u32[]{:S(2)}, u32[]{:S(2)}) async-start(f16[8,8,1152]{2,1,0:T(8,128)(2,1)} %convert_element_type.29), calls=%async_computation.1 | async-start | bytes 294912 | tf_op jit(solution)/shard_map/all_to_all | solution.py:44
  116.6 17.9 %copy-start = (bf16[16,16,4608]{2,1,0:T(8,128)(2,1)S(1)}, bf16[16,16,4608]{2,1,0:T(8,128)(2,1)}, u32[]{:S(2)}) copy-start(bf16[16,16,4608]{2,1,0:T(8,128)(2,1)} %reshape.64) | copy-start | bytes 7077892
  116.6 17.9 %collective-permute-start.1 = (bf16[16,16,4608]{2,1,0:T(8,128)(2,1)}, bf16[16,16,4608]{2,1,0:T(8,128)(2,1)}, u32[]{:S(2)}, u32[]{:S(2)}) collective-permute-start(bf16[16,16,4608]{2,1,0:T(8,128)(2,1)} %reshape.64), channel_id=1, source_target_pairs={{0,1},{1,0},{2,3},{3,2},{4,5},{5,4},{6,7},{7,6},{8,9},{9,8},{10,11... | collective-permute-start | bytes 7077896 | tf_op jit(solution)/shard_map/ppermute | solution.py:58
  121.8 11.7 %all-to-all-start.2 = ((f32[8,8,1152]{2,1,0:T(8,128)}), f32[8,8,1152]{2,1,0:T(8,128)S(1)}, u32[]{:S(2)}, u32[]{:S(2)}) async-start(f32[8,8,1152]{2,1,0:T(8,128)} %broadcast_in_dim.9), calls=%async_computation.2 | async-start | bytes 589824 | tf_op jit(solution)/shard_map/all_to_all | solution.py:22

commit v2 on v0

v2 whole, which is shorter than its diff:
```python
import jax
import jax.numpy as jnp
from jax import lax
from jax.experimental import pallas as pl
from jax.experimental.pallas import tpu as pltpu
from jax.sharding import Mesh, PartitionSpec as P

STEP = 10
XH, Y, XL, Z, CORES = 2, 4, 2, 8, 2
PLANE = ("xh", "y", "xl")
SWAP = [(0, 1), (1, 0)]
OWN = 16
PIECE = 384
LEFT, RIGHT = XH * Y, Y
BLOCKS = XL * Z
VMEM = pl.BlockSpec(memory_space=pltpu.VMEM)
ANY = pl.BlockSpec(memory_space=pl.ANY)


def columns(i):
    return pl.ds(i * PIECE, PIECE)


def views(whole, left, right, core):
    pairs = [(whole.at[:, core, :, columns(i)], left.at[i]) for i in range(LEFT)]
    for y in range(RIGHT):
        for xl in range(XL):
            block = whole.at[pl.ds(xl * Z, Z), core, :, columns(LEFT + y)]
            pairs.append((block, right.at[:, y, xl]))
    return pairs


N_VIEWS = LEFT + RIGHT * XL
LEFT_SHAPE = (LEFT, BLOCKS, OWN, PIECE)
RIGHT_SHAPE = (Z, RIGHT, XL, OWN, PIECE)


def run(copies):
    for copy in copies:
        copy.start()
    for copy in copies:
        copy.wait()


def split_mine_kernel(whole, left, right, sems):
    pairs = views(whole, left, right, lax.axis_index("c"))
    run([pltpu.make_async_copy(a, b, sems.at[k]) for k, (a, b) in enumerate(pairs)])


def split_theirs_kernel(whole, left, right, sems):
    pairs = views(whole, left, right, 1 - lax.axis_index("c"))
    run([pltpu.make_async_copy(a, b, sems.at[k]) for k, (a, b) in enumerate(pairs)])


def split(kernel, name, grad):
    return pl.pallas_call(
        kernel,
        out_shape=[pltpu.VMEM(s, grad.dtype) for s in (LEFT_SHAPE, RIGHT_SHAPE)],
        in_specs=[ANY],
        out_specs=[ANY] * 2,
        scratch_shapes=[pltpu.SemaphoreType.DMA((N_VIEWS,))],
        cost_estimate=pl.CostEstimate(flops=0, bytes_accessed=2 * grad.size, transcendentals=0),
        name=name,
    )(grad)


def place_mine_kernel(left, right, out, sems):
    pairs = views(out, left, right, lax.axis_index("c"))
    run([pltpu.make_async_copy(b, a, sems.at[k]) for k, (a, b) in enumerate(pairs)])


def place_theirs_kernel(half, left, right, out, sems):
    pairs = views(out, left, right, 1 - lax.axis_index("c"))
    run([pltpu.make_async_copy(b, a, sems.at[k]) for k, (a, b) in enumerate(pairs)])


def in_vmem(a):
    return pltpu.with_memory_space_constraint(a, pltpu.VMEM)


def place(kernel, name, left, right, half=()):
    shape = jax.ShapeDtypeStruct((BLOCKS, CORES, OWN, (LEFT + RIGHT) * PIECE), left.dtype)
    return pl.pallas_call(
        kernel,
        out_shape=shape,
        in_specs=[ANY] * (len(half) + 2),
        out_specs=ANY,
        scratch_shapes=[pltpu.SemaphoreType.DMA((N_VIEWS,))],
        input_output_aliases={0: 0} if half else {},
        cost_estimate=pl.CostEstimate(flops=0, bytes_accessed=6 * left.size, transcendentals=0),
        name=name,
    )(*half, in_vmem(left), in_vmem(right))


def join_kernel(*refs):
    out, sems, z = refs[Z], refs[Z + 1], lax.axis_index("z")
    run([pltpu.make_async_copy(refs[d], out.at[lax.rem(z - d + Z, Z)], sems.at[d]) for d in range(Z)])


def join(arrays):
    size = Z * arrays[0].size
    return pl.pallas_call(
        join_kernel,
        out_shape=pltpu.VMEM((Z, *arrays[0].shape), arrays[0].dtype),
        in_specs=[ANY] * Z,
        out_specs=ANY,
        scratch_shapes=[pltpu.SemaphoreType.DMA((Z,))],
        cost_estimate=pl.CostEstimate(flops=0, bytes_accessed=4 * size, transcendentals=0),
        name="join",
    )(*[in_vmem(a) for a in arrays])


def spread_kernel(*refs):
    out, z = refs[Z], lax.axis_index("z")
    for d in range(Z):
        piece = refs[d][...]
        for p in range(out.shape[0]):
            out[p, lax.rem(z - d + Z, Z)] = piece


def spread(pieces):
    shape = (XH * Y * XL, Z, OWN, PIECE)
    return pl.pallas_call(
        spread_kernel,
        out_shape=pltpu.VMEM(shape, pieces[0].dtype),
        in_specs=[VMEM] * Z,
        out_specs=VMEM,
        cost_estimate=pl.CostEstimate(flops=0, bytes_accessed=2 * XH * Y * XL * Z * OWN * PIECE, transcendentals=0),
        name="spread",
    )(*[in_vmem(a) for a in pieces])


def adam(grad, master, moment1, moment2):
    moment1_new = 0.9 * moment1 + 0.1 * grad
    moment2_new = 0.95 * moment2 + 0.05 * grad * grad
    first_fix = 1.0 - 0.9**STEP
    second_fix = 1.0 - 0.95**STEP
    update = moment1_new / first_fix / (jnp.sqrt(moment2_new / second_fix) + 1e-08)
    master_new = master * (1.0 - 0.02 * 0.1) - 0.02 * update
    return master_new, moment1_new, moment2_new


def states_kernel(own, other, master, moment1, moment2, master_new, moment1_new, moment2_new):
    xh, y = lax.axis_index("xh"), lax.axis_index("y")
    for k in range(Y):
        at_y = y ^ k
        grads = [(own[2 * k], Y * xh + at_y), (own[2 * k + 1], LEFT + at_y), (other[k], Y * (1 - xh) + at_y)]
        for grad, i in grads:
            at = (slice(None), pl.ds(pl.multiple_of(i * PIECE, 128), PIECE))
            new = adam(grad, master[at], moment1[at], moment2[at])
            master_new[at], moment1_new[at], moment2_new[at] = new


def states(own, other, master, moment1, moment2):
    return pl.pallas_call(
        states_kernel,
        out_shape=[jax.ShapeDtypeStruct(master.shape, master.dtype)] * 3,
        in_specs=[VMEM] * 5,
        out_specs=[VMEM] * 3,
        cost_estimate=pl.CostEstimate(flops=20 * master.size, bytes_accessed=28 * master.size, transcendentals=master.size),
        name="states",
    )(own, other, master, moment1, moment2)


def exchange(chunks, axes):
    return lax.all_to_all(chunks, axes, 0, 0, tiled=True)


def gather(piece, axes, n):
    return exchange(jnp.broadcast_to(piece, (n, *piece.shape)), axes)


def forward(chunk, d):
    return lax.ppermute(chunk, "z", [(z, (z + d) % Z) for z in range(Z)])


def along_z(piece):
    return [piece] + [forward(piece, d) for d in range(1, Z)]


def add(parts):
    return jnp.sum(parts.astype(jnp.float32), axis=0)


def half_width(a):
    return a.astype(jnp.float16)


def per_device(gradients, master, moment1, moment2):
    xh, y, z = (lax.axis_index(a) for a in ("xh", "y", "z"))
    rows, width = gradients.shape[2:]
    plane = XH * Y * XL
    local = gradients.reshape(BLOCKS, CORES, OWN, width)

    def ahead(chunks, d):
        return lax.dynamic_index_in_dim(chunks, lax.rem(z + d, Z), 0, keepdims=False)

    def sum_along_z(chunk_of):
        total = chunk_of(0).astype(jnp.float32)
        for d in range(1, Z):
            total = total + forward(chunk_of(d), d).astype(jnp.float32)
        return total

    their_left, their_right = split(split_theirs_kernel, "split_theirs", local)
    came_right = lax.ppermute(their_right, "c", SWAP)
    came_left = lax.ppermute(their_left, "c", SWAP)
    my_left, my_right = split(split_mine_kernel, "split_mine", local)

    def right_chunk(d):
        return half_width(ahead(my_right, d).astype(jnp.float32) + ahead(came_right, d).astype(jnp.float32))

    right = half_width(sum_along_z(right_chunk))
    left = half_width(my_left.astype(jnp.float32) + came_left.astype(jnp.float32))
    left = half_width(add(exchange(left.reshape(plane, Z, OWN, PIECE), PLANE)))
    left = sum_along_z(lambda d: ahead(left, d))
    right = jnp.broadcast_to(right, (XH, *right.shape)).reshape(plane, OWN, PIECE)
    right = add(exchange(right, PLANE))
    count = plane * Z * CORES
    left, right = left / count, right / count

    def new(grad, i):
        at = [lax.dynamic_slice_in_dim(a, i * PIECE, PIECE, 1) for a in (master, moment1, moment2)]
        return adam(grad, *at)[0].astype(jnp.bfloat16)

    lefts = along_z(new(left, Y * xh + y))
    new_right = gather(new(right, LEFT + y), ("y", "xl"), Y * XL).reshape(Y, XL, OWN, PIECE)
    lefts, new_right = lax.optimization_barrier((lefts, new_right))
    rights = along_z(new_right)
    new_left = exchange(spread(lefts), PLANE).reshape(LEFT_SHAPE)
    new_right = join(rights)

    own = jnp.stack([left, right])
    own = jnp.concatenate([own, lax.ppermute(own, "y", [(i, i ^ 1) for i in range(Y)])])
    own = jnp.concatenate([own, lax.ppermute(own, "y", [(i, i ^ 2) for i in range(Y)])])
    other = lax.ppermute(own.reshape(Y, 2, OWN, PIECE)[:, 0], "xh", SWAP)

    new_left, new_right, other = lax.optimization_barrier((new_left, new_right, other))
    their_right = lax.ppermute(new_right, "c", SWAP)
    their_left = lax.ppermute(new_left, "c", SWAP)
    half = place(place_mine_kernel, "place_mine", new_left, new_right)
    params = place(place_theirs_kernel, "place_theirs", their_left, their_right, (half,))
    master_new, moment1_new, moment2_new = states(own, other, master, moment1, moment2)
    return master_new, moment1_new, moment2_new, params.reshape(rows, width)


def solution(mesh):
    fine = Mesh(mesh.devices.reshape(XH, Y, XL, Z, CORES), ("xh", "y", "xl", "z", "c"))
    replica, shard = ("xh", "y"), ("xl", "z", "c")
    state = P(shard, None)
    return jax.shard_map(
        per_device,
        mesh=fine,
        in_specs=(P(replica, shard, None, None), state, state, state),
        out_specs=(state, state, state, P()),
        check_vma=False,
    )
```

time: 317 us -> 252 us (0.79)
  waiting for transfers between devices: 289 us -> 36.6 us
  Pallas kernels: 0 us -> 106 us
  starting transfers between devices: 0.12 us -> 98.1 us
  between operations: 13.7 us -> 1.06 us
  local copies, waits for them, and re-layouts: 4.84 us -> 1.4 us
    reduce_scatter x1 -> x0, waiting for transfers between devices: 131 us -> none  [per_device(): lax.psum_scatter(local, 'shard', scatter_dimension=0, tiled=True)]
    pallas_call x0 -> x7, Pallas kernels: none -> 106 us  [the longest x2 50.8 us: split(): pl.pallas_call(kernel, out_shape=[pltpu.VMEM(s, grad.dtype) for s in (LEF...]
    psum x1 -> x0, waiting for transfers between devices: 86.5 us -> none  [per_device(): total = lax.psum(partial_rows, 'replica')]
    ppermute x0 -> x35, starting transfers between devices: none -> 75.2 us  [the longest x28 52.6 us: forward(): return lax.ppermute(chunk, 'z', [(z, (z + d) % Z) for z in range(Z)])]
    all_gather x1 -> x0, waiting for transfers between devices: 71.5 us -> none  [per_device(): lax.all_gather(master_new.astype(jnp.bfloat16), 'shard', axis=0, tiled=True)]
    ppermute x0 -> x35, waiting for transfers between devices: none -> 36.6 us  [the longest x28 19.9 us: forward(): return lax.ppermute(chunk, 'z', [(z, (z + d) % Z) for z in range(Z)])]
    all_to_all x0 -> x4, starting transfers between devices: none -> 22.9 us  [exchange(): return lax.all_to_all(chunks, axes, 0, 0, tiled=True)]
    unnamed x7 -> x4, local copies, waits for them, and re-layouts: 4.84 us -> 0.01 us
  transfers between devices with their start and end apart: 3 -> 39, of which waited for: 3 -> 14; matrix products, arithmetic and copies ran while one was open for 0% -> 1% of each run, Pallas kernels for 0% -> 3%
where the time goes in v2:
time: 252 us; the launch traced here: 250 us
  Pallas kernels  106 us (42%)
  starting transfers between devices  98.1 us (39%)
  waiting for transfers between devices  36.6 us (15%)
  other arithmetic  6.65 us (3%)
    ppermute x28, starting transfers between devices, forward(): return lax.ppermute(chunk, 'z', [(z, (z + d) % Z) for z in range(Z)])  52.6 us
    pallas_call x2, Pallas kernels, split(): pl.pallas_call(kernel, out_shape=[pltpu.VMEM(s, grad.dtype) for s in (LEF...  50.8 us
    pallas_call x2, Pallas kernels, place(): pl.pallas_call(kernel, out_shape=shape, in_specs=[ANY] * (len(half) + 2),...  50.4 us
    all_to_all x4, starting transfers between devices, exchange(): return lax.all_to_all(chunks, axes, 0, 0, tiled=True)  22.9 us
    ppermute x28, waiting for transfers between devices, forward(): return lax.ppermute(chunk, 'z', [(z, (z + d) % Z) for z in range(Z)])  19.9 us
    ppermute x1, starting transfers between devices, per_device(): their_left = lax.ppermute(new_left, 'c', SWAP)  11.2 us
    ppermute x1, waiting for transfers between devices, per_device(): lax.ppermute(own, 'y', [(i, i ^ 2) for i in range(Y)])  7.85 us
    convert_element_type x4, other arithmetic, half_width(): return a.astype(jnp.float16)  5.47 us
  transfers between devices with their start and end apart: 39, of which 14 were waited for; matrix products, arithmetic and copies ran while one was open for 1% of the time, Pallas kernels for 3%

profile of v2, /device:TPU:1, one launch (start us, length us, event | category | flops | bytes accessed | tf_op | source)
XLA Modules:
  0.0 249.9 jit_solution(15101850913396989478)
XLA Ops:
  0.6 48.9 %split_theirs.1 = (bf16[8,16,16,384]{3,2,1,0:T(8,128)(2,1)}, bf16[8,4,2,16,384]{4,3,2,1,0:T(8,128)(2,1)S(1)}) custom-call(bf16[16,2,16,4608]{3,2,1,0:T(8,128)(2,1)} %bitcast.62), custom_call_target="tpu_custom_call" | custom-call | bytes 4718592 | tf_op jit(solution)/shard_map/split_theirs/pallas_call | solution.py:56
  49.5 3.3 %collective-permute-start = (bf16[8,16,16,384]{3,2,1,0:T(8,128)(2,1)}, bf16[8,16,16,384]{3,2,1,0:T(8,128)(2,1)}, u32[]{:S(2)}, u32[]{:S(2)}) collective-permute-start(bf16[8,16,16,384]{3,2,1,0:T(8,128)(2,1)} %get-tuple-element.24), channel_id=1, source_target_pairs={{0,1},{1,0},{2,3},{3,2},{4,5},{5,4},{6,7},{7,6},{8,9},{9,8},{10,11... | collective-permute-start | bytes 4718600 | tf_op jit(solution)/shard_map/ppermute | solution.py:206
  56.3 3.0 %add_convert_fusion = f16[8,16,16,384]{3,2,1,0:T(8,128)(2,1)} fusion(bf16[8,16,16,384]{3,2,1,0:T(8,128)(2,1)} %collective-permute-done, bf16[8,16,16,384]{3,2,1,0:T(8,128)(2,1)S(1)} %get-tuple-element.23), kind=kLoop, calls=%fused_computation.1 | loop fusion | flops 3145728 | bytes 4718592 | tf_op jit(solution)/shard_map/convert_element_type | solution.py:186
  59.3 5.0 %all-to-all-start = ((f16[16,8,16,384]{3,2,1,0:T(8,128)(2,1)}), f16[16,8,16,384]{3,2,1,0:T(8,128)(2,1)S(1)}, u32[]{:S(2)}, u32[]{:S(2)}) async-start(f16[16,8,16,384]{3,2,1,0:T(8,128)(2,1)} %bitcast.65), calls=%async_computation | async-start | bytes 3145728 | tf_op jit(solution)/shard_map/all_to_all | solution.py:166
  68.5 3.1 %collective-permute-start.10 = (f16[4,2,16,384]{3,2,1,0:T(8,128)(2,1)S(1)}, f16[4,2,16,384]{3,2,1,0:T(8,128)(2,1)S(1)}, u32[]{:S(2)}, u32[]{:S(2)}) collective-permute-start(f16[4,2,16,384]{3,2,1,0:T(8,128)(2,1)S(1)} %get-tuple-element.50), channel_id=1, source_target_pairs={{0,4},{2,6},{4,8},{6,10},{8,12},{10,14},{12,0},{14,2},{1,5},{3,7},... | collective-permute-start | bytes 294920 | tf_op jit(solution)/shard_map/ppermute | solution.py:174
  71.6 4.7 %collective-permute-start.11 = (f16[4,2,16,384]{3,2,1,0:T(8,128)(2,1)S(1)}, f16[4,2,16,384]{3,2,1,0:T(8,128)(2,1)S(1)}, u32[]{:S(2)}, u32[]{:S(2)}) collective-permute-start(f16[4,2,16,384]{3,2,1,0:T(8,128)(2,1)S(1)} %get-tuple-element.49), channel_id=1, source_target_pairs={{0,6},{2,8},{4,10},{6,12},{8,14},{10,0},{12,2},{14,4},{1,7},{3,9},... | collective-permute-start | bytes 294920 | tf_op jit(solution)/shard_map/ppermute | solution.py:174
  77.2 3.9 %collective-permute-start.13 = (f16[4,2,16,384]{3,2,1,0:T(8,128)(2,1)S(1)}, f16[4,2,16,384]{3,2,1,0:T(8,128)(2,1)S(1)}, u32[]{:S(2)}, u32[]{:S(2)}) collective-permute-start(f16[4,2,16,384]{3,2,1,0:T(8,128)(2,1)S(1)} %get-tuple-element.47), channel_id=1, source_target_pairs={{0,10},{2,12},{4,14},{6,0},{8,2},{10,4},{12,6},{14,8},{1,11},{3,13... | collective-permute-start | bytes 294920 | tf_op jit(solution)/shard_map/ppermute | solution.py:174
  83.5 4.7 %collective-permute-done.11 = f16[4,2,16,384]{3,2,1,0:T(8,128)(2,1)S(1)} collective-permute-done((f16[4,2,16,384]{3,2,1,0:T(8,128)(2,1)S(1)}, f16[4,2,16,384]{3,2,1,0:T(8,128)(2,1)S(1)}, u32[]{:S(2)}, u32[]{:S(2)}) %collective-permute-start.11) | collective-permute-done | bytes 98336 | tf_op jit(solution)/shard_map/ppermute | solution.py:174
  89.0 7.5 %collective-permute-done.14 = f16[4,2,16,384]{3,2,1,0:T(8,128)(2,1)S(1)} collective-permute-done((f16[4,2,16,384]{3,2,1,0:T(8,128)(2,1)S(1)}, f16[4,2,16,384]{3,2,1,0:T(8,128)(2,1)S(1)}, u32[]{:S(2)}, u32[]{:S(2)}) %collective-permute-start.14) | collective-permute-done | bytes 98336 | tf_op jit(solution)/shard_map/ppermute | solution.py:174
  98.2 6.9 %all-to-all-start.1 = ((f16[16,16,384]{2,1,0:T(8,128)(2,1)}), f16[16,16,384]{2,1,0:T(8,128)(2,1)S(1)}, u32[]{:S(2)}, u32[]{:S(2)}) async-start(f16[16,16,384]{2,1,0:T(8,128)(2,1)} %bitcast.19), calls=%async_computation.1 | async-start | bytes 393216 | tf_op jit(solution)/shard_map/all_to_all | solution.py:166
  105.4 3.0 %collective-permute-start.1 = (f16[16,384]{1,0:T(8,128)(2,1)S(1)}, f16[16,384]{1,0:T(8,128)(2,1)S(1)}, u32[]{:S(2)}, u32[]{:S(2)}) collective-permute-start(f16[16,384]{1,0:T(8,128)(2,1)S(1)} %get-tuple-element.52), channel_id=1, source_target_pairs={{0,2},{2,4},{4,6},{6,8},{8,10},{10,12},{12,14},{14,0},{1,3},{3,5},... | collective-permute-start | bytes 36872 | tf_op jit(solution)/shard_map/ppermute | solution.py:174
  109.5 4.3 %collective-permute-start.4 = (f16[16,384]{1,0:T(8,128)(2,1)S(1)}, f16[16,384]{1,0:T(8,128)(2,1)S(1)}, u32[]{:S(2)}, u32[]{:S(2)}) collective-permute-start(f16[16,384]{1,0:T(8,128)(2,1)S(1)} %get-tuple-element.56), channel_id=1, source_target_pairs={{0,8},{2,10},{4,12},{6,14},{8,0},{10,2},{12,4},{14,6},{1,9},{3,11}... | collective-permute-start | bytes 36872 | tf_op jit(solution)/shard_map/ppermute | solution.py:174
  121.9 4.6 %all-to-all-start.2 = ((bf16[8,16,384]{2,1,0:T(8,128)(2,1)}), bf16[8,16,384]{2,1,0:T(8,128)(2,1)S(1)}, u32[]{:S(2)}, u32[]{:S(2)}) async-start(bf16[8,16,384]{2,1,0:T(8,128)(2,1)} %broadcast_in_dim.7), calls=%async_computation.2 | async-start | bytes 196608 | tf_op jit(solution)/shard_map/all_to_all | solution.py:166
  127.2 3.3 %collective-permute-start.19 = (bf16[16,384]{1,0:T(8,128)(2,1)S(1)}, bf16[16,384]{1,0:T(8,128)(2,1)S(1)}, u32[]{:S(2)}, u32[]{:S(2)}) collective-permute-start(bf16[16,384]{1,0:T(8,128)(2,1)S(1)} %get-tuple-element.27.refs_0_), channel_id=1, source_target_pairs={{0,4},{2,6},{4,8},{6,10},{8,12},{10,14},{12,0},{14,2},{1,5},{3,7},... | collective-permute-start | bytes 36872 | tf_op jit(solution)/shard_map/ppermute | solution.py:174
  131.2 4.5 %collective-permute-start.21 = (bf16[16,384]{1,0:T(8,128)(2,1)S(1)}, bf16[16,384]{1,0:T(8,128)(2,1)S(1)}, u32[]{:S(2)}, u32[]{:S(2)}) collective-permute-start(bf16[16,384]{1,0:T(8,128)(2,1)S(1)} %get-tuple-element.27.refs_0_), channel_id=1, source_target_pairs={{0,8},{2,10},{4,12},{6,14},{8,0},{10,2},{12,4},{14,6},{1,9},{3,11}... | collective-permute-start | bytes 36872 | tf_op jit(solution)/shard_map/ppermute | solution.py:174
  136.3 2.8 %collective-permute-start.23 = (bf16[16,384]{1,0:T(8,128)(2,1)S(1)}, bf16[16,384]{1,0:T(8,128)(2,1)S(1)}, u32[]{:S(2)}, u32[]{:S(2)}) collective-permute-start(bf16[16,384]{1,0:T(8,128)(2,1)S(1)} %get-tuple-element.27.refs_0_), channel_id=1, source_target_pairs={{0,12},{2,14},{4,0},{6,2},{8,4},{10,6},{12,8},{14,10},{1,13},{3,15... | collective-permute-start | bytes 36872 | tf_op jit(solution)/shard_map/ppermute | solution.py:174
  143.3 6.4 %all-to-all-start.3 = ((bf16[16,8,16,384]{3,2,1,0:T(8,128)(2,1)}), bf16[16,8,16,384]{3,2,1,0:T(8,128)(2,1)S(1)}, u32[]{:S(2)}, u32[]{:S(2)}) async-start(bf16[16,8,16,384]{3,2,1,0:T(8,128)(2,1)} %spread.1), calls=%async_computation.3 | async-start | bytes 3145728 | tf_op jit(solution)/shard_map/all_to_all | solution.py:166
  151.2 5.1 %collective-permute-done.16 = f32[2,16,384]{2,1,0:T(8,128)S(1)} collective-permute-done((f32[2,16,384]{2,1,0:T(8,128)S(1)}, f32[2,16,384]{2,1,0:T(8,128)S(1)}, u32[]{:S(2)}, u32[]{:S(2)}) %collective-permute-start.16) | collective-permute-done | bytes 49184 | tf_op jit(solution)/shard_map/ppermute | solution.py:233
  156.3 3.2 %collective-permute-start.17 = (f32[4,16,384]{2,1,0:T(8,128)S(1)}, f32[4,16,384]{2,1,0:T(8,128)S(1)}, u32[]{:S(2)}, u32[]{:S(2)}) collective-permute-start(f32[4,16,384]{2,1,0:T(8,128)S(1)} %pad_maximum_fusion.1), channel_id=1, source_target_pairs={{0,64},{32,96},{64,0},{96,32},{1,65},{33,97},{65,1},{97,33},{2,66}... | collective-permute-start | bytes 294920 | tf_op jit(solution)/shard_map/ppermute | solution.py:234
  165.8 7.9 %collective-permute-done.17 = f32[4,16,384]{2,1,0:T(8,128)S(1)} collective-permute-done((f32[4,16,384]{2,1,0:T(8,128)S(1)}, f32[4,16,384]{2,1,0:T(8,128)S(1)}, u32[]{:S(2)}, u32[]{:S(2)}) %collective-permute-start.17) | collective-permute-done | bytes 98336 | tf_op jit(solution)/shard_map/ppermute | solution.py:234
  175.6 3.0 %collective-permute-start.30 = (bf16[4,2,16,384]{3,2,1,0:T(8,128)(2,1)S(1)}, bf16[4,2,16,384]{3,2,1,0:T(8,128)(2,1)S(1)}, u32[]{:S(2)}, u32[]{:S(2)}) collective-permute-start(bf16[4,2,16,384]{3,2,1,0:T(8,128)(2,1)S(1)} %bitcast.59), channel_id=1, source_target_pairs={{0,12},{2,14},{4,0},{6,2},{8,4},{10,6},{12,8},{14,10},{1,13},{3,15... | collective-permute-start | bytes 294920 | tf_op jit(solution)/shard_map/ppermute | solution.py:174
  178.6 2.6 %collective-permute-start.32 = (f32[4,16,384]{2,1,0:T(8,128)S(1)}, f32[4,16,384]{2,1,0:T(8,128)S(1)}, u32[]{:S(2)}, u32[]{:S(2)}) collective-permute-start(f32[4,16,384]{2,1,0:T(8,128)S(1)} %slice_bitcast_fusion), channel_id=1, source_target_pairs={{0,128},{128,0},{1,129},{129,1},{2,130},{130,2},{3,131},{131,3},{4... | collective-permute-start | bytes 294920 | tf_op jit(solution)/shard_map/ppermute | solution.py:235
  185.3 11.2 %collective-permute-start.33 = (bf16[8,16,16,384]{3,2,1,0:T(8,128)(2,1)S(1)}, bf16[8,16,16,384]{3,2,1,0:T(8,128)(2,1)}, u32[]{:S(2)}, u32[]{:S(2)}) collective-permute-start(bf16[8,16,16,384]{3,2,1,0:T(8,128)(2,1)S(1)} %bitcast.52), channel_id=1, source_target_pairs={{0,1},{1,0},{2,3},{3,2},{4,5},{5,4},{6,7},{7,6},{8,9},{9,8},{10,11... | collective-permute-start | bytes 4718600 | tf_op jit(solution)/shard_map/ppermute | solution.py:239
  200.8 48.9 %place_theirs.1 = bf16[16,2,16,4608]{3,2,1,0:T(8,128)(2,1)} custom-call(bf16[16,2,16,4608]{3,2,1,0:T(8,128)(2,1)} %place_mine.1.half, bf16[8,16,16,384]{3,2,1,0:T(8,128)(2,1)} %collective-permute-done.33.left, bf16[8,4,2,16,384]{4,3,2,1,0:T(8,128)(2,1)S(1)} %collective-permute-done.34.right), custom_call_target="tpu_custom_call", output_to_operand_aliasing={{}: (0, {})} | custom-call | bytes 4718592 | tf_op jit(solution)/shard_map/place_theirs/pallas_call | solution.py:83
  (81 shorter events, 47.1 us)
Async XLA Ops:
  59.3 38.2 %all-to-all-start = ((f16[16,8,16,384]{3,2,1,0:T(8,128)(2,1)}), f16[16,8,16,384]{3,2,1,0:T(8,128)(2,1)S(1)}, u32[]{:S(2)}, u32[]{:S(2)}) async-start(f16[16,8,16,384]{3,2,1,0:T(8,128)(2,1)} %bitcast.65), calls=%async_computation | async-start | bytes 3145728 | tf_op jit(solution)/shard_map/all_to_all | solution.py:166
  68.5 15.0 %collective-permute-start.10 = (f16[4,2,16,384]{3,2,1,0:T(8,128)(2,1)S(1)}, f16[4,2,16,384]{3,2,1,0:T(8,128)(2,1)S(1)}, u32[]{:S(2)}, u32[]{:S(2)}) collective-permute-start(f16[4,2,16,384]{3,2,1,0:T(8,128)(2,1)S(1)} %get-tuple-element.50), channel_id=1, source_target_pairs={{0,4},{2,6},{4,8},{6,10},{8,12},{10,14},{12,0},{14,2},{1,5},{3,7},... | collective-permute-start | bytes 294920 | tf_op jit(solution)/shard_map/ppermute | solution.py:174
  71.6 16.7 %collective-permute-start.11 = (f16[4,2,16,384]{3,2,1,0:T(8,128)(2,1)S(1)}, f16[4,2,16,384]{3,2,1,0:T(8,128)(2,1)S(1)}, u32[]{:S(2)}, u32[]{:S(2)}) collective-permute-start(f16[4,2,16,384]{3,2,1,0:T(8,128)(2,1)S(1)} %get-tuple-element.49), channel_id=1, source_target_pairs={{0,6},{2,8},{4,10},{6,12},{8,14},{10,0},{12,2},{14,4},{1,7},{3,9},... | collective-permute-start | bytes 294920 | tf_op jit(solution)/shard_map/ppermute | solution.py:174
  76.2 12.1 %collective-permute-start.12 = (f16[4,2,16,384]{3,2,1,0:T(8,128)(2,1)S(1)}, f16[4,2,16,384]{3,2,1,0:T(8,128)(2,1)S(1)}, u32[]{:S(2)}, u32[]{:S(2)}) collective-permute-start(f16[4,2,16,384]{3,2,1,0:T(8,128)(2,1)S(1)} %get-tuple-element.48), channel_id=1, source_target_pairs={{0,8},{2,10},{4,12},{6,14},{8,0},{10,2},{12,4},{14,6},{1,9},{3,11}... | collective-permute-start | bytes 294920 | tf_op jit(solution)/shard_map/ppermute | solution.py:174
  77.2 11.8 %collective-permute-start.13 = (f16[4,2,16,384]{3,2,1,0:T(8,128)(2,1)S(1)}, f16[4,2,16,384]{3,2,1,0:T(8,128)(2,1)S(1)}, u32[]{:S(2)}, u32[]{:S(2)}) collective-permute-start(f16[4,2,16,384]{3,2,1,0:T(8,128)(2,1)S(1)} %get-tuple-element.47), channel_id=1, source_target_pairs={{0,10},{2,12},{4,14},{6,0},{8,2},{10,4},{12,6},{14,8},{1,11},{3,13... | collective-permute-start | bytes 294920 | tf_op jit(solution)/shard_map/ppermute | solution.py:174
  81.2 15.3 %collective-permute-start.14 = (f16[4,2,16,384]{3,2,1,0:T(8,128)(2,1)S(1)}, f16[4,2,16,384]{3,2,1,0:T(8,128)(2,1)S(1)}, u32[]{:S(2)}, u32[]{:S(2)}) collective-permute-start(f16[4,2,16,384]{3,2,1,0:T(8,128)(2,1)S(1)} %get-tuple-element.46), channel_id=1, source_target_pairs={{0,12},{2,14},{4,0},{6,2},{8,4},{10,6},{12,8},{14,10},{1,13},{3,15... | collective-permute-start | bytes 294920 | tf_op jit(solution)/shard_map/ppermute | solution.py:174
  83.5 13.0 %collective-permute-start.15 = (f16[4,2,16,384]{3,2,1,0:T(8,128)(2,1)S(1)}, f16[4,2,16,384]{3,2,1,0:T(8,128)(2,1)S(1)}, u32[]{:S(2)}, u32[]{:S(2)}) collective-permute-start(f16[4,2,16,384]{3,2,1,0:T(8,128)(2,1)S(1)} %get-tuple-element.45), channel_id=1, source_target_pairs={{0,14},{2,0},{4,2},{6,4},{8,6},{10,8},{12,10},{14,12},{1,15},{3,1}... | collective-permute-start | bytes 294920 | tf_op jit(solution)/shard_map/ppermute | solution.py:174
  98.2 19.6 %all-to-all-start.1 = ((f16[16,16,384]{2,1,0:T(8,128)(2,1)}), f16[16,16,384]{2,1,0:T(8,128)(2,1)S(1)}, u32[]{:S(2)}, u32[]{:S(2)}) async-start(f16[16,16,384]{2,1,0:T(8,128)(2,1)} %bitcast.19), calls=%async_computation.1 | async-start | bytes 393216 | tf_op jit(solution)/shard_map/all_to_all | solution.py:166
  105.4 10.7 %collective-permute-start.1 = (f16[16,384]{1,0:T(8,128)(2,1)S(1)}, f16[16,384]{1,0:T(8,128)(2,1)S(1)}, u32[]{:S(2)}, u32[]{:S(2)}) collective-permute-start(f16[16,384]{1,0:T(8,128)(2,1)S(1)} %get-tuple-element.52), channel_id=1, source_target_pairs={{0,2},{2,4},{4,6},{6,8},{8,10},{10,12},{12,14},{14,0},{1,3},{3,5},... | collective-permute-start | bytes 36872 | tf_op jit(solution)/shard_map/ppermute | solution.py:174
  108.4 9.0 %collective-permute-start.2 = (f16[16,384]{1,0:T(8,128)(2,1)S(1)}, f16[16,384]{1,0:T(8,128)(2,1)S(1)}, u32[]{:S(2)}, u32[]{:S(2)}) collective-permute-start(f16[16,384]{1,0:T(8,128)(2,1)S(1)} %get-tuple-element.58), channel_id=1, source_target_pairs={{0,4},{2,6},{4,8},{6,10},{8,12},{10,14},{12,0},{14,2},{1,5},{3,7},... | collective-permute-start | bytes 36872 | tf_op jit(solution)/shard_map/ppermute | solution.py:174
  108.8 9.1 %collective-permute-start.3 = (f16[16,384]{1,0:T(8,128)(2,1)S(1)}, f16[16,384]{1,0:T(8,128)(2,1)S(1)}, u32[]{:S(2)}, u32[]{:S(2)}) collective-permute-start(f16[16,384]{1,0:T(8,128)(2,1)S(1)} %get-tuple-element.57), channel_id=1, source_target_pairs={{0,6},{2,8},{4,10},{6,12},{8,14},{10,0},{12,2},{14,4},{1,7},{3,9},... | collective-permute-start | bytes 36872 | tf_op jit(solution)/shard_map/ppermute | solution.py:174
  109.5 8.4 %collective-permute-start.4 = (f16[16,384]{1,0:T(8,128)(2,1)S(1)}, f16[16,384]{1,0:T(8,128)(2,1)S(1)}, u32[]{:S(2)}, u32[]{:S(2)}) collective-permute-start(f16[16,384]{1,0:T(8,128)(2,1)S(1)} %get-tuple-element.56), channel_id=1, source_target_pairs={{0,8},{2,10},{4,12},{6,14},{8,0},{10,2},{12,4},{14,6},{1,9},{3,11}... | collective-permute-start | bytes 36872 | tf_op jit(solution)/shard_map/ppermute | solution.py:174
  121.9 20.0 %all-to-all-start.2 = ((bf16[8,16,384]{2,1,0:T(8,128)(2,1)}), bf16[8,16,384]{2,1,0:T(8,128)(2,1)S(1)}, u32[]{:S(2)}, u32[]{:S(2)}) async-start(bf16[8,16,384]{2,1,0:T(8,128)(2,1)} %broadcast_in_dim.7), calls=%async_computation.2 | async-start | bytes 196608 | tf_op jit(solution)/shard_map/all_to_all | solution.py:166
  126.6 9.8 %collective-permute-start.18 = (bf16[16,384]{1,0:T(8,128)(2,1)S(1)}, bf16[16,384]{1,0:T(8,128)(2,1)S(1)}, u32[]{:S(2)}, u32[]{:S(2)}) collective-permute-start(bf16[16,384]{1,0:T(8,128)(2,1)S(1)} %get-tuple-element.27.refs_0_), channel_id=1, source_target_pairs={{0,2},{2,4},{4,6},{6,8},{8,10},{10,12},{12,14},{14,0},{1,3},{3,5},... | collective-permute-start | bytes 36872 | tf_op jit(solution)/shard_map/ppermute | solution.py:174
  127.2 11.9 %collective-permute-start.19 = (bf16[16,384]{1,0:T(8,128)(2,1)S(1)}, bf16[16,384]{1,0:T(8,128)(2,1)S(1)}, u32[]{:S(2)}, u32[]{:S(2)}) collective-permute-start(bf16[16,384]{1,0:T(8,128)(2,1)S(1)} %get-tuple-element.27.refs_0_), channel_id=1, source_target_pairs={{0,4},{2,6},{4,8},{6,10},{8,12},{10,14},{12,0},{14,2},{1,5},{3,7},... | collective-permute-start | bytes 36872 | tf_op jit(solution)/shard_map/ppermute | solution.py:174
  130.5 10.0 %collective-permute-start.20 = (bf16[16,384]{1,0:T(8,128)(2,1)S(1)}, bf16[16,384]{1,0:T(8,128)(2,1)S(1)}, u32[]{:S(2)}, u32[]{:S(2)}) collective-permute-start(bf16[16,384]{1,0:T(8,128)(2,1)S(1)} %get-tuple-element.27.refs_0_), channel_id=1, source_target_pairs={{0,6},{2,8},{4,10},{6,12},{8,14},{10,0},{12,2},{14,4},{1,7},{3,9},... | collective-permute-start | bytes 36872 | tf_op jit(solution)/shard_map/ppermute | solution.py:174
  131.2 9.2 %collective-permute-start.21 = (bf16[16,384]{1,0:T(8,128)(2,1)S(1)}, bf16[16,384]{1,0:T(8,128)(2,1)S(1)}, u32[]{:S(2)}, u32[]{:S(2)}) collective-permute-start(bf16[16,384]{1,0:T(8,128)(2,1)S(1)} %get-tuple-element.27.refs_0_), channel_id=1, source_target_pairs={{0,8},{2,10},{4,12},{6,14},{8,0},{10,2},{12,4},{14,6},{1,9},{3,11}... | collective-permute-start | bytes 36872 | tf_op jit(solution)/shard_map/ppermute | solution.py:174
  143.3 42.0 %all-to-all-start.3 = ((bf16[16,8,16,384]{3,2,1,0:T(8,128)(2,1)}), bf16[16,8,16,384]{3,2,1,0:T(8,128)(2,1)S(1)}, u32[]{:S(2)}, u32[]{:S(2)}) async-start(bf16[16,8,16,384]{3,2,1,0:T(8,128)(2,1)} %spread.1), calls=%async_computation.3 | async-start | bytes 3145728 | tf_op jit(solution)/shard_map/all_to_all | solution.py:166
  156.3 17.3 %collective-permute-start.17 = (f32[4,16,384]{2,1,0:T(8,128)S(1)}, f32[4,16,384]{2,1,0:T(8,128)S(1)}, u32[]{:S(2)}, u32[]{:S(2)}) collective-permute-start(f32[4,16,384]{2,1,0:T(8,128)S(1)} %pad_maximum_fusion.1), channel_id=1, source_target_pairs={{0,64},{32,96},{64,0},{96,32},{1,65},{33,97},{65,1},{97,33},{2,66}... | collective-permute-start | bytes 294920 | tf_op jit(solution)/shard_map/ppermute | solution.py:234
  159.5 16.1 %collective-permute-start.25 = (bf16[4,2,16,384]{3,2,1,0:T(8,128)(2,1)S(1)}, bf16[4,2,16,384]{3,2,1,0:T(8,128)(2,1)S(1)}, u32[]{:S(2)}, u32[]{:S(2)}) collective-permute-start(bf16[4,2,16,384]{3,2,1,0:T(8,128)(2,1)S(1)} %bitcast.54), channel_id=1, source_target_pairs={{0,2},{2,4},{4,6},{6,8},{8,10},{10,12},{12,14},{14,0},{1,3},{3,5},... | collective-permute-start | bytes 294920 | tf_op jit(solution)/shard_map/ppermute | solution.py:174
  159.5 19.1 %collective-permute-start.26 = (bf16[4,2,16,384]{3,2,1,0:T(8,128)(2,1)S(1)}, bf16[4,2,16,384]{3,2,1,0:T(8,128)(2,1)S(1)}, u32[]{:S(2)}, u32[]{:S(2)}) collective-permute-start(bf16[4,2,16,384]{3,2,1,0:T(8,128)(2,1)S(1)} %bitcast.55), channel_id=1, source_target_pairs={{0,4},{2,6},{4,8},{6,10},{8,12},{10,14},{12,0},{14,2},{1,5},{3,7},... | collective-permute-start | bytes 294920 | tf_op jit(solution)/shard_map/ppermute | solution.py:174
  161.9 16.7 %collective-permute-start.27 = (bf16[4,2,16,384]{3,2,1,0:T(8,128)(2,1)S(1)}, bf16[4,2,16,384]{3,2,1,0:T(8,128)(2,1)S(1)}, u32[]{:S(2)}, u32[]{:S(2)}) collective-permute-start(bf16[4,2,16,384]{3,2,1,0:T(8,128)(2,1)S(1)} %bitcast.56), channel_id=1, source_target_pairs={{0,6},{2,8},{4,10},{6,12},{8,14},{10,0},{12,2},{14,4},{1,7},{3,9},... | collective-permute-start | bytes 294920 | tf_op jit(solution)/shard_map/ppermute | solution.py:174
  163.7 17.5 %collective-permute-start.28 = (bf16[4,2,16,384]{3,2,1,0:T(8,128)(2,1)S(1)}, bf16[4,2,16,384]{3,2,1,0:T(8,128)(2,1)S(1)}, u32[]{:S(2)}, u32[]{:S(2)}) collective-permute-start(bf16[4,2,16,384]{3,2,1,0:T(8,128)(2,1)S(1)} %bitcast.57), channel_id=1, source_target_pairs={{0,8},{2,10},{4,12},{6,14},{8,0},{10,2},{12,4},{14,6},{1,9},{3,11}... | collective-permute-start | bytes 294920 | tf_op jit(solution)/shard_map/ppermute | solution.py:174
  185.3 15.5 %collective-permute-start.33 = (bf16[8,16,16,384]{3,2,1,0:T(8,128)(2,1)S(1)}, bf16[8,16,16,384]{3,2,1,0:T(8,128)(2,1)}, u32[]{:S(2)}, u32[]{:S(2)}) collective-permute-start(bf16[8,16,16,384]{3,2,1,0:T(8,128)(2,1)S(1)} %bitcast.52), channel_id=1, source_target_pairs={{0,1},{1,0},{2,3},{3,2},{4,5},{5,4},{6,7},{7,6},{8,9},{9,8},{10,11... | collective-permute-start | bytes 4718600 | tf_op jit(solution)/shard_map/ppermute | solution.py:239
  (17 other events, 114.8 us)

commit v3 on v1

v3 whole, which is shorter than its diff:
```python
import jax
import jax.numpy as jnp
from jax import lax
from jax.experimental import pallas as pl
from jax.experimental.pallas import tpu as pltpu
from jax.sharding import Mesh, PartitionSpec as P

STEP = 10
XH, Y, XL, Z, CORES = 2, 4, 2, 8, 2
PLANE = ("xh", "y", "xl")
SWAP = [(0, 1), (1, 0)]
LOW, COLS = 8, 1152
PIECES, BLOCKS = XH * Y, XL * Z
SHAPE = (PIECES, BLOCKS, LOW, COLS)
WHOLE = (BLOCKS, CORES, XH, LOW, Y * COLS)
VMEM = pl.BlockSpec(memory_space=pltpu.VMEM)
ANY = pl.BlockSpec(memory_space=pl.ANY)
SMALL = pltpu.CompilerParams(vmem_limit_bytes=2 * 2**20)


def views(whole, core):
    return [
        whole.at[:, core, xh, :, pl.ds(y * COLS, COLS)] for xh in range(XH) for y in range(Y)
    ]


def copy_all(sources, targets, sems):
    copies = [
        pltpu.make_async_copy(a, b, sems.at[k]) for k, (a, b) in enumerate(zip(sources, targets))
    ]
    for copy in copies:
        copy.start()
    for copy in copies:
        copy.wait()


def split_kernel(of_other, whole, pieces, sems):
    core = lax.axis_index("c")
    sources = views(whole, 1 - core if of_other else core)
    copy_all(sources, [pieces.at[i] for i in range(PIECES)], sems)


def split(of_other, whole):
    return pl.pallas_call(
        lambda *refs: split_kernel(of_other, *refs),
        out_shape=pltpu.VMEM(SHAPE, whole.dtype),
        in_specs=[ANY],
        out_specs=ANY,
        scratch_shapes=[pltpu.SemaphoreType.DMA((PIECES,))],
        compiler_params=SMALL,
        cost_estimate=pl.CostEstimate(flops=0, bytes_accessed=2 * whole.size, transcendentals=0),
        name="split_theirs" if of_other else "split_mine",
    )(whole)


def place_kernel(of_other, *refs):
    pieces, out, sems = refs[-3:]
    core = lax.axis_index("c")
    targets = views(out, 1 - core if of_other else core)
    copy_all([pieces.at[i] for i in range(PIECES)], targets, sems)


def place(of_other, pieces, half=()):
    return pl.pallas_call(
        lambda *refs: place_kernel(of_other, *refs),
        out_shape=jax.ShapeDtypeStruct(WHOLE, pieces.dtype),
        in_specs=[ANY] * (len(half) + 1),
        out_specs=ANY,
        scratch_shapes=[pltpu.SemaphoreType.DMA((PIECES,))],
        input_output_aliases={0: 0} if half else {},
        compiler_params=SMALL,
        cost_estimate=pl.CostEstimate(flops=0, bytes_accessed=4 * pieces.size, transcendentals=0),
        name="place_theirs" if of_other else "place_mine",
    )(*half, pltpu.with_memory_space_constraint(pieces, pltpu.VMEM))


def adam(grad, master, moment1, moment2):
    moment1_new = 0.9 * moment1 + 0.1 * grad
    moment2_new = 0.95 * moment2 + 0.05 * grad * grad
    first_fix = 1.0 - 0.9**STEP
    second_fix = 1.0 - 0.95**STEP
    update = moment1_new / first_fix / (jnp.sqrt(moment2_new / second_fix) + 1e-08)
    master_new = master * (1.0 - 0.02 * 0.1) - 0.02 * update
    return master_new, moment1_new, moment2_new


def states_kernel(mine, others, master, moment1, moment2, master_new, moment1_new, moment2_new):
    xh, y = lax.axis_index("xh"), lax.axis_index("y")
    for k in range(Y):
        for grad, low in ((mine[k], xh), (others[k], 1 - xh)):
            rows = pl.ds(pl.multiple_of(low * LOW, LOW), LOW)
            at = (rows, pl.ds(pl.multiple_of((y ^ k) * COLS, 128), COLS))
            new = adam(grad, master[at], moment1[at], moment2[at])
            master_new[at], moment1_new[at], moment2_new[at] = new


def states(mine, others, master, moment1, moment2):
    return pl.pallas_call(
        states_kernel,
        out_shape=[jax.ShapeDtypeStruct(master.shape, master.dtype)] * 3,
        in_specs=[VMEM] * 5,
        out_specs=[VMEM] * 3,
        compiler_params=pltpu.CompilerParams(vmem_limit_bytes=8 * 2**20),
        cost_estimate=pl.CostEstimate(
            flops=20 * master.size, bytes_accessed=28 * master.size, transcendentals=master.size
        ),
        name="states",
    )(mine, others, master, moment1, moment2)


def exchange(chunks, axes):
    return lax.all_to_all(chunks, axes, 0, 0, tiled=True)


def gather(piece, axes, n):
    return exchange(jnp.broadcast_to(piece, (n, *piece.shape)), axes)


def add(parts):
    return jnp.sum(parts.astype(jnp.float32), axis=0)


def per_device(gradients, master, moment1, moment2):
    xh, y = lax.axis_index("xh"), lax.axis_index("y")
    rows, width = gradients.shape[2:]
    plane = XH * Y * XL
    whole = pltpu.with_memory_space_constraint(gradients.reshape(WHOLE), pltpu.HBM)

    came = lax.ppermute(split(True, whole), "c", SWAP)
    pair = split(False, whole).astype(jnp.float32) + came.astype(jnp.float32)
    pair = pair.astype(jnp.float16).reshape(plane, Z, LOW, COLS)
    column = add(exchange(pair, PLANE)).astype(jnp.float16)
    grad = add(exchange(column, "z")) / (plane * Z * CORES)

    def piece(state):
        return lax.dynamic_slice(state, (xh * LOW, y * COLS), (LOW, COLS))

    part = adam(grad, piece(master), piece(moment1), piece(moment2))[0].astype(jnp.bfloat16)
    mine = jnp.stack([grad])
    came = lax.ppermute(mine, "y", [(i, i ^ 1) for i in range(Y)])
    part, came = lax.optimization_barrier((gather(part, "z", Z), came))
    mine = jnp.concatenate([mine, came])
    came = lax.ppermute(mine, "y", [(i, i ^ 2) for i in range(Y)])
    part, came = lax.optimization_barrier((gather(part, PLANE, plane), came))
    mine = jnp.concatenate([mine, came])
    others = lax.ppermute(mine, "xh", SWAP)
    part = part.reshape(SHAPE)
    came = lax.ppermute(part, "c", SWAP)
    params = place(True, came, (place(False, part),))
    master_new, moment1_new, moment2_new = states(mine, others, master, moment1, moment2)
    return master_new, moment1_new, moment2_new, params.reshape(rows, width)


def solution(mesh):
    fine = Mesh(mesh.devices.reshape(XH, Y, XL, Z, CORES), ("xh", "y", "xl", "z", "c"))
    replica, shard = ("xh", "y"), ("xl", "z", "c")
    state = P(shard, None)
    return jax.shard_map(
        per_device,
        mesh=fine,
        in_specs=(P(replica, shard, None, None), state, state, state),
        out_specs=(state, state, state, P()),
        check_vma=False,
    )
```

time: 140 us -> 126 us (0.900); the launches traced: 139 us -> 124 us
  blocking collectives: 77 us -> 35.5 us
  waiting for transfers between devices: 20.7 us -> 46.8 us
  local copies, waits for them, and re-layouts: 14.1 us -> 2.4 us
  starting transfers between devices: 19.4 us -> 29.1 us
  Pallas kernels: 0 us -> 7.44 us
  other arithmetic: 7.57 us -> 1.79 us
    all_to_all x3 -> x1, blocking collectives: 77 us -> 35.5 us  [exchange(): return lax.all_to_all(chunks, axes, 0, 0, tiled=True)]
    ppermute x2 -> x5, waiting for transfers between devices: 4.3 us -> 31 us  [the longest x1 22 us: per_device(): came = lax.ppermute(mine, 'y', [(i, i ^ 2) for i in range(Y)])]
    pallas_call x0 -> x5, Pallas kernels: none -> 7.44 us  [the longest x2 3.33 us: split(): pl.pallas_call(lambda *refs: split_kernel(of_other, *refs), out_shape=plt...]
    ppermute x2 -> x5, starting transfers between devices: 7.78 us -> 13.8 us  [the longest x1 5.56 us: per_device(): came = lax.ppermute(part, 'c', SWAP)]
    reshape x2 -> x0, local copies, waits for them, and re-layouts: 4.62 us -> none  [the longest x1 2.37 us: per_device(): part = part.reshape(blocks, own, width)]
    transpose x2 -> x0, local copies, waits for them, and re-layouts: 4.11 us -> none  [the longest x1 2.29 us: per_device(): pair.reshape(n_xl, n_z, n_xh, low, n_y, cols).transpose(2, 4, 0, 1, 3, 5)]
    all_to_all x2 -> x3, starting transfers between devices: 11.6 us -> 15.3 us  [exchange(): return lax.all_to_all(chunks, axes, 0, 0, tiled=True)]
    another operation x1 -> x0, local copies, waits for them, and re-layouts: 2.49 us -> none  [per_device(): jnp.stack([jnp.where(first, part, other), jnp.where(first, other, part)],...]
  transfers between devices with their start and end apart: 4 -> 8, of which waited for: 3 -> 7; matrix products, arithmetic and copies ran while one was open for 1% -> 0% of each run, Pallas kernels for 0% -> 3%
where the time goes in v3:
time: 126 us; the launch traced here: 124 us
  waiting for transfers between devices  46.8 us (37%)
  blocking collectives  35.5 us (28%)
  starting transfers between devices  29.1 us (23%)
  Pallas kernels  7.44 us (6%)
  local copies, waits for them, and re-layouts  2.4 us (2%)
  other arithmetic  1.79 us (1%)
    all_to_all x1, blocking collectives, exchange(): return lax.all_to_all(chunks, axes, 0, 0, tiled=True)  35.5 us
    ppermute x1, waiting for transfers between devices, per_device(): came = lax.ppermute(mine, 'y', [(i, i ^ 2) for i in range(Y)])  22 us
    all_to_all x3, waiting for transfers between devices, exchange(): return lax.all_to_all(chunks, axes, 0, 0, tiled=True)  15.8 us
    all_to_all x3, starting transfers between devices, exchange(): return lax.all_to_all(chunks, axes, 0, 0, tiled=True)  15.3 us
    ppermute x1, starting transfers between devices, per_device(): came = lax.ppermute(part, 'c', SWAP)  5.56 us
    ppermute x1, waiting for transfers between devices, per_device(): others = lax.ppermute(mine, 'xh', SWAP)  3.66 us
    pallas_call x2, Pallas kernels, split(): pl.pallas_call(lambda *refs: split_kernel(of_other, *refs), out_shape=plt...  3.33 us
    ppermute x1, starting transfers between devices, per_device(): came = lax.ppermute(split(True, whole), 'c', SWAP)  3.33 us
  transfers between devices with their start and end apart: 8, of which 7 were waited for; matrix products, arithmetic and copies ran while one was open for 0% of the time, Pallas kernels for 3%

profile of v3, /device:TPU:1, one launch (start us, length us, event | category | flops | bytes accessed | tf_op | source)
XLA Modules:
  0.0 123.7 jit_solution(3701530641428551695)
XLA Ops:
  0.6 1.7 %split_theirs.1 = bf16[8,16,8,1152]{3,2,1,0:T(8,128)(2,1)S(1)} custom-call(bf16[16,2,2,8,4608]{4,3,2,1,0:T(8,128)(2,1)} %bitcast.8), custom_call_target="tpu_custom_call" | custom-call | bytes 4718592 | tf_op jit(solution)/shard_map/split_theirs/pallas_call | solution.py:44
  2.3 3.3 %collective-permute-start = (bf16[8,16,8,1152]{3,2,1,0:T(8,128)(2,1)S(1)}, bf16[8,16,8,1152]{3,2,1,0:T(8,128)(2,1)S(1)}, u32[]{:S(2)}, u32[]{:S(2)}) collective-permute-start(bf16[8,16,8,1152]{3,2,1,0:T(8,128)(2,1)S(1)} %split_theirs.1), channel_id=1, source_target_pairs={{0,1},{1,0},{2,3},{3,2},{4,5},{5,4},{6,7},{7,6},{8,9},{9,8},{10,11... | collective-permute-start | bytes 7077896 | tf_op jit(solution)/shard_map/ppermute | solution.py:129
  5.6 1.7 %split_mine.1 = bf16[8,16,8,1152]{3,2,1,0:T(8,128)(2,1)S(1)} custom-call(bf16[16,2,2,8,4608]{4,3,2,1,0:T(8,128)(2,1)} %bitcast.9), custom_call_target="tpu_custom_call" | custom-call | bytes 4718592 | tf_op jit(solution)/shard_map/split_mine/pallas_call | solution.py:44
  7.3 2.5 %collective-permute-done = bf16[8,16,8,1152]{3,2,1,0:T(8,128)(2,1)S(1)} collective-permute-done((bf16[8,16,8,1152]{3,2,1,0:T(8,128)(2,1)S(1)}, bf16[8,16,8,1152]{3,2,1,0:T(8,128)(2,1)S(1)}, u32[]{:S(2)}, u32[]{:S(2)}) %collective-permute-start) | collective-permute-done | bytes 2359328 | tf_op jit(solution)/shard_map/ppermute | solution.py:129
  9.8 0.7 add_convert_fusion
  10.5 35.5 %all_to_all.20 = f16[16,8,8,1152]{3,2,1,0:T(8,128)(2,1)S(1)} all-to-all(f16[16,8,8,1152]{3,2,1,0:T(8,128)(2,1)S(1)} %bitcast.11), channel_id=1, replica_groups=mesh['xh'=2,'y'=4,'xl'=2,'z'=8,'c'=2] {'xh','y','xl'}, dimensions={0} | all-to-all | bytes 4718592 | tf_op jit(solution)/shard_map/all_to_all | solution.py:112
  46.3 0.7 convert_element_type.25
  47.0 8.2 %all-to-all-start.1 = ((f16[8,8,1152]{2,1,0:T(8,128)(2,1)}), f16[8,8,1152]{2,1,0:T(8,128)(2,1)S(1)}, u32[]{:S(2)}, u32[]{:S(2)}) async-start(f16[8,8,1152]{2,1,0:T(8,128)(2,1)} %convert_element_type.25), calls=%async_computation.1 | async-start | bytes 294912 | tf_op jit(solution)/shard_map/all_to_all | solution.py:112
  55.2 8.1 %all-to-all-done.1 = f16[8,8,1152]{2,1,0:T(8,128)(2,1)S(1)} async-done(((f16[8,8,1152]{2,1,0:T(8,128)(2,1)}), f16[8,8,1152]{2,1,0:T(8,128)(2,1)S(1)}, u32[]{:S(2)}, u32[]{:S(2)}) %all-to-all-start.1) | async-done | bytes 147488 | tf_op jit(solution)/shard_map/all_to_all | solution.py:112
  63.4 0.7 broadcast_in_dim.6
  64.1 3.4 %all-to-all-start.2 = ((bf16[8,8,1152]{2,1,0:T(8,128)(2,1)}), bf16[8,8,1152]{2,1,0:T(8,128)(2,1)S(1)}, u32[]{:S(2)}, u32[]{:S(2)}) async-start(bf16[8,8,1152]{2,1,0:T(8,128)(2,1)} %broadcast_in_dim.6), calls=%async_computation.2 | async-start | bytes 294912 | tf_op jit(solution)/shard_map/all_to_all | solution.py:112
  67.6 2.8 %collective-permute-done.1 = f32[1,8,1152]{2,1,0:T(8,128)S(1)} collective-permute-done((f32[1,8,1152]{2,1,0:T(8,128)S(1)}, f32[1,8,1152]{2,1,0:T(8,128)S(1)}, u32[]{:S(2)}, u32[]{:S(2)}) %collective-permute-start.1) | collective-permute-done | bytes 36896 | tf_op jit(solution)/shard_map/ppermute | solution.py:140
  70.4 5.1 %all-to-all-done.2 = bf16[8,8,1152]{2,1,0:T(8,128)(2,1)S(1)} async-done(((bf16[8,8,1152]{2,1,0:T(8,128)(2,1)}), bf16[8,8,1152]{2,1,0:T(8,128)(2,1)S(1)}, u32[]{:S(2)}, u32[]{:S(2)}) %all-to-all-start.2) | async-done | bytes 147488 | tf_op jit(solution)/shard_map/all_to_all | solution.py:112
  75.5 1.7 %broadcast_in_dim.7 = bf16[16,8,8,1152]{3,2,1,0:T(8,128)(2,1)} broadcast(bf16[8,8,1152]{2,1,0:T(8,128)(2,1)S(1)} %all-to-all-done.2), dimensions={1,2,3} | broadcast | bytes 2506752 | tf_op jit(solution)/shard_map/broadcast_in_dim | solution.py:116
  77.2 3.7 %all-to-all-start.3 = ((bf16[16,8,8,1152]{3,2,1,0:T(8,128)(2,1)}), bf16[16,8,8,1152]{3,2,1,0:T(8,128)(2,1)S(1)}, u32[]{:S(2)}, u32[]{:S(2)}) async-start(bf16[16,8,8,1152]{3,2,1,0:T(8,128)(2,1)} %broadcast_in_dim.7), calls=%async_computation.3 | async-start | bytes 4718592 | tf_op jit(solution)/shard_map/all_to_all | solution.py:112
  80.9 2.9 %collective-permute-start.2 = (f32[2,8,1152]{2,1,0:T(8,128)S(1)}, f32[2,8,1152]{2,1,0:T(8,128)S(1)}, u32[]{:S(2)}, u32[]{:S(2)}) collective-permute-start(f32[2,8,1152]{2,1,0:T(8,128)S(1)} %pad_maximum_fusion.1), channel_id=1, source_target_pairs={{0,64},{32,96},{64,0},{96,32},{1,65},{33,97},{65,1},{97,33},{2,66}... | collective-permute-start | bytes 221192 | tf_op jit(solution)/shard_map/ppermute | solution.py:143
  83.8 22.0 %collective-permute-done.2 = f32[2,8,1152]{2,1,0:T(8,128)S(1)} collective-permute-done((f32[2,8,1152]{2,1,0:T(8,128)S(1)}, f32[2,8,1152]{2,1,0:T(8,128)S(1)}, u32[]{:S(2)}, u32[]{:S(2)}) %collective-permute-start.2) | collective-permute-done | bytes 73760 | tf_op jit(solution)/shard_map/ppermute | solution.py:143
  105.8 2.6 %all-to-all-done.3 = bf16[16,8,8,1152]{3,2,1,0:T(8,128)(2,1)S(1)} async-done(((bf16[16,8,8,1152]{3,2,1,0:T(8,128)(2,1)}), bf16[16,8,8,1152]{3,2,1,0:T(8,128)(2,1)S(1)}, u32[]{:S(2)}, u32[]{:S(2)}) %all-to-all-start.3) | async-done | bytes 2359328 | tf_op jit(solution)/shard_map/all_to_all | solution.py:112
  108.4 5.6 %collective-permute-start.4 = (bf16[8,16,8,1152]{3,2,1,0:T(8,128)(2,1)S(1)}, bf16[8,16,8,1152]{3,2,1,0:T(8,128)(2,1)S(1)}, u32[]{:S(2)}, u32[]{:S(2)}) collective-permute-start(bf16[8,16,8,1152]{3,2,1,0:T(8,128)(2,1)S(1)} %bitcast.6), channel_id=1, source_target_pairs={{0,1},{1,0},{2,3},{3,2},{4,5},{5,4},{6,7},{7,6},{8,9},{9,8},{10,11... | collective-permute-start | bytes 7077896 | tf_op jit(solution)/shard_map/ppermute | solution.py:148
  113.9 1.9 %collective-permute-start.3 = (f32[4,8,1152]{2,1,0:T(8,128)S(1)}, f32[4,8,1152]{2,1,0:T(8,128)S(1)}, u32[]{:S(2)}, u32[]{:S(2)}) collective-permute-start(f32[4,8,1152]{2,1,0:T(8,128)S(1)} %pad_maximum_fusion.mine), channel_id=1, source_target_pairs={{0,128},{128,0},{1,129},{129,1},{2,130},{130,2},{3,131},{131,3},{4... | collective-permute-start | bytes 442376 | tf_op jit(solution)/shard_map/ppermute | solution.py:146
  115.9 1.5 %place_mine.1.refs_0_ = bf16[16,2,2,8,4608]{4,3,2,1,0:T(8,128)(2,1)} custom-call(bf16[8,16,8,1152]{3,2,1,0:T(8,128)(2,1)S(1)} %bitcast.7), custom_call_target="tpu_custom_call" | custom-call | bytes 4718592 | tf_op jit(solution)/shard_map/place_mine/pallas_call | solution.py:64
  117.4 3.7 %collective-permute-done.3.others = f32[4,8,1152]{2,1,0:T(8,128)S(1)} collective-permute-done((f32[4,8,1152]{2,1,0:T(8,128)S(1)}, f32[4,8,1152]{2,1,0:T(8,128)S(1)}, u32[]{:S(2)}, u32[]{:S(2)}) %collective-permute-start.3) | collective-permute-done | bytes 147488 | tf_op jit(solution)/shard_map/ppermute | solution.py:146
  121.0 1.2 states.1
  122.2 1.5 %place_theirs.1 = bf16[16,2,2,8,4608]{4,3,2,1,0:T(8,128)(2,1)} custom-call(bf16[16,2,2,8,4608]{4,3,2,1,0:T(8,128)(2,1)} %place_mine.1.refs_0_, bf16[8,16,8,1152]{3,2,1,0:T(8,128)(2,1)S(1)} %collective-permute-done.4.refs_1_), custom_call_target="tpu_custom_call", output_to_operand_aliasing={{}: (0, {})} | custom-call | bytes 4718592 | tf_op jit(solution)/shard_map/place_theirs/pallas_call | solution.py:64
  (13 shorter events, 0.5 us)
Async XLA Ops:
  2.3 7.5 %collective-permute-start = (bf16[8,16,8,1152]{3,2,1,0:T(8,128)(2,1)S(1)}, bf16[8,16,8,1152]{3,2,1,0:T(8,128)(2,1)S(1)}, u32[]{:S(2)}, u32[]{:S(2)}) collective-permute-start(bf16[8,16,8,1152]{3,2,1,0:T(8,128)(2,1)S(1)} %split_theirs.1), channel_id=1, source_target_pairs={{0,1},{1,0},{2,3},{3,2},{4,5},{5,4},{6,7},{7,6},{8,9},{9,8},{10,11... | collective-permute-start | bytes 7077896 | tf_op jit(solution)/shard_map/ppermute | solution.py:129
  46.0 17.3 %copy-start = (f32[16,4608]{1,0:T(8,128)S(1)}, f32[16,4608]{1,0:T(8,128)}, u32[]{:S(2)}) copy-start(f32[16,4608]{1,0:T(8,128)} %moment2.1) | copy-start | bytes 884740
  46.0 17.3 %copy-start.1 = (f32[16,4608]{1,0:T(8,128)S(1)}, f32[16,4608]{1,0:T(8,128)}, u32[]{:S(2)}) copy-start(f32[16,4608]{1,0:T(8,128)} %moment1.1) | copy-start | bytes 884740
  46.0 17.4 %copy-start.2 = (f32[16,4608]{1,0:T(8,128)S(1)}, f32[16,4608]{1,0:T(8,128)}, u32[]{:S(2)}) copy-start(f32[16,4608]{1,0:T(8,128)} %master.1) | copy-start | bytes 884740
  47.0 16.3 %all-to-all-start.1 = ((f16[8,8,1152]{2,1,0:T(8,128)(2,1)}), f16[8,8,1152]{2,1,0:T(8,128)(2,1)S(1)}, u32[]{:S(2)}, u32[]{:S(2)}) async-start(f16[8,8,1152]{2,1,0:T(8,128)(2,1)} %convert_element_type.25), calls=%async_computation.1 | async-start | bytes 294912 | tf_op jit(solution)/shard_map/all_to_all | solution.py:112
  64.1 11.4 %all-to-all-start.2 = ((bf16[8,8,1152]{2,1,0:T(8,128)(2,1)}), bf16[8,8,1152]{2,1,0:T(8,128)(2,1)S(1)}, u32[]{:S(2)}, u32[]{:S(2)}) async-start(bf16[8,8,1152]{2,1,0:T(8,128)(2,1)} %broadcast_in_dim.6), calls=%async_computation.2 | async-start | bytes 294912 | tf_op jit(solution)/shard_map/all_to_all | solution.py:112
  67.5 2.9 %collective-permute-start.1 = (f32[1,8,1152]{2,1,0:T(8,128)S(1)}, f32[1,8,1152]{2,1,0:T(8,128)S(1)}, u32[]{:S(2)}, u32[]{:S(2)}) collective-permute-start(f32[1,8,1152]{2,1,0:T(8,128)S(1)} %get-tuple-element.18), channel_id=1, source_target_pairs={{0,32},{32,0},{64,96},{96,64},{1,33},{33,1},{65,97},{97,65},{2,34}... | collective-permute-start | bytes 110600 | tf_op jit(solution)/shard_map/ppermute | solution.py:140
  77.2 31.2 %all-to-all-start.3 = ((bf16[16,8,8,1152]{3,2,1,0:T(8,128)(2,1)}), bf16[16,8,8,1152]{3,2,1,0:T(8,128)(2,1)S(1)}, u32[]{:S(2)}, u32[]{:S(2)}) async-start(bf16[16,8,8,1152]{3,2,1,0:T(8,128)(2,1)} %broadcast_in_dim.7), calls=%async_computation.3 | async-start | bytes 4718592 | tf_op jit(solution)/shard_map/all_to_all | solution.py:112
  80.9 24.9 %collective-permute-start.2 = (f32[2,8,1152]{2,1,0:T(8,128)S(1)}, f32[2,8,1152]{2,1,0:T(8,128)S(1)}, u32[]{:S(2)}, u32[]{:S(2)}) collective-permute-start(f32[2,8,1152]{2,1,0:T(8,128)S(1)} %pad_maximum_fusion.1), channel_id=1, source_target_pairs={{0,64},{32,96},{64,0},{96,32},{1,65},{33,97},{65,1},{97,33},{2,66}... | collective-permute-start | bytes 221192 | tf_op jit(solution)/shard_map/ppermute | solution.py:143
  108.4 13.8 %collective-permute-start.4 = (bf16[8,16,8,1152]{3,2,1,0:T(8,128)(2,1)S(1)}, bf16[8,16,8,1152]{3,2,1,0:T(8,128)(2,1)S(1)}, u32[]{:S(2)}, u32[]{:S(2)}) collective-permute-start(bf16[8,16,8,1152]{3,2,1,0:T(8,128)(2,1)S(1)} %bitcast.6), channel_id=1, source_target_pairs={{0,1},{1,0},{2,3},{3,2},{4,5},{5,4},{6,7},{7,6},{8,9},{9,8},{10,11... | collective-permute-start | bytes 7077896 | tf_op jit(solution)/shard_map/ppermute | solution.py:148
  113.9 7.1 %collective-permute-start.3 = (f32[4,8,1152]{2,1,0:T(8,128)S(1)}, f32[4,8,1152]{2,1,0:T(8,128)S(1)}, u32[]{:S(2)}, u32[]{:S(2)}) collective-permute-start(f32[4,8,1152]{2,1,0:T(8,128)S(1)} %pad_maximum_fusion.mine), channel_id=1, source_target_pairs={{0,128},{128,0},{1,129},{129,1},{2,130},{130,2},{3,131},{131,3},{4... | collective-permute-start | bytes 442376 | tf_op jit(solution)/shard_map/ppermute | solution.py:146

commit v4 on v3

v4 whole, which is shorter than its diff:
```python
import jax
import jax.numpy as jnp
from jax import lax
from jax.experimental import pallas as pl
from jax.experimental.pallas import tpu as pltpu
from jax.sharding import Mesh, PartitionSpec as P

STEP = 10
XH, Y, XL, ZH, ZL, CORES = 2, 4, 2, 4, 2, 2
BIG = ("xh", "y", "xl", "zl")
SWAP = [(0, 1), (1, 0)]
LOW, COLS = 8, 1152
SHAPE = (XH, Y, XL, ZL, ZH, LOW, COLS)
WHOLE = (XL, ZH, ZL, CORES, XH, LOW, Y * COLS)
COPIES = XH * Y * ZL
VMEM = pl.BlockSpec(memory_space=pltpu.VMEM)
ANY = pl.BlockSpec(memory_space=pl.ANY)
SMALL = pltpu.CompilerParams(vmem_limit_bytes=2 * 2**20)


def views(whole, pieces, core):
    return [
        (whole.at[:, :, zl, core, xh, :, pl.ds(y * COLS, COLS)], pieces.at[xh, y, :, zl])
        for xh in range(XH)
        for y in range(Y)
        for zl in range(ZL)
    ]


def copy_all(pairs, sems):
    copies = [pltpu.make_async_copy(a, b, sems.at[k]) for k, (a, b) in enumerate(pairs)]
    for copy in copies:
        copy.start()
    for copy in copies:
        copy.wait()


def split_kernel(of_other, whole, pieces, sems):
    core = lax.axis_index("c")
    copy_all(views(whole, pieces, 1 - core if of_other else core), sems)


def split(of_other, whole):
    return pl.pallas_call(
        lambda *refs: split_kernel(of_other, *refs),
        out_shape=pltpu.VMEM(SHAPE, whole.dtype),
        in_specs=[ANY],
        out_specs=ANY,
        scratch_shapes=[pltpu.SemaphoreType.DMA((COPIES,))],
        compiler_params=SMALL,
        cost_estimate=pl.CostEstimate(flops=0, bytes_accessed=2 * whole.size, transcendentals=0),
        name="split_theirs" if of_other else "split_mine",
    )(whole)


def place_kernel(of_other, *refs):
    pieces, out, sems = refs[-3:]
    core = lax.axis_index("c")
    pairs = views(out, pieces, 1 - core if of_other else core)
    copy_all([(b, a) for a, b in pairs], sems)


def place(of_other, pieces, half=()):
    return pl.pallas_call(
        lambda *refs: place_kernel(of_other, *refs),
        out_shape=jax.ShapeDtypeStruct(WHOLE, pieces.dtype),
        in_specs=[ANY] * (len(half) + 1),
        out_specs=ANY,
        scratch_shapes=[pltpu.SemaphoreType.DMA((COPIES,))],
        input_output_aliases={0: 0} if half else {},
        compiler_params=SMALL,
        cost_estimate=pl.CostEstimate(flops=0, bytes_accessed=4 * pieces.size, transcendentals=0),
        name="place_theirs" if of_other else "place_mine",
    )(*half, pltpu.with_memory_space_constraint(pieces, pltpu.VMEM))


def adam(grad, master, moment1, moment2):
    moment1_new = 0.9 * moment1 + 0.1 * grad
    moment2_new = 0.95 * moment2 + 0.05 * grad * grad
    first_fix = 1.0 - 0.9**STEP
    second_fix = 1.0 - 0.95**STEP
    update = moment1_new / first_fix / (jnp.sqrt(moment2_new / second_fix) + 1e-08)
    master_new = master * (1.0 - 0.02 * 0.1) - 0.02 * update
    return master_new, moment1_new, moment2_new


def states_kernel(*refs):
    pieces, old, new = refs[: XH * Y], refs[XH * Y : -3], refs[-3:]
    xh, y = lax.axis_index("xh"), lax.axis_index("y")
    for m, piece in enumerate(pieces):
        rows = pl.ds(pl.multiple_of((xh ^ (m // Y)) * LOW, LOW), LOW)
        at = (rows, pl.ds(pl.multiple_of((y ^ (m % Y)) * COLS, 128), COLS))
        for ref, value in zip(new, adam(piece[...], *[ref[at] for ref in old])):
            ref[at] = value


def states(pieces, master, moment1, moment2):
    return pl.pallas_call(
        states_kernel,
        out_shape=[jax.ShapeDtypeStruct(master.shape, master.dtype)] * 3,
        in_specs=[VMEM] * (XH * Y + 3),
        out_specs=[VMEM] * 3,
        compiler_params=pltpu.CompilerParams(vmem_limit_bytes=8 * 2**20),
        cost_estimate=pl.CostEstimate(
            flops=20 * master.size, bytes_accessed=28 * master.size, transcendentals=master.size
        ),
        name="states",
    )(*pieces, master, moment1, moment2)


def exchange(chunks):
    return lax.all_to_all(chunks.reshape(-1, ZH, LOW, COLS), BIG, 0, 0, tiled=True)


def forward(chunk, d):
    return lax.ppermute(chunk, "zh", [(i, (i + d) % ZH) for i in range(ZH)])


def add(parts):
    return jnp.sum(parts.astype(jnp.float32), axis=0)


def per_device(gradients, master, moment1, moment2):
    xh, y, zh = (lax.axis_index(a) for a in ("xh", "y", "zh"))
    rows, width = gradients.shape[2:]
    big = XH * Y * XL * ZL
    whole = pltpu.with_memory_space_constraint(gradients.reshape(WHOLE), pltpu.HBM)

    came = lax.ppermute(split(True, whole), "c", SWAP)
    pair = split(False, whole).astype(jnp.float32) + came.astype(jnp.float32)
    column = add(exchange(pair.astype(jnp.float16))).astype(jnp.float16)

    def ahead(d):
        return lax.dynamic_index_in_dim(column, lax.rem(zh + d, ZH), 0, keepdims=False)

    parts = [ahead(0)] + [forward(ahead(d), d) for d in range(1, ZH)]
    grad = sum(part.astype(jnp.float32) for part in parts) / (big * ZH * CORES)

    def piece(state):
        return lax.dynamic_slice(state, (xh * LOW, y * COLS), (LOW, COLS))

    part = adam(grad, piece(master), piece(moment1), piece(moment2))[0].astype(jnp.bfloat16)
    behind = [part] + [forward(part, d) for d in range(1, ZH)]
    behind = jnp.stack(behind[::-1] + behind[:0:-1])
    column = lax.dynamic_slice_in_dim(behind, ZH - 1 - zh, ZH, 0)
    part = exchange(jnp.broadcast_to(column, (big, *column.shape))).reshape(SHAPE)

    def across(m):
        return lax.ppermute(grad, ("xh", "y"), [(i, i ^ m) for i in range(XH * Y)])

    pieces = [grad] + [across(m) for m in range(1, XH * Y)]
    part, pieces = lax.optimization_barrier((part, pieces))

    came = lax.ppermute(part, "c", SWAP)
    params = place(True, came, (place(False, part),))
    master_new, moment1_new, moment2_new = states(pieces, master, moment1, moment2)
    return master_new, moment1_new, moment2_new, params.reshape(rows, width)


def solution(mesh):
    sizes = (XH, Y, XL, ZH, ZL, CORES)
    fine = Mesh(mesh.devices.reshape(sizes), ("xh", "y", "xl", "zh", "zl", "c"))
    replica, shard = ("xh", "y"), ("xl", "zh", "zl", "c")
    state = P(shard, None)
    return jax.shard_map(
        per_device,
        mesh=fine,
        in_specs=(P(replica, shard, None, None), state, state, state),
        out_specs=(state, state, state, P()),
        check_vma=False,
    )
```

time: 126 us -> 125 us (level); the launches traced: 124 us -> 124 us
  blocking collectives: 35.5 us -> 0 us
  starting transfers between devices: 29.1 us -> 51.7 us
  waiting for transfers between devices: 46.8 us -> 59.8 us
    all_to_all x1 -> x0, blocking collectives: 35.5 us -> none  [exchange(): return lax.all_to_all(chunks, axes, 0, 0, tiled=True)]
    ppermute x3 -> x13, starting transfers between devices: 4.88 us -> 32.7 us  [the longest x7 17.4 us: across(): return lax.ppermute(grad, ('xh', 'y'), [(i, i ^ m) for i in range(XH * Y)])]
    all_to_all x3 -> x2, waiting for transfers between devices: 15.8 us -> 31.9 us  [exchange(): lax.all_to_all(chunks.reshape(-1, ZH, LOW, COLS), BIG, 0, 0, tiled=True)]
    all_to_all x3 -> x2, starting transfers between devices: 15.3 us -> 10.8 us  [exchange(): lax.all_to_all(chunks.reshape(-1, ZH, LOW, COLS), BIG, 0, 0, tiled=True)]
    ppermute x3 -> x13, waiting for transfers between devices: 28.5 us -> 24.2 us  [the longest x7 18.3 us: across(): return lax.ppermute(grad, ('xh', 'y'), [(i, i ^ m) for i in range(XH * Y)])]
    ppermute x1, waiting for transfers between devices: 0.01 us -> 1.44 us  [per_device(): came = lax.ppermute(part, 'c', SWAP)]
  transfers between devices with their start and end apart: 8 -> 17, of which waited for: 7 -> 10; matrix products, arithmetic and copies ran while one was open for 0% -> 0% of each run, Pallas kernels for 3% -> 4%
where the time goes in v4:
time: 125 us; the launch traced here: 124 us
  waiting for transfers between devices  59.8 us (48%)
  starting transfers between devices  51.7 us (41%)
  Pallas kernels  7.94 us (6%)
  other arithmetic  2.53 us (2%)
  local copies, waits for them, and re-layouts  1.69 us (1%)
    all_to_all x2, waiting for transfers between devices, exchange(): lax.all_to_all(chunks.reshape(-1, ZH, LOW, COLS), BIG, 0, 0, tiled=True)  31.9 us
    ppermute x7, waiting for transfers between devices, across(): return lax.ppermute(grad, ('xh', 'y'), [(i, i ^ m) for i in range(XH * Y)])  18.3 us
    ppermute x7, starting transfers between devices, across(): return lax.ppermute(grad, ('xh', 'y'), [(i, i ^ m) for i in range(XH * Y)])  17.4 us
    ppermute x6, starting transfers between devices, forward(): return lax.ppermute(chunk, 'zh', [(i, (i + d) % ZH) for i in range(ZH)])  15.3 us
    all_to_all x2, starting transfers between devices, exchange(): lax.all_to_all(chunks.reshape(-1, ZH, LOW, COLS), BIG, 0, 0, tiled=True)  10.8 us
    ppermute x6, waiting for transfers between devices, forward(): return lax.ppermute(chunk, 'zh', [(i, (i + d) % ZH) for i in range(ZH)])  5.85 us
    ppermute x1, starting transfers between devices, per_device(): came = lax.ppermute(part, 'c', SWAP)  4.8 us
    pallas_call x2, Pallas kernels, split(): pl.pallas_call(lambda *refs: split_kernel(of_other, *refs), out_shape=plt...  3.7 us
  transfers between devices with their start and end apart: 17, of which 10 were waited for; matrix products, arithmetic and copies ran while one was open for 0% of the time, Pallas kernels for 4%

profile of v4, /device:TPU:1, one launch (start us, length us, event | category | flops | bytes accessed | tf_op | source)
XLA Modules:
  0.0 124.5 jit_solution(7428815648441366371)
XLA Ops:
  0.6 1.9 %split_theirs.1 = bf16[2,4,2,2,4,8,1152]{6,5,4,3,2,1,0:T(8,128)(2,1)S(1)} custom-call(bf16[2,4,2,2,2,8,4608]{6,5,4,3,2,1,0:T(8,128)(2,1)} %bitcast.30), custom_call_target="tpu_custom_call" | custom-call | bytes 4718592 | tf_op jit(solution)/shard_map/split_theirs/pallas_call | solution.py:44
  2.5 3.3 %collective-permute-start = (bf16[2,4,2,2,4,8,1152]{6,5,4,3,2,1,0:T(8,128)(2,1)S(1)}, bf16[2,4,2,2,4,8,1152]{6,5,4,3,2,1,0:T(8,128)(2,1)S(1)}, u32[]{:S(2)}, u32[]{:S(2)}) collective-permute-start(bf16[2,4,2,2,4,8,1152]{6,5,4,3,2,1,0:T(8,128)(2,1)S(1)} %split_theirs.1), channel_id=1, source_target_pairs={{0,1},{1,0},{2,3},{3,2},{4,5},{5,4},{6,7},{7,6},{8,9},{9,8},{10,11... | collective-permute-start | bytes 7077896 | tf_op jit(solution)/shard_map/ppermute | solution.py:129
  5.8 1.8 %split_mine.1 = bf16[2,4,2,2,4,8,1152]{6,5,4,3,2,1,0:T(8,128)(2,1)S(1)} custom-call(bf16[2,4,2,2,2,8,4608]{6,5,4,3,2,1,0:T(8,128)(2,1)} %bitcast.31), custom_call_target="tpu_custom_call" | custom-call | bytes 4718592 | tf_op jit(solution)/shard_map/split_mine/pallas_call | solution.py:44
  7.7 2.3 %collective-permute-done = bf16[2,4,2,2,4,8,1152]{6,5,4,3,2,1,0:T(8,128)(2,1)S(1)} collective-permute-done((bf16[2,4,2,2,4,8,1152]{6,5,4,3,2,1,0:T(8,128)(2,1)S(1)}, bf16[2,4,2,2,4,8,1152]{6,5,4,3,2,1,0:T(8,128)(2,1)S(1)}, u32[]{:S(2)}, u32[]{:S(2)}) %collective-permute-start) | collective-permute-done | bytes 2359328 | tf_op jit(solution)/shard_map/ppermute | solution.py:129
  10.0 2.1 %add_convert_fusion = f16[2,4,2,2,4,8,1152]{6,5,4,3,2,1,0:T(8,128)(2,1)} fusion(bf16[2,4,2,2,4,8,1152]{6,5,4,3,2,1,0:T(8,128)(2,1)S(1)} %collective-permute-done, bf16[2,4,2,2,4,8,1152]{6,5,4,3,2,1,0:T(8,128)(2,1)S(1)} %split_mine.1), kind=kLoop, calls=%fused_computation.1 | loop fusion | flops 4718592 | bytes 7077888 | tf_op jit(solution)/shard_map/convert_element_type | solution.py:131
  12.1 6.7 %all-to-all-start = ((f16[32,4,8,1152]{3,2,1,0:T(8,128)(2,1)}), f16[32,4,8,1152]{3,2,1,0:T(8,128)(2,1)S(1)}, u32[]{:S(2)}, u32[]{:S(2)}) async-start(f16[32,4,8,1152]{3,2,1,0:T(8,128)(2,1)} %bitcast.1), calls=%async_computation | async-start | bytes 4718592 | tf_op jit(solution)/shard_map/all_to_all | solution.py:112
  18.9 31.9 %all-to-all-done = f16[32,4,8,1152]{3,2,1,0:T(8,128)(2,1)S(1)} async-done(((f16[32,4,8,1152]{3,2,1,0:T(8,128)(2,1)}), f16[32,4,8,1152]{3,2,1,0:T(8,128)(2,1)S(1)}, u32[]{:S(2)}, u32[]{:S(2)}) %all-to-all-start) | async-done | bytes 2359328 | tf_op jit(solution)/shard_map/all_to_all | solution.py:112
  51.1 3.1 %collective-permute-start.1 = (f16[8,1152]{1,0:T(8,128)(2,1)S(1)}, f16[8,1152]{1,0:T(8,128)(2,1)S(1)}, u32[]{:S(2)}, u32[]{:S(2)}) collective-permute-start(f16[8,1152]{1,0:T(8,128)(2,1)S(1)} %get-tuple-element.30), channel_id=1, source_target_pairs={{0,4},{4,8},{8,12},{12,0},{1,5},{5,9},{9,13},{13,1},{2,6},{6,10},{... | collective-permute-start | bytes 55304 | tf_op jit(solution)/shard_map/ppermute | solution.py:116
  54.2 4.2 %collective-permute-start.2 = (f16[8,1152]{1,0:T(8,128)(2,1)S(1)}, f16[8,1152]{1,0:T(8,128)(2,1)S(1)}, u32[]{:S(2)}, u32[]{:S(2)}) collective-permute-start(f16[8,1152]{1,0:T(8,128)(2,1)S(1)} %get-tuple-element.32), channel_id=1, source_target_pairs={{0,8},{4,12},{8,0},{12,4},{1,9},{5,13},{9,1},{13,5},{2,10},{6,14},... | collective-permute-start | bytes 55304 | tf_op jit(solution)/shard_map/ppermute | solution.py:116
  58.4 2.4 %collective-permute-start.3 = (f16[8,1152]{1,0:T(8,128)(2,1)S(1)}, f16[8,1152]{1,0:T(8,128)(2,1)S(1)}, u32[]{:S(2)}, u32[]{:S(2)}) collective-permute-start(f16[8,1152]{1,0:T(8,128)(2,1)S(1)} %get-tuple-element.31), channel_id=1, source_target_pairs={{0,12},{4,0},{8,4},{12,8},{1,13},{5,1},{9,5},{13,9},{2,14},{6,2},{... | collective-permute-start | bytes 55304 | tf_op jit(solution)/shard_map/ppermute | solution.py:116
  62.3 3.5 %collective-permute-start.4 = (bf16[8,1152]{1,0:T(8,128)(2,1)S(1)}, bf16[8,1152]{1,0:T(8,128)(2,1)S(1)}, u32[]{:S(2)}, u32[]{:S(2)}) collective-permute-start(bf16[8,1152]{1,0:T(8,128)(2,1)S(1)} %get-tuple-element.29), channel_id=1, source_target_pairs={{0,12},{4,0},{8,4},{12,8},{1,13},{5,1},{9,5},{13,9},{2,14},{6,2},{... | collective-permute-start | bytes 55304 | tf_op jit(solution)/shard_map/ppermute | solution.py:116
  65.8 1.7 %collective-permute-start.5 = (bf16[8,1152]{1,0:T(8,128)(2,1)S(1)}, bf16[8,1152]{1,0:T(8,128)(2,1)S(1)}, u32[]{:S(2)}, u32[]{:S(2)}) collective-permute-start(bf16[8,1152]{1,0:T(8,128)(2,1)S(1)} %get-tuple-element.29), channel_id=1, source_target_pairs={{0,8},{4,12},{8,0},{12,4},{1,9},{5,13},{9,1},{13,5},{2,10},{6,14},... | collective-permute-start | bytes 55304 | tf_op jit(solution)/shard_map/ppermute | solution.py:116
  67.9 4.4 %collective-permute-done.5 = bf16[8,1152]{1,0:T(8,128)(2,1)S(1)} collective-permute-done((bf16[8,1152]{1,0:T(8,128)(2,1)S(1)}, bf16[8,1152]{1,0:T(8,128)(2,1)S(1)}, u32[]{:S(2)}, u32[]{:S(2)}) %collective-permute-start.5) | collective-permute-done | bytes 18464 | tf_op jit(solution)/shard_map/ppermute | solution.py:116
  72.5 1.6 %broadcast_in_dim.3 = bf16[32,4,8,1152]{3,2,1,0:T(8,128)(2,1)} broadcast(bf16[4,8,1152]{2,1,0:T(8,128)(2,1)S(1)} %constant_dynamic-slice_fusion), dimensions={1,2,3} | broadcast | bytes 2433024 | tf_op jit(solution)/shard_map/broadcast_in_dim | solution.py:146
  74.0 4.2 %all-to-all-start.1 = ((bf16[32,4,8,1152]{3,2,1,0:T(8,128)(2,1)}), bf16[32,4,8,1152]{3,2,1,0:T(8,128)(2,1)S(1)}, u32[]{:S(2)}, u32[]{:S(2)}) async-start(bf16[32,4,8,1152]{3,2,1,0:T(8,128)(2,1)} %broadcast_in_dim.3), calls=%async_computation.1 | async-start | bytes 4718592 | tf_op jit(solution)/shard_map/all_to_all | solution.py:112
  78.2 2.8 %collective-permute-start.10 = (f32[8,1152]{1,0:T(8,128)S(1)}, f32[8,1152]{1,0:T(8,128)S(1)}, u32[]{:S(2)}, u32[]{:S(2)}) collective-permute-start(f32[8,1152]{1,0:T(8,128)S(1)} %get-tuple-element.16.refs_0_), channel_id=1, source_target_pairs={{0,128},{32,160},{64,192},{96,224},{128,0},{160,32},{192,64},{224,... | collective-permute-start | bytes 110600 | tf_op jit(solution)/shard_map/ppermute | solution.py:149
  82.2 4.9 %collective-permute-start.12 = (f32[8,1152]{1,0:T(8,128)S(1)}, f32[8,1152]{1,0:T(8,128)S(1)}, u32[]{:S(2)}, u32[]{:S(2)}) collective-permute-start(f32[8,1152]{1,0:T(8,128)S(1)} %get-tuple-element.16.refs_0_), channel_id=1, source_target_pairs={{0,192},{32,224},{64,128},{96,160},{128,64},{160,96},{192,0},{224,... | collective-permute-start | bytes 110600 | tf_op jit(solution)/shard_map/ppermute | solution.py:149
  87.3 15.7 %collective-permute-done.10.refs_4_ = f32[8,1152]{1,0:T(8,128)S(1)} collective-permute-done((f32[8,1152]{1,0:T(8,128)S(1)}, f32[8,1152]{1,0:T(8,128)S(1)}, u32[]{:S(2)}, u32[]{:S(2)}) %collective-permute-start.10) | collective-permute-done | bytes 36896 | tf_op jit(solution)/shard_map/ppermute | solution.py:149
  103.0 6.4 %collective-permute-start.8 = (f32[8,1152]{1,0:T(8,128)S(1)}, f32[8,1152]{1,0:T(8,128)S(1)}, u32[]{:S(2)}, u32[]{:S(2)}) collective-permute-start(f32[8,1152]{1,0:T(8,128)S(1)} %get-tuple-element.16.refs_0_), channel_id=1, source_target_pairs={{0,64},{32,96},{64,0},{96,32},{128,192},{160,224},{192,128},{224,1... | collective-permute-start | bytes 110600 | tf_op jit(solution)/shard_map/ppermute | solution.py:149
  109.5 1.9 %collective-permute-start.9 = (f32[8,1152]{1,0:T(8,128)S(1)}, f32[8,1152]{1,0:T(8,128)S(1)}, u32[]{:S(2)}, u32[]{:S(2)}) collective-permute-start(f32[8,1152]{1,0:T(8,128)S(1)} %get-tuple-element.16.refs_0_), channel_id=1, source_target_pairs={{0,96},{32,64},{64,32},{96,0},{128,224},{160,192},{192,160},{224,1... | collective-permute-start | bytes 110600 | tf_op jit(solution)/shard_map/ppermute | solution.py:149
  114.0 4.8 %collective-permute-start.14 = (bf16[2,4,2,2,4,8,1152]{6,5,4,3,2,1,0:T(8,128)(2,1)S(1)}, bf16[2,4,2,2,4,8,1152]{6,5,4,3,2,1,0:T(8,128)(2,1)S(1)}, u32[]{:S(2)}, u32[]{:S(2)}) collective-permute-start(bf16[2,4,2,2,4,8,1152]{6,5,4,3,2,1,0:T(8,128)(2,1)S(1)} %bitcast.28), channel_id=1, source_target_pairs={{0,1},{1,0},{2,3},{3,2},{4,5},{5,4},{6,7},{7,6},{8,9},{9,8},{10,11... | collective-permute-start | bytes 7077896 | tf_op jit(solution)/shard_map/ppermute | solution.py:154
  118.8 1.5 %place_mine.1.refs_0_ = bf16[2,4,2,2,2,8,4608]{6,5,4,3,2,1,0:T(8,128)(2,1)} custom-call(bf16[2,4,2,2,4,8,1152]{6,5,4,3,2,1,0:T(8,128)(2,1)S(1)} %bitcast.29), custom_call_target="tpu_custom_call" | custom-call | bytes 4718592 | tf_op jit(solution)/shard_map/place_mine/pallas_call | solution.py:64
  121.5 1.4 %collective-permute-done.14.refs_1_ = bf16[2,4,2,2,4,8,1152]{6,5,4,3,2,1,0:T(8,128)(2,1)S(1)} collective-permute-done((bf16[2,4,2,2,4,8,1152]{6,5,4,3,2,1,0:T(8,128)(2,1)S(1)}, bf16[2,4,2,2,4,8,1152]{6,5,4,3,2,1,0:T(8,128)(2,1)S(1)}, u32[]{:S(2)}, u32[]{:S(2)}) %collective-permute-start.14) | collective-permute-done | bytes 2359328 | tf_op jit(solution)/shard_map/ppermute | solution.py:154
  122.9 1.5 %place_theirs.1 = bf16[2,4,2,2,2,8,4608]{6,5,4,3,2,1,0:T(8,128)(2,1)} custom-call(bf16[2,4,2,2,2,8,4608]{6,5,4,3,2,1,0:T(8,128)(2,1)} %place_mine.1.refs_0_, bf16[2,4,2,2,4,8,1152]{6,5,4,3,2,1,0:T(8,128)(2,1)S(1)} %collective-permute-done.14.refs_1_), custom_call_target="tpu_custom_call", output_to_operand_aliasing={{}: (0, {})} | custom-call | bytes 4718592 | tf_op jit(solution)/shard_map/place_theirs/pallas_call | solution.py:64
  (35 shorter events, 7.6 us)
Async XLA Ops:
  2.5 7.5 %collective-permute-start = (bf16[2,4,2,2,4,8,1152]{6,5,4,3,2,1,0:T(8,128)(2,1)S(1)}, bf16[2,4,2,2,4,8,1152]{6,5,4,3,2,1,0:T(8,128)(2,1)S(1)}, u32[]{:S(2)}, u32[]{:S(2)}) collective-permute-start(bf16[2,4,2,2,4,8,1152]{6,5,4,3,2,1,0:T(8,128)(2,1)S(1)} %split_theirs.1), channel_id=1, source_target_pairs={{0,1},{1,0},{2,3},{3,2},{4,5},{5,4},{6,7},{7,6},{8,9},{9,8},{10,11... | collective-permute-start | bytes 7077896 | tf_op jit(solution)/shard_map/ppermute | solution.py:129
  12.1 38.6 %all-to-all-start = ((f16[32,4,8,1152]{3,2,1,0:T(8,128)(2,1)}), f16[32,4,8,1152]{3,2,1,0:T(8,128)(2,1)S(1)}, u32[]{:S(2)}, u32[]{:S(2)}) async-start(f16[32,4,8,1152]{3,2,1,0:T(8,128)(2,1)} %bitcast.1), calls=%async_computation | async-start | bytes 4718592 | tf_op jit(solution)/shard_map/all_to_all | solution.py:112
  18.8 43.4 %copy-start = (f32[16,4608]{1,0:T(8,128)S(1)}, f32[16,4608]{1,0:T(8,128)}, u32[]{:S(2)}) copy-start(f32[16,4608]{1,0:T(8,128)} %refs_10_.1) | copy-start | bytes 884740
  18.8 43.4 %copy-start.1 = (f32[16,4608]{1,0:T(8,128)S(1)}, f32[16,4608]{1,0:T(8,128)}, u32[]{:S(2)}) copy-start(f32[16,4608]{1,0:T(8,128)} %refs_9_.1) | copy-start | bytes 884740
  18.8 43.4 %copy-start.2 = (f32[16,4608]{1,0:T(8,128)S(1)}, f32[16,4608]{1,0:T(8,128)}, u32[]{:S(2)}) copy-start(f32[16,4608]{1,0:T(8,128)} %refs_8_.1) | copy-start | bytes 884740
  51.1 9.7 %collective-permute-start.1 = (f16[8,1152]{1,0:T(8,128)(2,1)S(1)}, f16[8,1152]{1,0:T(8,128)(2,1)S(1)}, u32[]{:S(2)}, u32[]{:S(2)}) collective-permute-start(f16[8,1152]{1,0:T(8,128)(2,1)S(1)} %get-tuple-element.30), channel_id=1, source_target_pairs={{0,4},{4,8},{8,12},{12,0},{1,5},{5,9},{9,13},{13,1},{2,6},{6,10},{... | collective-permute-start | bytes 55304 | tf_op jit(solution)/shard_map/ppermute | solution.py:116
  54.2 6.6 %collective-permute-start.2 = (f16[8,1152]{1,0:T(8,128)(2,1)S(1)}, f16[8,1152]{1,0:T(8,128)(2,1)S(1)}, u32[]{:S(2)}, u32[]{:S(2)}) collective-permute-start(f16[8,1152]{1,0:T(8,128)(2,1)S(1)} %get-tuple-element.32), channel_id=1, source_target_pairs={{0,8},{4,12},{8,0},{12,4},{1,9},{5,13},{9,1},{13,5},{2,10},{6,14},... | collective-permute-start | bytes 55304 | tf_op jit(solution)/shard_map/ppermute | solution.py:116
  58.4 3.8 %collective-permute-start.3 = (f16[8,1152]{1,0:T(8,128)(2,1)S(1)}, f16[8,1152]{1,0:T(8,128)(2,1)S(1)}, u32[]{:S(2)}, u32[]{:S(2)}) collective-permute-start(f16[8,1152]{1,0:T(8,128)(2,1)S(1)} %get-tuple-element.31), channel_id=1, source_target_pairs={{0,12},{4,0},{8,4},{12,8},{1,13},{5,1},{9,5},{13,9},{2,14},{6,2},{... | collective-permute-start | bytes 55304 | tf_op jit(solution)/shard_map/ppermute | solution.py:116
  62.3 5.7 %collective-permute-start.4 = (bf16[8,1152]{1,0:T(8,128)(2,1)S(1)}, bf16[8,1152]{1,0:T(8,128)(2,1)S(1)}, u32[]{:S(2)}, u32[]{:S(2)}) collective-permute-start(bf16[8,1152]{1,0:T(8,128)(2,1)S(1)} %get-tuple-element.29), channel_id=1, source_target_pairs={{0,12},{4,0},{8,4},{12,8},{1,13},{5,1},{9,5},{13,9},{2,14},{6,2},{... | collective-permute-start | bytes 55304 | tf_op jit(solution)/shard_map/ppermute | solution.py:116
  65.8 6.6 %collective-permute-start.5 = (bf16[8,1152]{1,0:T(8,128)(2,1)S(1)}, bf16[8,1152]{1,0:T(8,128)(2,1)S(1)}, u32[]{:S(2)}, u32[]{:S(2)}) collective-permute-start(bf16[8,1152]{1,0:T(8,128)(2,1)S(1)} %get-tuple-element.29), channel_id=1, source_target_pairs={{0,8},{4,12},{8,0},{12,4},{1,9},{5,13},{9,1},{13,5},{2,10},{6,14},... | collective-permute-start | bytes 55304 | tf_op jit(solution)/shard_map/ppermute | solution.py:116
  67.4 4.9 %collective-permute-start.6 = (bf16[8,1152]{1,0:T(8,128)(2,1)S(1)}, bf16[8,1152]{1,0:T(8,128)(2,1)S(1)}, u32[]{:S(2)}, u32[]{:S(2)}) collective-permute-start(bf16[8,1152]{1,0:T(8,128)(2,1)S(1)} %get-tuple-element.29), channel_id=1, source_target_pairs={{0,4},{4,8},{8,12},{12,0},{1,5},{5,9},{9,13},{13,1},{2,6},{6,10},{... | collective-permute-start | bytes 55304 | tf_op jit(solution)/shard_map/ppermute | solution.py:116
  74.0 39.9 %all-to-all-start.1 = ((bf16[32,4,8,1152]{3,2,1,0:T(8,128)(2,1)}), bf16[32,4,8,1152]{3,2,1,0:T(8,128)(2,1)S(1)}, u32[]{:S(2)}, u32[]{:S(2)}) async-start(bf16[32,4,8,1152]{3,2,1,0:T(8,128)(2,1)} %broadcast_in_dim.3), calls=%async_computation.1 | async-start | bytes 4718592 | tf_op jit(solution)/shard_map/all_to_all | solution.py:112
  78.2 24.8 %collective-permute-start.10 = (f32[8,1152]{1,0:T(8,128)S(1)}, f32[8,1152]{1,0:T(8,128)S(1)}, u32[]{:S(2)}, u32[]{:S(2)}) collective-permute-start(f32[8,1152]{1,0:T(8,128)S(1)} %get-tuple-element.16.refs_0_), channel_id=1, source_target_pairs={{0,128},{32,160},{64,192},{96,224},{128,0},{160,32},{192,64},{224,... | collective-permute-start | bytes 110600 | tf_op jit(solution)/shard_map/ppermute | solution.py:149
  81.0 28.4 %collective-permute-start.11 = (f32[8,1152]{1,0:T(8,128)S(1)}, f32[8,1152]{1,0:T(8,128)S(1)}, u32[]{:S(2)}, u32[]{:S(2)}) collective-permute-start(f32[8,1152]{1,0:T(8,128)S(1)} %get-tuple-element.16.refs_0_), channel_id=1, source_target_pairs={{0,160},{32,128},{64,224},{96,192},{128,32},{160,0},{192,96},{224,... | collective-permute-start | bytes 110600 | tf_op jit(solution)/shard_map/ppermute | solution.py:149
  82.2 29.8 %collective-permute-start.12 = (f32[8,1152]{1,0:T(8,128)S(1)}, f32[8,1152]{1,0:T(8,128)S(1)}, u32[]{:S(2)}, u32[]{:S(2)}) collective-permute-start(f32[8,1152]{1,0:T(8,128)S(1)} %get-tuple-element.16.refs_0_), channel_id=1, source_target_pairs={{0,192},{32,224},{64,128},{96,160},{128,64},{160,96},{192,0},{224,... | collective-permute-start | bytes 110600 | tf_op jit(solution)/shard_map/ppermute | solution.py:149
  87.1 25.0 %collective-permute-start.13 = (f32[8,1152]{1,0:T(8,128)S(1)}, f32[8,1152]{1,0:T(8,128)S(1)}, u32[]{:S(2)}, u32[]{:S(2)}) collective-permute-start(f32[8,1152]{1,0:T(8,128)S(1)} %get-tuple-element.16.refs_0_), channel_id=1, source_target_pairs={{0,224},{32,192},{64,160},{96,128},{128,96},{160,64},{192,32},{224... | collective-permute-start | bytes 110600 | tf_op jit(solution)/shard_map/ppermute | solution.py:149
  87.3 24.8 %collective-permute-start.7 = (f32[8,1152]{1,0:T(8,128)S(1)}, f32[8,1152]{1,0:T(8,128)S(1)}, u32[]{:S(2)}, u32[]{:S(2)}) collective-permute-start(f32[8,1152]{1,0:T(8,128)S(1)} %get-tuple-element.16.refs_0_), channel_id=1, source_target_pairs={{0,32},{32,0},{64,96},{96,64},{128,160},{160,128},{192,224},{224,1... | collective-permute-start | bytes 110600 | tf_op jit(solution)/shard_map/ppermute | solution.py:149
  103.0 9.7 %collective-permute-start.8 = (f32[8,1152]{1,0:T(8,128)S(1)}, f32[8,1152]{1,0:T(8,128)S(1)}, u32[]{:S(2)}, u32[]{:S(2)}) collective-permute-start(f32[8,1152]{1,0:T(8,128)S(1)} %get-tuple-element.16.refs_0_), channel_id=1, source_target_pairs={{0,64},{32,96},{64,0},{96,32},{128,192},{160,224},{192,128},{224,1... | collective-permute-start | bytes 110600 | tf_op jit(solution)/shard_map/ppermute | solution.py:149
  109.5 4.5 %collective-permute-start.9 = (f32[8,1152]{1,0:T(8,128)S(1)}, f32[8,1152]{1,0:T(8,128)S(1)}, u32[]{:S(2)}, u32[]{:S(2)}) collective-permute-start(f32[8,1152]{1,0:T(8,128)S(1)} %get-tuple-element.16.refs_0_), channel_id=1, source_target_pairs={{0,96},{32,64},{64,32},{96,0},{128,224},{160,192},{192,160},{224,1... | collective-permute-start | bytes 110600 | tf_op jit(solution)/shard_map/ppermute | solution.py:149
  114.0 9.0 %collective-permute-start.14 = (bf16[2,4,2,2,4,8,1152]{6,5,4,3,2,1,0:T(8,128)(2,1)S(1)}, bf16[2,4,2,2,4,8,1152]{6,5,4,3,2,1,0:T(8,128)(2,1)S(1)}, u32[]{:S(2)}, u32[]{:S(2)}) collective-permute-start(bf16[2,4,2,2,4,8,1152]{6,5,4,3,2,1,0:T(8,128)(2,1)S(1)} %bitcast.28), channel_id=1, source_target_pairs={{0,1},{1,0},{2,3},{3,2},{4,5},{5,4},{6,7},{7,6},{8,9},{9,8},{10,11... | collective-permute-start | bytes 7077896 | tf_op jit(solution)/shard_map/ppermute | solution.py:154

commit v5 on v4

v5 whole, which is shorter than its diff:
```python
import jax
import jax.numpy as jnp
from jax import lax
from jax.experimental import pallas as pl
from jax.experimental.pallas import tpu as pltpu
from jax.sharding import Mesh, PartitionSpec as P

STEP = 10
XH, Y, XL, ZH, ZM, ZL, CORES = 2, 4, 2, 2, 2, 2, 2
BIG = ("xh", "y", "xl", "zl")
SWAP = [(0, 1), (1, 0)]
LOW, COLS = 8, 1152
SHAPE = (XH, Y, XL, ZL, ZH, ZM, LOW, COLS)
WHOLE = (XL, ZH, ZM, ZL, CORES, XH, LOW, Y * COLS)
COPIES = XH * Y * ZH * ZM
STATES = 3
VMEM = pl.BlockSpec(memory_space=pltpu.VMEM)
ANY = pl.BlockSpec(memory_space=pl.ANY)
SMALL = pltpu.CompilerParams(vmem_limit_bytes=2 * 2**20)


def views(whole, pieces, core):
    zh, zm = lax.axis_index("zh"), lax.axis_index("zm")
    return [
        (whole.at[:, zh ^ j, zm ^ k, :, core, xh, :, pl.ds(y * COLS, COLS)], pieces.at[xh, y, :, :, j, k])
        for xh in range(XH)
        for y in range(Y)
        for j in range(ZH)
        for k in range(ZM)
    ]


def copy_all(pairs, sems):
    copies = [pltpu.make_async_copy(a, b, sems.at[k]) for k, (a, b) in enumerate(pairs)]
    for copy in copies:
        copy.start()
    for copy in copies:
        copy.wait()


def split_theirs_kernel(whole, pieces, sems):
    copy_all(views(whole, pieces, 1 - lax.axis_index("c")), sems)


def split_mine_kernel(whole, master, moment1, moment2, pieces, olds, sems):
    rows = pl.ds(pl.multiple_of(lax.axis_index("xh") * LOW, LOW), LOW)
    cols = pl.ds(pl.multiple_of(lax.axis_index("y") * COLS, 128), COLS)
    states = [(state.at[rows, cols], olds.at[i]) for i, state in enumerate((master, moment1, moment2))]
    copy_all(views(whole, pieces, lax.axis_index("c")) + states, sems)


def split_theirs(whole):
    return pl.pallas_call(
        split_theirs_kernel,
        out_shape=pltpu.VMEM(SHAPE, whole.dtype),
        in_specs=[ANY],
        out_specs=ANY,
        scratch_shapes=[pltpu.SemaphoreType.DMA((COPIES,))],
        compiler_params=SMALL,
        cost_estimate=pl.CostEstimate(flops=0, bytes_accessed=2 * whole.size, transcendentals=0),
        name="split_theirs",
    )(whole)


def split_mine(whole, *states):
    return pl.pallas_call(
        split_mine_kernel,
        out_shape=[pltpu.VMEM(SHAPE, whole.dtype), pltpu.VMEM((STATES, LOW, COLS), jnp.float32)],
        in_specs=[ANY] * (1 + STATES),
        out_specs=[ANY] * 2,
        scratch_shapes=[pltpu.SemaphoreType.DMA((COPIES + STATES,))],
        compiler_params=SMALL,
        cost_estimate=pl.CostEstimate(flops=0, bytes_accessed=2 * whole.size, transcendentals=0),
        name="split_mine",
    )(whole, *states)


def place_kernel(of_other, *refs):
    pieces, out, sems = refs[-3:]
    core = lax.axis_index("c")
    pairs = views(out, pieces, 1 - core if of_other else core)
    copy_all([(b, a) for a, b in pairs], sems)


def place(of_other, pieces, half=()):
    return pl.pallas_call(
        lambda *refs: place_kernel(of_other, *refs),
        out_shape=jax.ShapeDtypeStruct(WHOLE, pieces.dtype),
        in_specs=[ANY] * (len(half) + 1),
        out_specs=ANY,
        scratch_shapes=[pltpu.SemaphoreType.DMA((COPIES,))],
        input_output_aliases={0: 0} if half else {},
        compiler_params=SMALL,
        cost_estimate=pl.CostEstimate(flops=0, bytes_accessed=4 * pieces.size, transcendentals=0),
        name="place_theirs" if of_other else "place_mine",
    )(*half, pltpu.with_memory_space_constraint(pieces, pltpu.VMEM))


def adam(grad, master, moment1, moment2):
    moment1_new = 0.9 * moment1 + 0.1 * grad
    moment2_new = 0.95 * moment2 + 0.05 * grad * grad
    first_fix = 1.0 - 0.9**STEP
    second_fix = 1.0 - 0.95**STEP
    update = moment1_new / first_fix / (jnp.sqrt(moment2_new / second_fix) + 1e-08)
    master_new = master * (1.0 - 0.02 * 0.1) - 0.02 * update
    return master_new, moment1_new, moment2_new


def new_states_kernel(mine, others, *refs):
    old, new = refs[:3], refs[3:]
    xh, y = lax.axis_index("xh"), lax.axis_index("y")
    for k in range(XH * Y // 2):
        for grad, low in ((mine[k], 0), (others[k], 1)):
            rows = pl.ds(pl.multiple_of((xh ^ (k % 2)) * LOW, LOW), LOW)
            at = (rows, pl.ds(pl.multiple_of((y ^ (k // 2 * 2 + low)) * COLS, 128), COLS))
            for ref, value in zip(new, adam(grad, *[ref[at] for ref in old])):
                ref[at] = value


def new_states(mine, others, master, moment1, moment2):
    return pl.pallas_call(
        new_states_kernel,
        out_shape=[jax.ShapeDtypeStruct(master.shape, master.dtype)] * 3,
        in_specs=[VMEM] * 5,
        out_specs=[VMEM] * 3,
        compiler_params=pltpu.CompilerParams(vmem_limit_bytes=8 * 2**20),
        cost_estimate=pl.CostEstimate(
            flops=20 * master.size, bytes_accessed=28 * master.size, transcendentals=master.size
        ),
        name="new_states",
    )(mine, others, master, moment1, moment2)


def exchange(chunks):
    return lax.all_to_all(chunks.reshape(-1, ZH, ZM, LOW, COLS), BIG, 0, 0, tiled=True)


def partner(a, axis, bit=1):
    return lax.ppermute(a, axis, [(i, i ^ bit) for i in range(lax.axis_size(axis))])


def halve(a, axis):
    return a[0] + partner(a[1].astype(jnp.float16), axis).astype(jnp.float32)


def add(parts):
    return jnp.sum(parts.astype(jnp.float32), axis=0)


def per_device(gradients, *states):
    rows, width = gradients.shape[2:]
    big = XH * Y * XL * ZL

    def in_hbm(a):
        return pltpu.with_memory_space_constraint(a, pltpu.HBM)

    whole = in_hbm(gradients.reshape(WHOLE))
    came = lax.ppermute(split_theirs(whole), "c", SWAP)
    pair, olds = split_mine(whole, *[in_hbm(state) for state in states])
    pair = pair.astype(jnp.float32) + came.astype(jnp.float32)
    column = add(exchange(pair.astype(jnp.float16)))

    grad = halve(halve(column, "zh"), "zm") / (big * ZH * ZM * CORES)

    part = adam(grad, *olds)[0].astype(jnp.bfloat16)
    mine = grad[None]
    part = jnp.stack([part, partner(part, "zm")])
    mine = jnp.concatenate([mine, partner(mine, "xh")])
    part, mine = lax.optimization_barrier((part, mine))
    part = jnp.stack([part, partner(part, "zh")])
    mine = jnp.concatenate([mine, partner(mine, "y", 2)])
    part, mine = lax.optimization_barrier((part, mine))
    part = exchange(jnp.broadcast_to(part, (big, *part.shape))).reshape(SHAPE)
    part, mine = lax.optimization_barrier((part, mine))
    came = lax.ppermute(part, "c", SWAP)
    others = partner(mine, "y", 1)
    params = place(True, came, (place(False, part),))
    return *new_states(mine, others, *states), params.reshape(rows, width)


def solution(mesh):
    sizes = (XH, Y, XL, ZH, ZM, ZL, CORES)
    fine = Mesh(mesh.devices.reshape(sizes), ("xh", "y", "xl", "zh", "zm", "zl", "c"))
    replica, shard = ("xh", "y"), ("xl", "zh", "zm", "zl", "c")
    state = P(shard, None)
    return jax.shard_map(
        per_device,
        mesh=fine,
        in_specs=(P(replica, shard, None, None), state, state, state),
        out_specs=(state, state, state, P()),
        check_vma=False,
    )
```

time: 125 us -> 121 us (0.968)
  blocking collectives: 0 us -> 67.2 us
  waiting for transfers between devices: 59.8 us -> 15.9 us
  starting transfers between devices: 51.7 us -> 26.9 us
  local copies, waits for them, and re-layouts: 1.69 us -> 0.18 us
  other arithmetic: 2.53 us -> 1.19 us
    all_to_all x0 -> x2, blocking collectives: none -> 67.2 us  [exchange(): lax.all_to_all(chunks.reshape(-1, ZH, ZM, LOW, COLS), BIG, 0, 0, tiled=True)]
    all_to_all x2 -> x0, waiting for transfers between devices: 31.9 us -> none  [exchange(): lax.all_to_all(chunks.reshape(-1, ZH, LOW, COLS), BIG, 0, 0, tiled=True)]
    ppermute x14 -> x8, starting transfers between devices: 36.1 us -> 20 us  [the longest x7 16.7 us: partner(): lax.ppermute(a, axis, [(i, i ^ bit) for i in range(lax.axis_size(axis))])]
    all_to_all x2 -> x0, starting transfers between devices: 10.8 us -> none  [exchange(): lax.all_to_all(chunks.reshape(-1, ZH, LOW, COLS), BIG, 0, 0, tiled=True)]
    ppermute x14 -> x8, waiting for transfers between devices: 26.5 us -> 15.9 us  [the longest x7 13.7 us: partner(): lax.ppermute(a, axis, [(i, i ^ bit) for i in range(lax.axis_size(axis))])]
    ppermute x1, starting transfers between devices: 4.8 us -> 6.95 us  [per_device(): came = lax.ppermute(part, 'c', SWAP)]
    ppermute x1, waiting for transfers between devices: 1.44 us -> 0.01 us  [per_device(): came = lax.ppermute(part, 'c', SWAP)]
    broadcast_in_dim x1, local copies, waits for them, and re-layouts: 1.57 us -> 0.17 us  [per_device(): part = exchange(jnp.broadcast_to(part, (big, *part.shape))).reshape(SHAPE)]
  transfers between devices with their start and end apart: 17 -> 9, of which waited for: 10 -> 7; matrix products, arithmetic and copies ran while one was open for 0% -> 0% of each run, Pallas kernels for 4% -> 4%
where the time goes in v5:
time: 121 us
  blocking collectives  67.2 us (56%)
  starting transfers between devices  26.9 us (22%)
  waiting for transfers between devices  15.9 us (13%)
  Pallas kernels  8.57 us (7%)
    all_to_all x2, blocking collectives, exchange(): lax.all_to_all(chunks.reshape(-1, ZH, ZM, LOW, COLS), BIG, 0, 0, tiled=True)  67.2 us
    ppermute x7, starting transfers between devices, partner(): lax.ppermute(a, axis, [(i, i ^ bit) for i in range(lax.axis_size(axis))])  16.7 us
    ppermute x7, waiting for transfers between devices, partner(): lax.ppermute(a, axis, [(i, i ^ bit) for i in range(lax.axis_size(axis))])  13.7 us
    ppermute x1, starting transfers between devices, per_device(): came = lax.ppermute(part, 'c', SWAP)  6.95 us
    pallas_call x2, Pallas kernels, place(): pl.pallas_call(lambda *refs: place_kernel(of_other, *refs), out_shape=jax...  3.34 us
    ppermute x1, starting transfers between devices, per_device(): came = lax.ppermute(split_theirs(whole), 'c', SWAP)  3.33 us
  transfers between devices with their start and end apart: 9, of which 7 were waited for; matrix products, arithmetic and copies ran while one was open for 0% of the time, Pallas kernels for 4%

profile of v5, /device:TPU:1, one launch (start us, length us, event | category | flops | bytes accessed | tf_op | source)
XLA Modules:
  0.0 120.7 jit_solution(10758198634160756137)
XLA Ops:
  0.6 2.0 %split_theirs.1 = bf16[2,4,2,2,2,2,8,1152]{7,6,5,4,3,2,1,0:T(8,128)(2,1)S(1)} custom-call(bf16[2,2,2,2,2,2,8,4608]{7,6,5,4,3,2,1,0:T(8,128)(2,1)} %bitcast.56), custom_call_target="tpu_custom_call" | custom-call | bytes 4718592 | tf_op jit(solution)/shard_map/split_theirs/pallas_call | solution.py:53
  2.7 3.3 %collective-permute-start = (bf16[2,4,2,2,2,2,8,1152]{7,6,5,4,3,2,1,0:T(8,128)(2,1)S(1)}, bf16[2,4,2,2,2,2,8,1152]{7,6,5,4,3,2,1,0:T(8,128)(2,1)S(1)}, u32[]{:S(2)}, u32[]{:S(2)}) collective-permute-start(bf16[2,4,2,2,2,2,8,1152]{7,6,5,4,3,2,1,0:T(8,128)(2,1)S(1)} %split_theirs.1), channel_id=1, source_target_pairs={{0,1},{1,0},{2,3},{3,2},{4,5},{5,4},{6,7},{7,6},{8,9},{9,8},{10,11... | collective-permute-start | bytes 7077896 | tf_op jit(solution)/shard_map/ppermute | solution.py:158
  6.0 2.0 %split_mine.1 = (bf16[2,4,2,2,2,2,8,1152]{7,6,5,4,3,2,1,0:T(8,128)(2,1)S(1)}, f32[3,8,1152]{2,1,0:T(8,128)S(1)}) custom-call(bf16[2,2,2,2,2,2,8,4608]{7,6,5,4,3,2,1,0:T(8,128)(2,1)} %bitcast.57, f32[16,4608]{1,0:T(8,128)} %refs_0_.1, f32[16,4608]{1,0:T(8,128)} %refs_1_.1, f32[16,4608]{1,0:T(8,128)} %refs_2_.1), custom_call_target="tpu_custom_call" | custom-call | bytes 4718592 | tf_op jit(solution)/shard_map/split_mine/pallas_call | solution.py:66
  8.0 2.1 %collective-permute-done = bf16[2,4,2,2,2,2,8,1152]{7,6,5,4,3,2,1,0:T(8,128)(2,1)S(1)} collective-permute-done((bf16[2,4,2,2,2,2,8,1152]{7,6,5,4,3,2,1,0:T(8,128)(2,1)S(1)}, bf16[2,4,2,2,2,2,8,1152]{7,6,5,4,3,2,1,0:T(8,128)(2,1)S(1)}, u32[]{:S(2)}, u32[]{:S(2)}) %collective-permute-start) | collective-permute-done | bytes 2359328 | tf_op jit(solution)/shard_map/ppermute | solution.py:158
  10.2 0.8 add_convert_fusion
  10.9 37.6 %all_to_all.10 = f16[32,2,2,8,1152]{4,3,2,1,0:T(8,128)(2,1)S(1)} all-to-all(f16[32,2,2,8,1152]{4,3,2,1,0:T(8,128)(2,1)S(1)} %bitcast.59), channel_id=1, replica_groups=mesh['xh'=2,'y'=4,'xl'=2,'zh'=2,'zm'=2,'zl'=2,'c'=2] {'xh','y','xl','zl'}, dimensions={0} | all-to-all | bytes 4718592 | tf_op jit(solution)/shard_map/all_to_all | solution.py:135
  48.6 0.3 convert_reduce_fusion
  48.9 6.1 %collective-permute-start.1 = (f16[2,8,1152]{2,1,0:T(8,128)(2,1)S(1)}, f16[2,8,1152]{2,1,0:T(8,128)(2,1)S(1)}, u32[]{:S(2)}, u32[]{:S(2)}) collective-permute-start(f16[2,8,1152]{2,1,0:T(8,128)(2,1)S(1)} %fusion.1), channel_id=1, source_target_pairs={{0,8},{8,0},{1,9},{9,1},{2,10},{10,2},{3,11},{11,3},{4,12},{12,4},... | collective-permute-start | bytes 110600 | tf_op jit(solution)/shard_map/ppermute | solution.py:139
  55.0 1.4 %collective-permute-done.1 = f16[2,8,1152]{2,1,0:T(8,128)(2,1)S(1)} collective-permute-done((f16[2,8,1152]{2,1,0:T(8,128)(2,1)S(1)}, f16[2,8,1152]{2,1,0:T(8,128)(2,1)S(1)}, u32[]{:S(2)}, u32[]{:S(2)}) %collective-permute-start.1) | collective-permute-done | bytes 36896 | tf_op jit(solution)/shard_map/ppermute | solution.py:139
  56.4 2.7 %collective-permute-start.2 = (f16[8,1152]{1,0:T(8,128)(2,1)S(1)}, f16[8,1152]{1,0:T(8,128)(2,1)S(1)}, u32[]{:S(2)}, u32[]{:S(2)}) collective-permute-start(f16[8,1152]{1,0:T(8,128)(2,1)S(1)} %fusion.11), channel_id=1, source_target_pairs={{0,4},{4,0},{1,5},{5,1},{2,6},{6,2},{3,7},{7,3},{8,12},{12,8},{9,1... | collective-permute-start | bytes 55304 | tf_op jit(solution)/shard_map/ppermute | solution.py:139
  59.0 1.2 collective-permute-done.2
  60.2 2.4 %collective-permute-start.3 = (bf16[8,1152]{1,0:T(8,128)(2,1)S(1)}, bf16[8,1152]{1,0:T(8,128)(2,1)S(1)}, u32[]{:S(2)}, u32[]{:S(2)}) collective-permute-start(bf16[8,1152]{1,0:T(8,128)(2,1)S(1)} %get-tuple-element.27), channel_id=1, source_target_pairs={{0,4},{4,0},{1,5},{5,1},{2,6},{6,2},{3,7},{7,3},{8,12},{12,8},{9,1... | collective-permute-start | bytes 55304 | tf_op jit(solution)/shard_map/ppermute | solution.py:139
  62.7 1.2 collective-permute-start.4
  63.9 3.1 %collective-permute-done.4 = f32[1,8,1152]{2,1,0:T(8,128)S(1)} collective-permute-done((f32[1,8,1152]{2,1,0:T(8,128)S(1)}, f32[1,8,1152]{2,1,0:T(8,128)S(1)}, u32[]{:S(2)}, u32[]{:S(2)}) %collective-permute-start.4) | collective-permute-done | bytes 36896 | tf_op jit(solution)/shard_map/ppermute | solution.py:139
  67.0 4.0 %collective-permute-start.5 = (bf16[2,8,1152]{2,1,0:T(8,128)(2,1)S(1)}, bf16[2,8,1152]{2,1,0:T(8,128)(2,1)S(1)}, u32[]{:S(2)}, u32[]{:S(2)}) collective-permute-start(bf16[2,8,1152]{2,1,0:T(8,128)(2,1)S(1)} %pad_maximum_fusion.3), channel_id=1, source_target_pairs={{0,8},{8,0},{1,9},{9,1},{2,10},{10,2},{3,11},{11,3},{4,12},{12,4},... | collective-permute-start | bytes 110600 | tf_op jit(solution)/shard_map/ppermute | solution.py:139
  71.0 0.2 collective-permute-start.6
  71.2 2.5 %collective-permute-done.5 = bf16[2,8,1152]{2,1,0:T(8,128)(2,1)S(1)} collective-permute-done((bf16[2,8,1152]{2,1,0:T(8,128)(2,1)S(1)}, bf16[2,8,1152]{2,1,0:T(8,128)(2,1)S(1)}, u32[]{:S(2)}, u32[]{:S(2)}) %collective-permute-start.5) | collective-permute-done | bytes 36896 | tf_op jit(solution)/shard_map/ppermute | solution.py:139
  73.7 2.0 %collective-permute-done.6 = f32[2,8,1152]{2,1,0:T(8,128)S(1)} collective-permute-done((f32[2,8,1152]{2,1,0:T(8,128)S(1)}, f32[2,8,1152]{2,1,0:T(8,128)S(1)}, u32[]{:S(2)}, u32[]{:S(2)}) %collective-permute-start.6) | collective-permute-done | bytes 73760 | tf_op jit(solution)/shard_map/ppermute | solution.py:139
  75.9 29.6 %all_to_all.11 = bf16[32,2,2,8,1152]{4,3,2,1,0:T(8,128)(2,1)S(1)} all-to-all(bf16[32,2,2,8,1152]{4,3,2,1,0:T(8,128)(2,1)S(1)} %broadcast_in_dim.7), channel_id=1, replica_groups=mesh['xh'=2,'y'=4,'xl'=2,'zh'=2,'zm'=2,'zl'=2,'c'=2] {'xh','y','xl','zl'}, dimensions={0} | all-to-all | bytes 4718592 | tf_op jit(solution)/shard_map/all_to_all | solution.py:135
  105.5 7.0 %collective-permute-start.8 = (bf16[2,4,2,2,2,2,8,1152]{7,6,5,4,3,2,1,0:T(8,128)(2,1)S(1)}, bf16[2,4,2,2,2,2,8,1152]{7,6,5,4,3,2,1,0:T(8,128)(2,1)S(1)}, u32[]{:S(2)}, u32[]{:S(2)}) collective-permute-start(bf16[2,4,2,2,2,2,8,1152]{7,6,5,4,3,2,1,0:T(8,128)(2,1)S(1)} %bitcast.54), channel_id=1, source_target_pairs={{0,1},{1,0},{2,3},{3,2},{4,5},{5,4},{6,7},{7,6},{8,9},{9,8},{10,11... | collective-permute-start | bytes 7077896 | tf_op jit(solution)/shard_map/ppermute | solution.py:175
  112.5 1.7 %place_mine.1.refs_0_ = bf16[2,2,2,2,2,2,8,4608]{7,6,5,4,3,2,1,0:T(8,128)(2,1)} custom-call(bf16[2,4,2,2,2,2,8,1152]{7,6,5,4,3,2,1,0:T(8,128)(2,1)S(1)} %bitcast.55), custom_call_target="tpu_custom_call" | custom-call | bytes 4718592 | tf_op jit(solution)/shard_map/place_mine/pallas_call | solution.py:86
  114.2 3.7 %collective-permute-done.7.others = f32[4,8,1152]{2,1,0:T(8,128)S(1)} collective-permute-done((f32[4,8,1152]{2,1,0:T(8,128)S(1)}, f32[4,8,1152]{2,1,0:T(8,128)S(1)}, u32[]{:S(2)}, u32[]{:S(2)}) %collective-permute-start.7) | collective-permute-done | bytes 147488 | tf_op jit(solution)/shard_map/ppermute | solution.py:139
  117.8 1.2 new_states.1
  119.0 1.7 %place_theirs.1 = bf16[2,2,2,2,2,2,8,4608]{7,6,5,4,3,2,1,0:T(8,128)(2,1)} custom-call(bf16[2,2,2,2,2,2,8,4608]{7,6,5,4,3,2,1,0:T(8,128)(2,1)} %place_mine.1.refs_0_, bf16[2,4,2,2,2,2,8,1152]{7,6,5,4,3,2,1,0:T(8,128)(2,1)S(1)} %collective-permute-done.8.refs_1_), custom_call_target="tpu_custom_call", output_to_operand_aliasing={{}: (0, {})} | custom-call | bytes 4718592 | tf_op jit(solution)/shard_map/place_theirs/pallas_call | solution.py:86
  (18 shorter events, 0.4 us)
Async XLA Ops:
  2.7 7.5 %collective-permute-start = (bf16[2,4,2,2,2,2,8,1152]{7,6,5,4,3,2,1,0:T(8,128)(2,1)S(1)}, bf16[2,4,2,2,2,2,8,1152]{7,6,5,4,3,2,1,0:T(8,128)(2,1)S(1)}, u32[]{:S(2)}, u32[]{:S(2)}) collective-permute-start(bf16[2,4,2,2,2,2,8,1152]{7,6,5,4,3,2,1,0:T(8,128)(2,1)S(1)} %split_theirs.1), channel_id=1, source_target_pairs={{0,1},{1,0},{2,3},{3,2},{4,5},{5,4},{6,7},{7,6},{8,9},{9,8},{10,11... | collective-permute-start | bytes 7077896 | tf_op jit(solution)/shard_map/ppermute | solution.py:158
  48.9 7.5 %collective-permute-start.1 = (f16[2,8,1152]{2,1,0:T(8,128)(2,1)S(1)}, f16[2,8,1152]{2,1,0:T(8,128)(2,1)S(1)}, u32[]{:S(2)}, u32[]{:S(2)}) collective-permute-start(f16[2,8,1152]{2,1,0:T(8,128)(2,1)S(1)} %fusion.1), channel_id=1, source_target_pairs={{0,8},{8,0},{1,9},{9,1},{2,10},{10,2},{3,11},{11,3},{4,12},{12,4},... | collective-permute-start | bytes 110600 | tf_op jit(solution)/shard_map/ppermute | solution.py:139
  56.4 3.8 %collective-permute-start.2 = (f16[8,1152]{1,0:T(8,128)(2,1)S(1)}, f16[8,1152]{1,0:T(8,128)(2,1)S(1)}, u32[]{:S(2)}, u32[]{:S(2)}) collective-permute-start(f16[8,1152]{1,0:T(8,128)(2,1)S(1)} %fusion.11), channel_id=1, source_target_pairs={{0,4},{4,0},{1,5},{5,1},{2,6},{6,2},{3,7},{7,3},{8,12},{12,8},{9,1... | collective-permute-start | bytes 55304 | tf_op jit(solution)/shard_map/ppermute | solution.py:139
  60.2 3.6 %collective-permute-start.3 = (bf16[8,1152]{1,0:T(8,128)(2,1)S(1)}, bf16[8,1152]{1,0:T(8,128)(2,1)S(1)}, u32[]{:S(2)}, u32[]{:S(2)}) collective-permute-start(bf16[8,1152]{1,0:T(8,128)(2,1)S(1)} %get-tuple-element.27), channel_id=1, source_target_pairs={{0,4},{4,0},{1,5},{5,1},{2,6},{6,2},{3,7},{7,3},{8,12},{12,8},{9,1... | collective-permute-start | bytes 55304 | tf_op jit(solution)/shard_map/ppermute | solution.py:139
  62.7 4.3 %collective-permute-start.4 = (f32[1,8,1152]{2,1,0:T(8,128)S(1)}, f32[1,8,1152]{2,1,0:T(8,128)S(1)}, u32[]{:S(2)}, u32[]{:S(2)}) collective-permute-start(f32[1,8,1152]{2,1,0:T(8,128)S(1)} %get-tuple-element.26), channel_id=1, source_target_pairs={{0,128},{128,0},{1,129},{129,1},{2,130},{130,2},{3,131},{131,3},{4... | collective-permute-start | bytes 110600 | tf_op jit(solution)/shard_map/ppermute | solution.py:139
  67.0 6.7 %collective-permute-start.5 = (bf16[2,8,1152]{2,1,0:T(8,128)(2,1)S(1)}, bf16[2,8,1152]{2,1,0:T(8,128)(2,1)S(1)}, u32[]{:S(2)}, u32[]{:S(2)}) collective-permute-start(bf16[2,8,1152]{2,1,0:T(8,128)(2,1)S(1)} %pad_maximum_fusion.3), channel_id=1, source_target_pairs={{0,8},{8,0},{1,9},{9,1},{2,10},{10,2},{3,11},{11,3},{4,12},{12,4},... | collective-permute-start | bytes 110600 | tf_op jit(solution)/shard_map/ppermute | solution.py:139
  71.0 4.7 %collective-permute-start.6 = (f32[2,8,1152]{2,1,0:T(8,128)S(1)}, f32[2,8,1152]{2,1,0:T(8,128)S(1)}, u32[]{:S(2)}, u32[]{:S(2)}) collective-permute-start(f32[2,8,1152]{2,1,0:T(8,128)S(1)} %pad_maximum_fusion.1), channel_id=1, source_target_pairs={{0,64},{32,96},{64,0},{96,32},{1,65},{33,97},{65,1},{97,33},{2,66}... | collective-permute-start | bytes 221192 | tf_op jit(solution)/shard_map/ppermute | solution.py:139
  105.5 12.4 %copy-start = (f32[16,4608]{1,0:T(8,128)S(1)}, f32[16,4608]{1,0:T(8,128)}, u32[]{:S(2)}) copy-start(f32[16,4608]{1,0:T(8,128)} %refs_0_.1) | copy-start | bytes 884740
  105.5 12.4 %copy-start.1 = (f32[16,4608]{1,0:T(8,128)S(1)}, f32[16,4608]{1,0:T(8,128)}, u32[]{:S(2)}) copy-start(f32[16,4608]{1,0:T(8,128)} %refs_1_.1) | copy-start | bytes 884740
  105.5 12.4 %copy-start.2 = (f32[16,4608]{1,0:T(8,128)S(1)}, f32[16,4608]{1,0:T(8,128)}, u32[]{:S(2)}) copy-start(f32[16,4608]{1,0:T(8,128)} %refs_2_.1) | copy-start | bytes 884740
  105.5 13.6 %collective-permute-start.8 = (bf16[2,4,2,2,2,2,8,1152]{7,6,5,4,3,2,1,0:T(8,128)(2,1)S(1)}, bf16[2,4,2,2,2,2,8,1152]{7,6,5,4,3,2,1,0:T(8,128)(2,1)S(1)}, u32[]{:S(2)}, u32[]{:S(2)}) collective-permute-start(bf16[2,4,2,2,2,2,8,1152]{7,6,5,4,3,2,1,0:T(8,128)(2,1)S(1)} %bitcast.54), channel_id=1, source_target_pairs={{0,1},{1,0},{2,3},{3,2},{4,5},{5,4},{6,7},{7,6},{8,9},{9,8},{10,11... | collective-permute-start | bytes 7077896 | tf_op jit(solution)/shard_map/ppermute | solution.py:175
  112.4 5.4 %collective-permute-start.7 = (f32[4,8,1152]{2,1,0:T(8,128)S(1)}, f32[4,8,1152]{2,1,0:T(8,128)S(1)}, u32[]{:S(2)}, u32[]{:S(2)}) collective-permute-start(f32[4,8,1152]{2,1,0:T(8,128)S(1)} %pad_maximum_fusion.mine), channel_id=1, source_target_pairs={{0,32},{32,0},{64,96},{96,64},{1,33},{33,1},{65,97},{97,65},{2,34}... | collective-permute-start | bytes 442376 | tf_op jit(solution)/shard_map/ppermute | solution.py:139

commit v6 on v5

--- a/solution.py
+++ b/solution.py
@@ -106,41 +106,34 @@
     return master_new, moment1_new, moment2_new
 
 
-def new_states_kernel(mine, others, *refs):
-    old, new = refs[:3], refs[3:]
-    xh, y = lax.axis_index("xh"), lax.axis_index("y")
-    for k in range(XH * Y // 2):
-        for grad, low in ((mine[k], 0), (others[k], 1)):
-            rows = pl.ds(pl.multiple_of((xh ^ (k % 2)) * LOW, LOW), LOW)
-            at = (rows, pl.ds(pl.multiple_of((y ^ (k // 2 * 2 + low)) * COLS, 128), COLS))
-            for ref, value in zip(new, adam(grad, *[ref[at] for ref in old])):
-                ref[at] = value
+def new_states_kernel(grads, *refs):
+    old, new = refs[:STATES], refs[STATES:]
+    for i in range(XH * Y):
+        xh, y = divmod(i, Y)
+        at = (pl.ds(xh * LOW, LOW), pl.ds(y * COLS, COLS))
+        for ref, value in zip(new, adam(grads[i], *[ref[at] for ref in old])):
+            ref[at] = value
 
 
-def new_states(mine, others, master, moment1, moment2):
+def new_states(grads, *states):
+    size = states[0].size
     return pl.pallas_call(
         new_states_kernel,
-        out_shape=[jax.ShapeDtypeStruct(master.shape, master.dtype)] * 3,
-        in_specs=[VMEM] * 5,
-        out_specs=[VMEM] * 3,
+        out_shape=[jax.ShapeDtypeStruct(state.shape, state.dtype) for state in states],
+        in_specs=[VMEM] * (1 + STATES),
+        out_specs=[VMEM] * STATES,
         compiler_params=pltpu.CompilerParams(vmem_limit_bytes=8 * 2**20),
-        cost_estimate=pl.CostEstimate(
-            flops=20 * master.size, bytes_accessed=28 * master.size, transcendentals=master.size
-        ),
+        cost_estimate=pl.CostEstimate(flops=20 * size, bytes_accessed=28 * size, transcendentals=size),
         name="new_states",
-    )(mine, others, master, moment1, moment2)
+    )(grads, *states)
 
 
 def exchange(chunks):
-    return lax.all_to_all(chunks.reshape(-1, ZH, ZM, LOW, COLS), BIG, 0, 0, tiled=True)
+    return lax.all_to_all(chunks.reshape(-1, ZH * ZM, LOW, COLS), BIG, 0, 0, tiled=True)
 
 
-def partner(a, axis, bit=1):
-    return lax.ppermute(a, axis, [(i, i ^ bit) for i in range(lax.axis_size(axis))])
-
-
-def halve(a, axis):
-    return a[0] + partner(a[1].astype(jnp.float16), axis).astype(jnp.float32)
+def partner(a, m):
+    return lax.ppermute(a, ("zh", "zm"), [(i, i ^ m) for i in range(ZH * ZM)])
 
 
 def add(parts):
@@ -160,22 +153,18 @@
     pair = pair.astype(jnp.float32) + came.astype(jnp.float32)
     column = add(exchange(pair.astype(jnp.float16)))
 
-    grad = halve(halve(column, "zh"), "zm") / (big * ZH * ZM * CORES)
+    came = [partner(column[m].astype(jnp.float16), m) for m in range(1, ZH * ZM)]
+    grad = sum((a.astype(jnp.float32) for a in came), column[0]) / (big * ZH * ZM * CORES)
 
     part = adam(grad, *olds)[0].astype(jnp.bfloat16)
-    mine = grad[None]
-    part = jnp.stack([part, partner(part, "zm")])
-    mine = jnp.concatenate([mine, partner(mine, "xh")])
-    part, mine = lax.optimization_barrier((part, mine))
-    part = jnp.stack([part, partner(part, "zh")])
-    mine = jnp.concatenate([mine, partner(mine, "y", 2)])
-    part, mine = lax.optimization_barrier((part, mine))
+    grads = lax.all_to_all(jnp.broadcast_to(grad, (XH * Y, LOW, COLS)), ("xh", "y"), 0, 0, tiled=True)
+    part = jnp.stack([part] + [partner(part, m) for m in range(1, ZH * ZM)])
+    part, grads = lax.optimization_barrier((part, grads))
     part = exchange(jnp.broadcast_to(part, (big, *part.shape))).reshape(SHAPE)
-    part, mine = lax.optimization_barrier((part, mine))
+    part, grads = lax.optimization_barrier((part, grads))
     came = lax.ppermute(part, "c", SWAP)
-    others = partner(mine, "y", 1)
     params = place(True, came, (place(False, part),))
-    return *new_states(mine, others, *states), params.reshape(rows, width)
+    return *new_states(grads, *states), params.reshape(rows, width)
 
 
 def solution(mesh):

time: 121 us -> 119 us (0.983)
  waiting for transfers between devices: 15.9 us -> 10.7 us
  blocking collectives: 67.2 us -> 71.4 us
  starting transfers between devices: 26.9 us -> 25.5 us
    ppermute x7 -> x6, waiting for transfers between devices: 13.7 us -> 7.19 us  [partner(): return lax.ppermute(a, ('zh', 'zm'), [(i, i ^ m) for i in range(ZH * ZM)])]
    all_to_all x2, blocking collectives: 67.2 us -> 71.4 us  [exchange(): lax.all_to_all(chunks.reshape(-1, ZH * ZM, LOW, COLS), BIG, 0, 0, tiled=T...]
    ppermute x7 -> x6, starting transfers between devices: 16.7 us -> 13 us  [partner(): return lax.ppermute(a, ('zh', 'zm'), [(i, i ^ m) for i in range(ZH * ZM)])]
    all_to_all x0 -> x1, starting transfers between devices: none -> 3.42 us  [per_device(): lax.all_to_all(jnp.broadcast_to(grad, (XH * Y, LOW, COLS)), ('xh', 'y'),...]
    ppermute x1, waiting for transfers between devices: 0.01 us -> 1.41 us  [per_device(): came = lax.ppermute(part, 'c', SWAP)]
    ppermute x1, starting transfers between devices: 6.95 us -> 5.73 us  [per_device(): came = lax.ppermute(part, 'c', SWAP)]
  transfers between devices with their start and end apart: 9 -> 9, of which waited for: 7 -> 6; matrix products, arithmetic and copies ran while one was open for 0% -> 0% of each run, Pallas kernels for 4% -> 4%
where the time goes in v6:
time: 119 us
  blocking collectives  71.4 us (60%)
  starting transfers between devices  25.5 us (21%)
  waiting for transfers between devices  10.7 us (9%)
  Pallas kernels  8.44 us (7%)
    all_to_all x2, blocking collectives, exchange(): lax.all_to_all(chunks.reshape(-1, ZH * ZM, LOW, COLS), BIG, 0, 0, tiled=T...  71.4 us
    ppermute x6, starting transfers between devices, partner(): return lax.ppermute(a, ('zh', 'zm'), [(i, i ^ m) for i in range(ZH * ZM)])  13 us
    ppermute x6, waiting for transfers between devices, partner(): return lax.ppermute(a, ('zh', 'zm'), [(i, i ^ m) for i in range(ZH * ZM)])  7.19 us
    ppermute x1, starting transfers between devices, per_device(): came = lax.ppermute(part, 'c', SWAP)  5.73 us
    all_to_all x1, starting transfers between devices, per_device(): lax.all_to_all(jnp.broadcast_to(grad, (XH * Y, LOW, COLS)), ('xh', 'y'),...  3.42 us
    pallas_call x2, Pallas kernels, place(): pl.pallas_call(lambda *refs: place_kernel(of_other, *refs), out_shape=jax...  3.33 us
    ppermute x1, starting transfers between devices, per_device(): came = lax.ppermute(split_theirs(whole), 'c', SWAP)  3.33 us
  transfers between devices with their start and end apart: 9, of which 6 were waited for; matrix products, arithmetic and copies ran while one was open for 0% of the time, Pallas kernels for 4%

profile of v6, /device:TPU:1, one launch (start us, length us, event | category | flops | bytes accessed | tf_op | source)
XLA Modules:
  0.0 118.9 jit_solution(16383788326707125383)
XLA Ops:
  0.6 2.0 %split_theirs.1 = bf16[2,4,2,2,2,2,8,1152]{7,6,5,4,3,2,1,0:T(8,128)(2,1)S(1)} custom-call(bf16[2,2,2,2,2,2,8,4608]{7,6,5,4,3,2,1,0:T(8,128)(2,1)} %bitcast.56), custom_call_target="tpu_custom_call" | custom-call | bytes 4718592 | tf_op jit(solution)/shard_map/split_theirs/pallas_call | solution.py:53
  2.7 3.3 %collective-permute-start = (bf16[2,4,2,2,2,2,8,1152]{7,6,5,4,3,2,1,0:T(8,128)(2,1)S(1)}, bf16[2,4,2,2,2,2,8,1152]{7,6,5,4,3,2,1,0:T(8,128)(2,1)S(1)}, u32[]{:S(2)}, u32[]{:S(2)}) collective-permute-start(bf16[2,4,2,2,2,2,8,1152]{7,6,5,4,3,2,1,0:T(8,128)(2,1)S(1)} %split_theirs.1), channel_id=1, source_target_pairs={{0,1},{1,0},{2,3},{3,2},{4,5},{5,4},{6,7},{7,6},{8,9},{9,8},{10,11... | collective-permute-start | bytes 7077896 | tf_op jit(solution)/shard_map/ppermute | solution.py:151
  6.0 2.0 %split_mine.1 = (bf16[2,4,2,2,2,2,8,1152]{7,6,5,4,3,2,1,0:T(8,128)(2,1)S(1)}, f32[3,8,1152]{2,1,0:T(8,128)S(1)}) custom-call(bf16[2,2,2,2,2,2,8,4608]{7,6,5,4,3,2,1,0:T(8,128)(2,1)} %bitcast.57, f32[16,4608]{1,0:T(8,128)} %refs_0_.1, f32[16,4608]{1,0:T(8,128)} %refs_1_.1, f32[16,4608]{1,0:T(8,128)} %refs_2_.1), custom_call_target="tpu_custom_call" | custom-call | bytes 4718592 | tf_op jit(solution)/shard_map/split_mine/pallas_call | solution.py:66
  8.0 2.1 %collective-permute-done = bf16[2,4,2,2,2,2,8,1152]{7,6,5,4,3,2,1,0:T(8,128)(2,1)S(1)} collective-permute-done((bf16[2,4,2,2,2,2,8,1152]{7,6,5,4,3,2,1,0:T(8,128)(2,1)S(1)}, bf16[2,4,2,2,2,2,8,1152]{7,6,5,4,3,2,1,0:T(8,128)(2,1)S(1)}, u32[]{:S(2)}, u32[]{:S(2)}) %collective-permute-start) | collective-permute-done | bytes 2359328 | tf_op jit(solution)/shard_map/ppermute | solution.py:151
  10.2 0.8 add_convert_fusion
  10.9 37.6 %all_to_all.15 = f16[32,4,8,1152]{3,2,1,0:T(8,128)(2,1)S(1)} all-to-all(f16[32,4,8,1152]{3,2,1,0:T(8,128)(2,1)S(1)} %bitcast.59), channel_id=1, replica_groups=mesh['xh'=2,'y'=4,'xl'=2,'zh'=2,'zm'=2,'zl'=2,'c'=2] {'xh','y','xl','zl'}, dimensions={0} | all-to-all | bytes 4718592 | tf_op jit(solution)/shard_map/all_to_all | solution.py:132
  48.6 0.3 convert_reduce_fusion
  48.9 3.1 %collective-permute-start.1 = (f16[8,1152]{1,0:T(8,128)(2,1)S(1)}, f16[8,1152]{1,0:T(8,128)(2,1)S(1)}, u32[]{:S(2)}, u32[]{:S(2)}) collective-permute-start(f16[8,1152]{1,0:T(8,128)(2,1)S(1)} %get-tuple-element.24), channel_id=1, source_target_pairs={{0,4},{4,0},{8,12},{12,8},{1,5},{5,1},{9,13},{13,9},{2,6},{6,2},{1... | collective-permute-start | bytes 55304 | tf_op jit(solution)/shard_map/ppermute | solution.py:136
  52.0 4.2 %collective-permute-start.2 = (f16[8,1152]{1,0:T(8,128)(2,1)S(1)}, f16[8,1152]{1,0:T(8,128)(2,1)S(1)}, u32[]{:S(2)}, u32[]{:S(2)}) collective-permute-start(f16[8,1152]{1,0:T(8,128)(2,1)S(1)} %get-tuple-element.26), channel_id=1, source_target_pairs={{0,8},{4,12},{8,0},{12,4},{1,9},{5,13},{9,1},{13,5},{2,10},{6,14},... | collective-permute-start | bytes 55304 | tf_op jit(solution)/shard_map/ppermute | solution.py:136
  56.2 2.4 %collective-permute-done.2 = f16[8,1152]{1,0:T(8,128)(2,1)S(1)} collective-permute-done((f16[8,1152]{1,0:T(8,128)(2,1)S(1)}, f16[8,1152]{1,0:T(8,128)(2,1)S(1)}, u32[]{:S(2)}, u32[]{:S(2)}) %collective-permute-start.2) | collective-permute-done | bytes 18464 | tf_op jit(solution)/shard_map/ppermute | solution.py:136
  58.6 2.6 %collective-permute-done.3 = f16[8,1152]{1,0:T(8,128)(2,1)S(1)} collective-permute-done((f16[8,1152]{1,0:T(8,128)(2,1)S(1)}, f16[8,1152]{1,0:T(8,128)(2,1)S(1)}, u32[]{:S(2)}, u32[]{:S(2)}) %collective-permute-start.3) | collective-permute-done | bytes 18464 | tf_op jit(solution)/shard_map/ppermute | solution.py:136
  61.3 0.7 broadcast_in_dim.6
  62.0 3.4 %all-to-all-start.1 = ((f32[8,8,1152]{2,1,0:T(8,128)}), f32[8,8,1152]{2,1,0:T(8,128)S(1)}, u32[]{:S(2)}, u32[]{:S(2)}) async-start(f32[8,8,1152]{2,1,0:T(8,128)} %broadcast_in_dim.6), calls=%async_computation.1 | async-start | bytes 589824 | tf_op jit(solution)/shard_map/all_to_all | solution.py:160
  65.5 1.0 collective-permute-start.4
  66.4 1.8 %collective-permute-start.5 = (bf16[8,1152]{1,0:T(8,128)(2,1)S(1)}, bf16[8,1152]{1,0:T(8,128)(2,1)S(1)}, u32[]{:S(2)}, u32[]{:S(2)}) collective-permute-start(bf16[8,1152]{1,0:T(8,128)(2,1)S(1)} %get-tuple-element.23), channel_id=1, source_target_pairs={{0,8},{4,12},{8,0},{12,4},{1,9},{5,13},{9,1},{13,5},{2,10},{6,14},... | collective-permute-start | bytes 55304 | tf_op jit(solution)/shard_map/ppermute | solution.py:136
  68.2 3.0 %collective-permute-start.6 = (bf16[8,1152]{1,0:T(8,128)(2,1)S(1)}, bf16[8,1152]{1,0:T(8,128)(2,1)S(1)}, u32[]{:S(2)}, u32[]{:S(2)}) collective-permute-start(bf16[8,1152]{1,0:T(8,128)(2,1)S(1)} %get-tuple-element.23), channel_id=1, source_target_pairs={{0,12},{4,8},{8,4},{12,0},{1,13},{5,9},{9,5},{13,1},{2,14},{6,10},... | collective-permute-start | bytes 55304 | tf_op jit(solution)/shard_map/ppermute | solution.py:136
  71.2 1.9 %collective-permute-done.5 = bf16[8,1152]{1,0:T(8,128)(2,1)S(1)} collective-permute-done((bf16[8,1152]{1,0:T(8,128)(2,1)S(1)}, bf16[8,1152]{1,0:T(8,128)(2,1)S(1)}, u32[]{:S(2)}, u32[]{:S(2)}) %collective-permute-start.5) | collective-permute-done | bytes 18464 | tf_op jit(solution)/shard_map/ppermute | solution.py:136
  73.1 0.2 collective-permute-done.6
  73.6 33.8 %all_to_all.16 = bf16[32,4,8,1152]{3,2,1,0:T(8,128)(2,1)S(1)} all-to-all(bf16[32,4,8,1152]{3,2,1,0:T(8,128)(2,1)S(1)} %broadcast_in_dim.7), channel_id=1, replica_groups=mesh['xh'=2,'y'=4,'xl'=2,'zh'=2,'zm'=2,'zl'=2,'c'=2] {'xh','y','xl','zl'}, dimensions={0} | all-to-all | bytes 4718592 | tf_op jit(solution)/shard_map/all_to_all | solution.py:132
  107.4 5.7 %collective-permute-start.7 = (bf16[2,4,2,2,2,2,8,1152]{7,6,5,4,3,2,1,0:T(8,128)(2,1)S(1)}, bf16[2,4,2,2,2,2,8,1152]{7,6,5,4,3,2,1,0:T(8,128)(2,1)S(1)}, u32[]{:S(2)}, u32[]{:S(2)}) collective-permute-start(bf16[2,4,2,2,2,2,8,1152]{7,6,5,4,3,2,1,0:T(8,128)(2,1)S(1)} %bitcast.54), channel_id=1, source_target_pairs={{0,1},{1,0},{2,3},{3,2},{4,5},{5,4},{6,7},{7,6},{8,9},{9,8},{10,11... | collective-permute-start | bytes 7077896 | tf_op jit(solution)/shard_map/ppermute | solution.py:165
  113.1 1.7 %place_mine.1.refs_0_ = bf16[2,2,2,2,2,2,8,4608]{7,6,5,4,3,2,1,0:T(8,128)(2,1)} custom-call(bf16[2,4,2,2,2,2,8,1152]{7,6,5,4,3,2,1,0:T(8,128)(2,1)S(1)} %bitcast.55), custom_call_target="tpu_custom_call" | custom-call | bytes 4718592 | tf_op jit(solution)/shard_map/place_mine/pallas_call | solution.py:86
  114.8 1.0 new_states.1
  115.8 1.4 %collective-permute-done.7.refs_1_ = bf16[2,4,2,2,2,2,8,1152]{7,6,5,4,3,2,1,0:T(8,128)(2,1)S(1)} collective-permute-done((bf16[2,4,2,2,2,2,8,1152]{7,6,5,4,3,2,1,0:T(8,128)(2,1)S(1)}, bf16[2,4,2,2,2,2,8,1152]{7,6,5,4,3,2,1,0:T(8,128)(2,1)S(1)}, u32[]{:S(2)}, u32[]{:S(2)}) %collective-permute-start.7) | collective-permute-done | bytes 2359328 | tf_op jit(solution)/shard_map/ppermute | solution.py:165
  117.2 1.7 %place_theirs.1 = bf16[2,2,2,2,2,2,8,4608]{7,6,5,4,3,2,1,0:T(8,128)(2,1)} custom-call(bf16[2,2,2,2,2,2,8,4608]{7,6,5,4,3,2,1,0:T(8,128)(2,1)} %place_mine.1.refs_0_, bf16[2,4,2,2,2,2,8,1152]{7,6,5,4,3,2,1,0:T(8,128)(2,1)S(1)} %collective-permute-done.7.refs_1_), custom_call_target="tpu_custom_call", output_to_operand_aliasing={{}: (0, {})} | custom-call | bytes 4718592 | tf_op jit(solution)/shard_map/place_theirs/pallas_call | solution.py:86
  (15 shorter events, 0.3 us)
Async XLA Ops:
  2.7 7.5 %collective-permute-start = (bf16[2,4,2,2,2,2,8,1152]{7,6,5,4,3,2,1,0:T(8,128)(2,1)S(1)}, bf16[2,4,2,2,2,2,8,1152]{7,6,5,4,3,2,1,0:T(8,128)(2,1)S(1)}, u32[]{:S(2)}, u32[]{:S(2)}) collective-permute-start(bf16[2,4,2,2,2,2,8,1152]{7,6,5,4,3,2,1,0:T(8,128)(2,1)S(1)} %split_theirs.1), channel_id=1, source_target_pairs={{0,1},{1,0},{2,3},{3,2},{4,5},{5,4},{6,7},{7,6},{8,9},{9,8},{10,11... | collective-permute-start | bytes 7077896 | tf_op jit(solution)/shard_map/ppermute | solution.py:151
  48.9 7.3 %collective-permute-start.1 = (f16[8,1152]{1,0:T(8,128)(2,1)S(1)}, f16[8,1152]{1,0:T(8,128)(2,1)S(1)}, u32[]{:S(2)}, u32[]{:S(2)}) collective-permute-start(f16[8,1152]{1,0:T(8,128)(2,1)S(1)} %get-tuple-element.24), channel_id=1, source_target_pairs={{0,4},{4,0},{8,12},{12,8},{1,5},{5,1},{9,13},{13,9},{2,6},{6,2},{1... | collective-permute-start | bytes 55304 | tf_op jit(solution)/shard_map/ppermute | solution.py:136
  52.0 6.6 %collective-permute-start.2 = (f16[8,1152]{1,0:T(8,128)(2,1)S(1)}, f16[8,1152]{1,0:T(8,128)(2,1)S(1)}, u32[]{:S(2)}, u32[]{:S(2)}) collective-permute-start(f16[8,1152]{1,0:T(8,128)(2,1)S(1)} %get-tuple-element.26), channel_id=1, source_target_pairs={{0,8},{4,12},{8,0},{12,4},{1,9},{5,13},{9,1},{13,5},{2,10},{6,14},... | collective-permute-start | bytes 55304 | tf_op jit(solution)/shard_map/ppermute | solution.py:136
  56.2 5.0 %collective-permute-start.3 = (f16[8,1152]{1,0:T(8,128)(2,1)S(1)}, f16[8,1152]{1,0:T(8,128)(2,1)S(1)}, u32[]{:S(2)}, u32[]{:S(2)}) collective-permute-start(f16[8,1152]{1,0:T(8,128)(2,1)S(1)} %get-tuple-element.25), channel_id=1, source_target_pairs={{0,12},{4,8},{8,4},{12,0},{1,13},{5,9},{9,5},{13,1},{2,14},{6,10},... | collective-permute-start | bytes 55304 | tf_op jit(solution)/shard_map/ppermute | solution.py:136
  62.0 11.4 %all-to-all-start.1 = ((f32[8,8,1152]{2,1,0:T(8,128)}), f32[8,8,1152]{2,1,0:T(8,128)S(1)}, u32[]{:S(2)}, u32[]{:S(2)}) async-start(f32[8,8,1152]{2,1,0:T(8,128)} %broadcast_in_dim.6), calls=%async_computation.1 | async-start | bytes 589824 | tf_op jit(solution)/shard_map/all_to_all | solution.py:160
  65.5 5.7 %collective-permute-start.4 = (bf16[8,1152]{1,0:T(8,128)(2,1)S(1)}, bf16[8,1152]{1,0:T(8,128)(2,1)S(1)}, u32[]{:S(2)}, u32[]{:S(2)}) collective-permute-start(bf16[8,1152]{1,0:T(8,128)(2,1)S(1)} %get-tuple-element.23), channel_id=1, source_target_pairs={{0,4},{4,0},{8,12},{12,8},{1,5},{5,1},{9,13},{13,9},{2,6},{6,2},{1... | collective-permute-start | bytes 55304 | tf_op jit(solution)/shard_map/ppermute | solution.py:136
  66.4 6.7 %collective-permute-start.5 = (bf16[8,1152]{1,0:T(8,128)(2,1)S(1)}, bf16[8,1152]{1,0:T(8,128)(2,1)S(1)}, u32[]{:S(2)}, u32[]{:S(2)}) collective-permute-start(bf16[8,1152]{1,0:T(8,128)(2,1)S(1)} %get-tuple-element.23), channel_id=1, source_target_pairs={{0,8},{4,12},{8,0},{12,4},{1,9},{5,13},{9,1},{13,5},{2,10},{6,14},... | collective-permute-start | bytes 55304 | tf_op jit(solution)/shard_map/ppermute | solution.py:136
  68.2 5.2 %collective-permute-start.6 = (bf16[8,1152]{1,0:T(8,128)(2,1)S(1)}, bf16[8,1152]{1,0:T(8,128)(2,1)S(1)}, u32[]{:S(2)}, u32[]{:S(2)}) collective-permute-start(bf16[8,1152]{1,0:T(8,128)(2,1)S(1)} %get-tuple-element.23), channel_id=1, source_target_pairs={{0,12},{4,8},{8,4},{12,0},{1,13},{5,9},{9,5},{13,1},{2,14},{6,10},... | collective-permute-start | bytes 55304 | tf_op jit(solution)/shard_map/ppermute | solution.py:136
  107.3 7.4 %copy-start = (f32[16,4608]{1,0:T(8,128)S(1)}, f32[16,4608]{1,0:T(8,128)}, u32[]{:S(2)}) copy-start(f32[16,4608]{1,0:T(8,128)} %refs_0_.1) | copy-start | bytes 884740
  107.4 7.4 %copy-start.1 = (f32[16,4608]{1,0:T(8,128)S(1)}, f32[16,4608]{1,0:T(8,128)}, u32[]{:S(2)}) copy-start(f32[16,4608]{1,0:T(8,128)} %refs_1_.1) | copy-start | bytes 884740
  107.4 7.4 %copy-start.2 = (f32[16,4608]{1,0:T(8,128)S(1)}, f32[16,4608]{1,0:T(8,128)}, u32[]{:S(2)}) copy-start(f32[16,4608]{1,0:T(8,128)} %refs_2_.1) | copy-start | bytes 884740
  107.4 9.9 %collective-permute-start.7 = (bf16[2,4,2,2,2,2,8,1152]{7,6,5,4,3,2,1,0:T(8,128)(2,1)S(1)}, bf16[2,4,2,2,2,2,8,1152]{7,6,5,4,3,2,1,0:T(8,128)(2,1)S(1)}, u32[]{:S(2)}, u32[]{:S(2)}) collective-permute-start(bf16[2,4,2,2,2,2,8,1152]{7,6,5,4,3,2,1,0:T(8,128)(2,1)S(1)} %bitcast.54), channel_id=1, source_target_pairs={{0,1},{1,0},{2,3},{3,2},{4,5},{5,4},{6,7},{7,6},{8,9},{9,8},{10,11... | collective-permute-start | bytes 7077896 | tf_op jit(solution)/shard_map/ppermute | solution.py:165

commit v7 on v6

--- a/solution.py
+++ b/solution.py
@@ -106,26 +106,28 @@
     return master_new, moment1_new, moment2_new
 
 
-def new_states_kernel(grads, *refs):
+def new_states_kernel(early, late, *refs):
     old, new = refs[:STATES], refs[STATES:]
-    for i in range(XH * Y):
-        xh, y = divmod(i, Y)
-        at = (pl.ds(xh * LOW, LOW), pl.ds(y * COLS, COLS))
-        for ref, value in zip(new, adam(grads[i], *[ref[at] for ref in old])):
+    xh, y, core = (lax.axis_index(a) for a in ("xh", "y", "c"))
+    for k in range(XH * Y):
+        grad = jnp.where(core == 0, early[k], late[k])
+        rows = pl.ds(pl.multiple_of((xh ^ (k // Y)) * LOW, LOW), LOW)
+        at = (rows, pl.ds(pl.multiple_of((y ^ (k % Y)) * COLS, 128), COLS))
+        for ref, value in zip(new, adam(grad, *[ref[at] for ref in old])):
             ref[at] = value
 
 
-def new_states(grads, *states):
+def new_states(early, late, *states):
     size = states[0].size
     return pl.pallas_call(
         new_states_kernel,
         out_shape=[jax.ShapeDtypeStruct(state.shape, state.dtype) for state in states],
-        in_specs=[VMEM] * (1 + STATES),
+        in_specs=[VMEM] * (2 + STATES),
         out_specs=[VMEM] * STATES,
         compiler_params=pltpu.CompilerParams(vmem_limit_bytes=8 * 2**20),
         cost_estimate=pl.CostEstimate(flops=20 * size, bytes_accessed=28 * size, transcendentals=size),
         name="new_states",
-    )(grads, *states)
+    )(early, late, *states)
 
 
 def exchange(chunks):
@@ -134,6 +136,17 @@
 
 def partner(a, m):
     return lax.ppermute(a, ("zh", "zm"), [(i, i ^ m) for i in range(ZH * ZM)])
+
+
+def across(a, core, m):
+    pairs = [(i * CORES + core, (i ^ m) * CORES + core) for i in range(XH * Y)]
+    return lax.ppermute(a, ("xh", "y", "c"), pairs)
+
+
+def pieces(grad, core):
+    for m in (1, 2, 4):
+        grad = jnp.concatenate([grad, across(grad, core, m)])
+    return grad
 
 
 def add(parts):
@@ -157,14 +170,16 @@
     grad = sum((a.astype(jnp.float32) for a in came), column[0]) / (big * ZH * ZM * CORES)
 
     part = adam(grad, *olds)[0].astype(jnp.bfloat16)
-    grads = lax.all_to_all(jnp.broadcast_to(grad, (XH * Y, LOW, COLS)), ("xh", "y"), 0, 0, tiled=True)
+    early = pieces(grad[None], 0)
     part = jnp.stack([part] + [partner(part, m) for m in range(1, ZH * ZM)])
-    part, grads = lax.optimization_barrier((part, grads))
+    part, early, grad = lax.optimization_barrier((part, early, grad))
     part = exchange(jnp.broadcast_to(part, (big, *part.shape))).reshape(SHAPE)
-    part, grads = lax.optimization_barrier((part, grads))
+    part, early, grad = lax.optimization_barrier((part, early, grad))
+    late = pieces(grad[None], 1)
+    part, early, late = lax.optimization_barrier((part, early, late))
     came = lax.ppermute(part, "c", SWAP)
     params = place(True, came, (place(False, part),))
-    return *new_states(grads, *states), params.reshape(rows, width)
+    return *new_states(early, late, *states), params.reshape(rows, width)
 
 
 def solution(mesh):

time: 119 us -> 129 us (1.084); the launches traced: 119 us -> 127 us
  waiting for transfers between devices: 10.7 us -> 22.3 us
  blocking collectives: 71.4 us -> 61.5 us
  starting transfers between devices: 25.5 us -> 32.8 us
    ppermute x0 -> x6, starting transfers between devices: none -> 15.4 us  [across(): return lax.ppermute(a, ('xh', 'y', 'c'), pairs)]
    ppermute x0 -> x6, waiting for transfers between devices: none -> 12.7 us  [across(): return lax.ppermute(a, ('xh', 'y', 'c'), pairs)]
    all_to_all x2, blocking collectives: 71.4 us -> 61.5 us  [exchange(): lax.all_to_all(chunks.reshape(-1, ZH * ZM, LOW, COLS), BIG, 0, 0, tiled=T...]
    ppermute x1, starting transfers between devices: 5.73 us -> 1.04 us  [per_device(): came = lax.ppermute(part, 'c', SWAP)]
    all_to_all x1 -> x0, starting transfers between devices: 3.42 us -> none  [per_device(): lax.all_to_all(jnp.broadcast_to(grad, (XH * Y, LOW, COLS)), ('xh', 'y'),...]
  transfers between devices with their start and end apart: 9 -> 14, of which waited for: 6 -> 9; matrix products, arithmetic and copies ran while one was open for 0% -> 0% of each run, Pallas kernels for 4% -> 4%
where the time goes in v7:
time: 129 us; the launch traced here: 127 us
  blocking collectives  61.5 us (48%)
  starting transfers between devices  32.8 us (25%)
  waiting for transfers between devices  22.3 us (17%)
  Pallas kernels  8.59 us (7%)
    all_to_all x2, blocking collectives, exchange(): lax.all_to_all(chunks.reshape(-1, ZH * ZM, LOW, COLS), BIG, 0, 0, tiled=T...  61.5 us
    ppermute x6, starting transfers between devices, across(): return lax.ppermute(a, ('xh', 'y', 'c'), pairs)  15.4 us
    ppermute x6, starting transfers between devices, partner(): return lax.ppermute(a, ('zh', 'zm'), [(i, i ^ m) for i in range(ZH * ZM)])  13 us
    ppermute x6, waiting for transfers between devices, across(): return lax.ppermute(a, ('xh', 'y', 'c'), pairs)  12.7 us
    ppermute x6, waiting for transfers between devices, partner(): return lax.ppermute(a, ('zh', 'zm'), [(i, i ^ m) for i in range(ZH * ZM)])  6.25 us
    pallas_call x2, Pallas kernels, place(): pl.pallas_call(lambda *refs: place_kernel(of_other, *refs), out_shape=jax...  3.33 us
    ppermute x1, starting transfers between devices, per_device(): came = lax.ppermute(split_theirs(whole), 'c', SWAP)  3.33 us
  transfers between devices with their start and end apart: 14, of which 9 were waited for; matrix products, arithmetic and copies ran while one was open for 0% of the time, Pallas kernels for 4%

profile of v7, /device:TPU:1, one launch (start us, length us, event | category | flops | bytes accessed | tf_op | source)
XLA Modules:
  0.0 127.4 jit_solution(15877424116388750141)
XLA Ops:
  0.6 2.0 %split_theirs.1 = bf16[2,4,2,2,2,2,8,1152]{7,6,5,4,3,2,1,0:T(8,128)(2,1)S(1)} custom-call(bf16[2,2,2,2,2,2,8,4608]{7,6,5,4,3,2,1,0:T(8,128)(2,1)} %bitcast.56), custom_call_target="tpu_custom_call" | custom-call | bytes 4718592 | tf_op jit(solution)/shard_map/split_theirs/pallas_call | solution.py:53
  2.7 3.3 %collective-permute-start = (bf16[2,4,2,2,2,2,8,1152]{7,6,5,4,3,2,1,0:T(8,128)(2,1)S(1)}, bf16[2,4,2,2,2,2,8,1152]{7,6,5,4,3,2,1,0:T(8,128)(2,1)S(1)}, u32[]{:S(2)}, u32[]{:S(2)}) collective-permute-start(bf16[2,4,2,2,2,2,8,1152]{7,6,5,4,3,2,1,0:T(8,128)(2,1)S(1)} %split_theirs.1), channel_id=1, source_target_pairs={{0,1},{1,0},{2,3},{3,2},{4,5},{5,4},{6,7},{7,6},{8,9},{9,8},{10,11... | collective-permute-start | bytes 7077896 | tf_op jit(solution)/shard_map/ppermute | solution.py:164
  6.0 2.0 %split_mine.1 = (bf16[2,4,2,2,2,2,8,1152]{7,6,5,4,3,2,1,0:T(8,128)(2,1)S(1)}, f32[3,8,1152]{2,1,0:T(8,128)S(1)}) custom-call(bf16[2,2,2,2,2,2,8,4608]{7,6,5,4,3,2,1,0:T(8,128)(2,1)} %bitcast.57, f32[16,4608]{1,0:T(8,128)} %refs_0_.1, f32[16,4608]{1,0:T(8,128)} %refs_1_.1, f32[16,4608]{1,0:T(8,128)} %refs_2_.1), custom_call_target="tpu_custom_call" | custom-call | bytes 4718592 | tf_op jit(solution)/shard_map/split_mine/pallas_call | solution.py:66
  8.0 2.1 %collective-permute-done = bf16[2,4,2,2,2,2,8,1152]{7,6,5,4,3,2,1,0:T(8,128)(2,1)S(1)} collective-permute-done((bf16[2,4,2,2,2,2,8,1152]{7,6,5,4,3,2,1,0:T(8,128)(2,1)S(1)}, bf16[2,4,2,2,2,2,8,1152]{7,6,5,4,3,2,1,0:T(8,128)(2,1)S(1)}, u32[]{:S(2)}, u32[]{:S(2)}) %collective-permute-start) | collective-permute-done | bytes 2359328 | tf_op jit(solution)/shard_map/ppermute | solution.py:164
  10.9 37.6 %all_to_all.10 = f16[32,4,8,1152]{3,2,1,0:T(8,128)(2,1)S(1)} all-to-all(f16[32,4,8,1152]{3,2,1,0:T(8,128)(2,1)S(1)} %bitcast.59), channel_id=1, replica_groups=mesh['xh'=2,'y'=4,'xl'=2,'zh'=2,'zm'=2,'zl'=2,'c'=2] {'xh','y','xl','zl'}, dimensions={0} | all-to-all | bytes 4718592 | tf_op jit(solution)/shard_map/all_to_all | solution.py:134
  48.9 3.1 %collective-permute-start.1 = (f16[8,1152]{1,0:T(8,128)(2,1)S(1)}, f16[8,1152]{1,0:T(8,128)(2,1)S(1)}, u32[]{:S(2)}, u32[]{:S(2)}) collective-permute-start(f16[8,1152]{1,0:T(8,128)(2,1)S(1)} %get-tuple-element.34), channel_id=1, source_target_pairs={{0,4},{4,0},{8,12},{12,8},{1,5},{5,1},{9,13},{13,9},{2,6},{6,2},{1... | collective-permute-start | bytes 55304 | tf_op jit(solution)/shard_map/ppermute | solution.py:138
  52.0 4.2 %collective-permute-start.2 = (f16[8,1152]{1,0:T(8,128)(2,1)S(1)}, f16[8,1152]{1,0:T(8,128)(2,1)S(1)}, u32[]{:S(2)}, u32[]{:S(2)}) collective-permute-start(f16[8,1152]{1,0:T(8,128)(2,1)S(1)} %get-tuple-element.36), channel_id=1, source_target_pairs={{0,8},{4,12},{8,0},{12,4},{1,9},{5,13},{9,1},{13,5},{2,10},{6,14},... | collective-permute-start | bytes 55304 | tf_op jit(solution)/shard_map/ppermute | solution.py:138
  56.2 2.4 %collective-permute-done.2 = f16[8,1152]{1,0:T(8,128)(2,1)S(1)} collective-permute-done((f16[8,1152]{1,0:T(8,128)(2,1)S(1)}, f16[8,1152]{1,0:T(8,128)(2,1)S(1)}, u32[]{:S(2)}, u32[]{:S(2)}) %collective-permute-start.2) | collective-permute-done | bytes 18464 | tf_op jit(solution)/shard_map/ppermute | solution.py:138
  58.6 2.6 %collective-permute-done.3 = f16[8,1152]{1,0:T(8,128)(2,1)S(1)} collective-permute-done((f16[8,1152]{1,0:T(8,128)(2,1)S(1)}, f16[8,1152]{1,0:T(8,128)(2,1)S(1)}, u32[]{:S(2)}, u32[]{:S(2)}) %collective-permute-start.3) | collective-permute-done | bytes 18464 | tf_op jit(solution)/shard_map/ppermute | solution.py:138
  63.7 1.8 %collective-permute-start.5 = (bf16[8,1152]{1,0:T(8,128)(2,1)S(1)}, bf16[8,1152]{1,0:T(8,128)(2,1)S(1)}, u32[]{:S(2)}, u32[]{:S(2)}) collective-permute-start(bf16[8,1152]{1,0:T(8,128)(2,1)S(1)} %get-tuple-element.38), channel_id=1, source_target_pairs={{0,8},{4,12},{8,0},{12,4},{1,9},{5,13},{9,1},{13,5},{2,10},{6,14},... | collective-permute-start | bytes 55304 | tf_op jit(solution)/shard_map/ppermute | solution.py:138
  65.4 3.0 %collective-permute-start.6 = (bf16[8,1152]{1,0:T(8,128)(2,1)S(1)}, bf16[8,1152]{1,0:T(8,128)(2,1)S(1)}, u32[]{:S(2)}, u32[]{:S(2)}) collective-permute-start(bf16[8,1152]{1,0:T(8,128)(2,1)S(1)} %get-tuple-element.38), channel_id=1, source_target_pairs={{0,12},{4,8},{8,4},{12,0},{1,13},{5,9},{9,5},{13,1},{2,14},{6,10},... | collective-permute-start | bytes 55304 | tf_op jit(solution)/shard_map/ppermute | solution.py:138
  69.1 1.2 collective-permute-done.5
  70.6 23.8 %all_to_all.11 = bf16[32,4,8,1152]{3,2,1,0:T(8,128)(2,1)S(1)} all-to-all(bf16[32,4,8,1152]{3,2,1,0:T(8,128)(2,1)S(1)} %broadcast_in_dim.10), channel_id=1, replica_groups=mesh['xh'=2,'y'=4,'xl'=2,'zh'=2,'zm'=2,'zl'=2,'c'=2] {'xh','y','xl','zl'}, dimensions={0} | all-to-all | bytes 4718592 | tf_op jit(solution)/shard_map/all_to_all | solution.py:134
  94.4 2.1 %collective-permute-start.10 = (f32[1,8,1152]{2,1,0:T(8,128)S(1)}, f32[1,8,1152]{2,1,0:T(8,128)S(1)}, u32[]{:S(2)}, u32[]{:S(2)}) collective-permute-start(f32[1,8,1152]{2,1,0:T(8,128)S(1)} %bitcast.60), channel_id=1, source_target_pairs={{1,33},{33,1},{65,97},{97,65},{129,161},{161,129},{193,225},{225,1... | collective-permute-start | bytes 110600 | tf_op jit(solution)/shard_map/ppermute | solution.py:143
  96.5 2.6 %collective-permute-done.10 = f32[1,8,1152]{2,1,0:T(8,128)S(1)} collective-permute-done((f32[1,8,1152]{2,1,0:T(8,128)S(1)}, f32[1,8,1152]{2,1,0:T(8,128)S(1)}, u32[]{:S(2)}, u32[]{:S(2)}) %collective-permute-start.10) | collective-permute-done | bytes 36896 | tf_op jit(solution)/shard_map/ppermute | solution.py:143
  99.1 2.5 %collective-permute-start.11 = (f32[2,8,1152]{2,1,0:T(8,128)S(1)}, f32[2,8,1152]{2,1,0:T(8,128)S(1)}, u32[]{:S(2)}, u32[]{:S(2)}) collective-permute-start(f32[2,8,1152]{2,1,0:T(8,128)S(1)} %pad_maximum_fusion.6), channel_id=1, source_target_pairs={{1,65},{33,97},{65,1},{97,33},{129,193},{161,225},{193,129},{225,1... | collective-permute-start | bytes 221192 | tf_op jit(solution)/shard_map/ppermute | solution.py:143
  101.6 7.6 %collective-permute-done.11 = f32[2,8,1152]{2,1,0:T(8,128)S(1)} collective-permute-done((f32[2,8,1152]{2,1,0:T(8,128)S(1)}, f32[2,8,1152]{2,1,0:T(8,128)S(1)}, u32[]{:S(2)}, u32[]{:S(2)}) %collective-permute-start.11) | collective-permute-done | bytes 73760 | tf_op jit(solution)/shard_map/ppermute | solution.py:143
  109.2 8.8 %collective-permute-start.12 = (f32[4,8,1152]{2,1,0:T(8,128)S(1)}, f32[4,8,1152]{2,1,0:T(8,128)S(1)}, u32[]{:S(2)}, u32[]{:S(2)}) collective-permute-start(f32[4,8,1152]{2,1,0:T(8,128)S(1)} %pad_maximum_fusion.3), channel_id=1, source_target_pairs={{1,129},{33,161},{65,193},{97,225},{129,1},{161,33},{193,65},{225,... | collective-permute-start | bytes 442376 | tf_op jit(solution)/shard_map/ppermute | solution.py:143
  118.0 2.5 %collective-permute-done.12 = f32[4,8,1152]{2,1,0:T(8,128)S(1)} collective-permute-done((f32[4,8,1152]{2,1,0:T(8,128)S(1)}, f32[4,8,1152]{2,1,0:T(8,128)S(1)}, u32[]{:S(2)}, u32[]{:S(2)}) %collective-permute-start.12) | collective-permute-done | bytes 147488 | tf_op jit(solution)/shard_map/ppermute | solution.py:143
  120.5 1.0 collective-permute-start.13
  121.6 1.7 %place_mine.1.refs_0_ = bf16[2,2,2,2,2,2,8,4608]{7,6,5,4,3,2,1,0:T(8,128)(2,1)} custom-call(bf16[2,4,2,2,2,2,8,1152]{7,6,5,4,3,2,1,0:T(8,128)(2,1)S(1)} %bitcast.55), custom_call_target="tpu_custom_call" | custom-call | bytes 4718592 | tf_op jit(solution)/shard_map/place_mine/pallas_call | solution.py:86
  123.3 1.2 new_states.1
  124.5 1.3 collective-permute-done.13.refs_1_
  125.7 1.7 %place_theirs.1 = bf16[2,2,2,2,2,2,8,4608]{7,6,5,4,3,2,1,0:T(8,128)(2,1)} custom-call(bf16[2,2,2,2,2,2,8,4608]{7,6,5,4,3,2,1,0:T(8,128)(2,1)} %place_mine.1.refs_0_, bf16[2,4,2,2,2,2,8,1152]{7,6,5,4,3,2,1,0:T(8,128)(2,1)S(1)} %collective-permute-done.13.refs_1_), custom_call_target="tpu_custom_call", output_to_operand_aliasing={{}: (0, {})} | custom-call | bytes 4718592 | tf_op jit(solution)/shard_map/place_theirs/pallas_call | solution.py:86
  (31 shorter events, 4.5 us)
Async XLA Ops:
  2.7 7.5 %collective-permute-start = (bf16[2,4,2,2,2,2,8,1152]{7,6,5,4,3,2,1,0:T(8,128)(2,1)S(1)}, bf16[2,4,2,2,2,2,8,1152]{7,6,5,4,3,2,1,0:T(8,128)(2,1)S(1)}, u32[]{:S(2)}, u32[]{:S(2)}) collective-permute-start(bf16[2,4,2,2,2,2,8,1152]{7,6,5,4,3,2,1,0:T(8,128)(2,1)S(1)} %split_theirs.1), channel_id=1, source_target_pairs={{0,1},{1,0},{2,3},{3,2},{4,5},{5,4},{6,7},{7,6},{8,9},{9,8},{10,11... | collective-permute-start | bytes 7077896 | tf_op jit(solution)/shard_map/ppermute | solution.py:164
  48.9 7.3 %collective-permute-start.1 = (f16[8,1152]{1,0:T(8,128)(2,1)S(1)}, f16[8,1152]{1,0:T(8,128)(2,1)S(1)}, u32[]{:S(2)}, u32[]{:S(2)}) collective-permute-start(f16[8,1152]{1,0:T(8,128)(2,1)S(1)} %get-tuple-element.34), channel_id=1, source_target_pairs={{0,4},{4,0},{8,12},{12,8},{1,5},{5,1},{9,13},{13,9},{2,6},{6,2},{1... | collective-permute-start | bytes 55304 | tf_op jit(solution)/shard_map/ppermute | solution.py:138
  52.0 6.6 %collective-permute-start.2 = (f16[8,1152]{1,0:T(8,128)(2,1)S(1)}, f16[8,1152]{1,0:T(8,128)(2,1)S(1)}, u32[]{:S(2)}, u32[]{:S(2)}) collective-permute-start(f16[8,1152]{1,0:T(8,128)(2,1)S(1)} %get-tuple-element.36), channel_id=1, source_target_pairs={{0,8},{4,12},{8,0},{12,4},{1,9},{5,13},{9,1},{13,5},{2,10},{6,14},... | collective-permute-start | bytes 55304 | tf_op jit(solution)/shard_map/ppermute | solution.py:138
  56.2 5.0 %collective-permute-start.3 = (f16[8,1152]{1,0:T(8,128)(2,1)S(1)}, f16[8,1152]{1,0:T(8,128)(2,1)S(1)}, u32[]{:S(2)}, u32[]{:S(2)}) collective-permute-start(f16[8,1152]{1,0:T(8,128)(2,1)S(1)} %get-tuple-element.35), channel_id=1, source_target_pairs={{0,12},{4,8},{8,4},{12,0},{1,13},{5,9},{9,5},{13,1},{2,14},{6,10},... | collective-permute-start | bytes 55304 | tf_op jit(solution)/shard_map/ppermute | solution.py:138
  61.3 0.7 collective-permute-start.7
  62.0 6.4 %collective-permute-start.8 = (f32[2,8,1152]{2,1,0:T(8,128)S(1)}, f32[2,8,1152]{2,1,0:T(8,128)S(1)}, u32[]{:S(2)}, u32[]{:S(2)}) collective-permute-start(f32[2,8,1152]{2,1,0:T(8,128)S(1)} %pad_maximum_fusion.5), channel_id=1, source_target_pairs={{0,64},{32,96},{64,0},{96,32},{128,192},{160,224},{192,128},{224,1... | collective-permute-start | bytes 221192 | tf_op jit(solution)/shard_map/ppermute | solution.py:143
  62.7 6.4 %collective-permute-start.4 = (bf16[8,1152]{1,0:T(8,128)(2,1)S(1)}, bf16[8,1152]{1,0:T(8,128)(2,1)S(1)}, u32[]{:S(2)}, u32[]{:S(2)}) collective-permute-start(bf16[8,1152]{1,0:T(8,128)(2,1)S(1)} %get-tuple-element.38), channel_id=1, source_target_pairs={{0,4},{4,0},{8,12},{12,8},{1,5},{5,1},{9,13},{13,9},{2,6},{6,2},{1... | collective-permute-start | bytes 55304 | tf_op jit(solution)/shard_map/ppermute | solution.py:138
  63.7 6.6 %collective-permute-start.5 = (bf16[8,1152]{1,0:T(8,128)(2,1)S(1)}, bf16[8,1152]{1,0:T(8,128)(2,1)S(1)}, u32[]{:S(2)}, u32[]{:S(2)}) collective-permute-start(bf16[8,1152]{1,0:T(8,128)(2,1)S(1)} %get-tuple-element.38), channel_id=1, source_target_pairs={{0,8},{4,12},{8,0},{12,4},{1,9},{5,13},{9,1},{13,5},{2,10},{6,14},... | collective-permute-start | bytes 55304 | tf_op jit(solution)/shard_map/ppermute | solution.py:138
  65.4 4.9 %collective-permute-start.6 = (bf16[8,1152]{1,0:T(8,128)(2,1)S(1)}, bf16[8,1152]{1,0:T(8,128)(2,1)S(1)}, u32[]{:S(2)}, u32[]{:S(2)}) collective-permute-start(bf16[8,1152]{1,0:T(8,128)(2,1)S(1)} %get-tuple-element.38), channel_id=1, source_target_pairs={{0,12},{4,8},{8,4},{12,0},{1,13},{5,9},{9,5},{13,1},{2,14},{6,10},... | collective-permute-start | bytes 55304 | tf_op jit(solution)/shard_map/ppermute | solution.py:138
  68.4 1.9 %collective-permute-start.9 = (f32[4,8,1152]{2,1,0:T(8,128)S(1)}, f32[4,8,1152]{2,1,0:T(8,128)S(1)}, u32[]{:S(2)}, u32[]{:S(2)}) collective-permute-start(f32[4,8,1152]{2,1,0:T(8,128)S(1)} %pad_maximum_fusion.2), channel_id=1, source_target_pairs={{0,128},{32,160},{64,192},{96,224},{128,0},{160,32},{192,64},{224,... | collective-permute-start | bytes 442376 | tf_op jit(solution)/shard_map/ppermute | solution.py:143
  94.4 4.7 %collective-permute-start.10 = (f32[1,8,1152]{2,1,0:T(8,128)S(1)}, f32[1,8,1152]{2,1,0:T(8,128)S(1)}, u32[]{:S(2)}, u32[]{:S(2)}) collective-permute-start(f32[1,8,1152]{2,1,0:T(8,128)S(1)} %bitcast.60), channel_id=1, source_target_pairs={{1,33},{33,1},{65,97},{97,65},{129,161},{161,129},{193,225},{225,1... | collective-permute-start | bytes 110600 | tf_op jit(solution)/shard_map/ppermute | solution.py:143
  99.1 10.0 %collective-permute-start.11 = (f32[2,8,1152]{2,1,0:T(8,128)S(1)}, f32[2,8,1152]{2,1,0:T(8,128)S(1)}, u32[]{:S(2)}, u32[]{:S(2)}) collective-permute-start(f32[2,8,1152]{2,1,0:T(8,128)S(1)} %pad_maximum_fusion.6), channel_id=1, source_target_pairs={{1,65},{33,97},{65,1},{97,33},{129,193},{161,225},{193,129},{225,1... | collective-permute-start | bytes 221192 | tf_op jit(solution)/shard_map/ppermute | solution.py:143
  109.2 11.3 %collective-permute-start.12 = (f32[4,8,1152]{2,1,0:T(8,128)S(1)}, f32[4,8,1152]{2,1,0:T(8,128)S(1)}, u32[]{:S(2)}, u32[]{:S(2)}) collective-permute-start(f32[4,8,1152]{2,1,0:T(8,128)S(1)} %pad_maximum_fusion.3), channel_id=1, source_target_pairs={{1,129},{33,161},{65,193},{97,225},{129,1},{161,33},{193,65},{225,... | collective-permute-start | bytes 442376 | tf_op jit(solution)/shard_map/ppermute | solution.py:143
  120.5 2.8 %copy-start = (f32[16,4608]{1,0:T(8,128)S(1)}, f32[16,4608]{1,0:T(8,128)}, u32[]{:S(2)}) copy-start(f32[16,4608]{1,0:T(8,128)} %refs_0_.1) | copy-start | bytes 884740
  120.5 2.8 %copy-start.1 = (f32[16,4608]{1,0:T(8,128)S(1)}, f32[16,4608]{1,0:T(8,128)}, u32[]{:S(2)}) copy-start(f32[16,4608]{1,0:T(8,128)} %refs_1_.1) | copy-start | bytes 884740
  120.5 2.7 %copy-start.2 = (f32[16,4608]{1,0:T(8,128)S(1)}, f32[16,4608]{1,0:T(8,128)}, u32[]{:S(2)}) copy-start(f32[16,4608]{1,0:T(8,128)} %refs_2_.1) | copy-start | bytes 884740
  120.5 5.2 %collective-permute-start.13 = (bf16[2,4,2,2,2,2,8,1152]{7,6,5,4,3,2,1,0:T(8,128)(2,1)S(1)}, bf16[2,4,2,2,2,2,8,1152]{7,6,5,4,3,2,1,0:T(8,128)(2,1)S(1)}, u32[]{:S(2)}, u32[]{:S(2)}) collective-permute-start(bf16[2,4,2,2,2,2,8,1152]{7,6,5,4,3,2,1,0:T(8,128)(2,1)S(1)} %bitcast.54), channel_id=1, source_target_pairs={{0,1},{1,0},{2,3},{3,2},{4,5},{5,4},{6,7},{7,6},{8,9},{9,8},{10,11... | collective-permute-start | bytes 7077896 | tf_op jit(solution)/shard_map/ppermute | solution.py:180

commit v8 on v6

--- a/solution.py
+++ b/solution.py
@@ -14,6 +14,7 @@
 WHOLE = (XL, ZH, ZM, ZL, CORES, XH, LOW, Y * COLS)
 COPIES = XH * Y * ZH * ZM
 STATES = 3
+PAIR_SCALE, COLUMN_SCALE = 256.0, 8.0
 VMEM = pl.BlockSpec(memory_space=pltpu.VMEM)
 ANY = pl.BlockSpec(memory_space=pl.ANY)
 SMALL = pltpu.CompilerParams(vmem_limit_bytes=2 * 2**20)
@@ -151,10 +152,11 @@
     came = lax.ppermute(split_theirs(whole), "c", SWAP)
     pair, olds = split_mine(whole, *[in_hbm(state) for state in states])
     pair = pair.astype(jnp.float32) + came.astype(jnp.float32)
-    column = add(exchange(pair.astype(jnp.float16)))
+    column = add(exchange((PAIR_SCALE * pair).astype(jnp.float16))) * (COLUMN_SCALE / PAIR_SCALE)
 
     came = [partner(column[m].astype(jnp.float16), m) for m in range(1, ZH * ZM)]
-    grad = sum((a.astype(jnp.float32) for a in came), column[0]) / (big * ZH * ZM * CORES)
+    grad = sum((a.astype(jnp.float32) for a in came), column[0])
+    grad = grad / (COLUMN_SCALE * big * ZH * ZM * CORES)
 
     part = adam(grad, *olds)[0].astype(jnp.bfloat16)
     grads = lax.all_to_all(jnp.broadcast_to(grad, (XH * Y, LOW, COLS)), ("xh", "y"), 0, 0, tiled=True)

time: 119 us -> 119 us (level)
  no operation moved by 1% of the time
where the time goes in v8:
time: 119 us
  blocking collectives  71.4 us (60%)
  starting transfers between devices  25.5 us (21%)
  waiting for transfers between devices  10.7 us (9%)
  Pallas kernels  8.44 us (7%)
  other arithmetic  1.29 us (1%)
    all_to_all x2, blocking collectives, exchange(): lax.all_to_all(chunks.reshape(-1, ZH * ZM, LOW, COLS), BIG, 0, 0, tiled=T...  71.4 us
    ppermute x6, starting transfers between devices, partner(): return lax.ppermute(a, ('zh', 'zm'), [(i, i ^ m) for i in range(ZH * ZM)])  13 us
    ppermute x6, waiting for transfers between devices, partner(): return lax.ppermute(a, ('zh', 'zm'), [(i, i ^ m) for i in range(ZH * ZM)])  7.19 us
    ppermute x1, starting transfers between devices, per_device(): came = lax.ppermute(part, 'c', SWAP)  5.73 us
    all_to_all x1, starting transfers between devices, per_device(): lax.all_to_all(jnp.broadcast_to(grad, (XH * Y, LOW, COLS)), ('xh', 'y'),...  3.42 us
    pallas_call x2, Pallas kernels, place(): pl.pallas_call(lambda *refs: place_kernel(of_other, *refs), out_shape=jax...  3.33 us
    ppermute x1, starting transfers between devices, per_device(): came = lax.ppermute(split_theirs(whole), 'c', SWAP)  3.33 us
  transfers between devices with their start and end apart: 9, of which 6 were waited for; matrix products, arithmetic and copies ran while one was open for 0% of the time, Pallas kernels for 4%

profile of v8, /device:TPU:1, one launch (start us, length us, event | category | flops | bytes accessed | tf_op | source)
XLA Modules:
  0.0 119.0 jit_solution(5699889332716650463)
XLA Ops:
  0.6 2.0 %split_theirs.1 = bf16[2,4,2,2,2,2,8,1152]{7,6,5,4,3,2,1,0:T(8,128)(2,1)S(1)} custom-call(bf16[2,2,2,2,2,2,8,4608]{7,6,5,4,3,2,1,0:T(8,128)(2,1)} %bitcast.56), custom_call_target="tpu_custom_call" | custom-call | bytes 4718592 | tf_op jit(solution)/shard_map/split_theirs/pallas_call | solution.py:54
  2.7 3.3 %collective-permute-start = (bf16[2,4,2,2,2,2,8,1152]{7,6,5,4,3,2,1,0:T(8,128)(2,1)S(1)}, bf16[2,4,2,2,2,2,8,1152]{7,6,5,4,3,2,1,0:T(8,128)(2,1)S(1)}, u32[]{:S(2)}, u32[]{:S(2)}) collective-permute-start(bf16[2,4,2,2,2,2,8,1152]{7,6,5,4,3,2,1,0:T(8,128)(2,1)S(1)} %split_theirs.1), channel_id=1, source_target_pairs={{0,1},{1,0},{2,3},{3,2},{4,5},{5,4},{6,7},{7,6},{8,9},{9,8},{10,11... | collective-permute-start | bytes 7077896 | tf_op jit(solution)/shard_map/ppermute | solution.py:152
  6.0 2.0 %split_mine.1 = (bf16[2,4,2,2,2,2,8,1152]{7,6,5,4,3,2,1,0:T(8,128)(2,1)S(1)}, f32[3,8,1152]{2,1,0:T(8,128)S(1)}) custom-call(bf16[2,2,2,2,2,2,8,4608]{7,6,5,4,3,2,1,0:T(8,128)(2,1)} %bitcast.57, f32[16,4608]{1,0:T(8,128)} %refs_0_.1, f32[16,4608]{1,0:T(8,128)} %refs_1_.1, f32[16,4608]{1,0:T(8,128)} %refs_2_.1), custom_call_target="tpu_custom_call" | custom-call | bytes 4718592 | tf_op jit(solution)/shard_map/split_mine/pallas_call | solution.py:67
  8.0 2.1 %collective-permute-done = bf16[2,4,2,2,2,2,8,1152]{7,6,5,4,3,2,1,0:T(8,128)(2,1)S(1)} collective-permute-done((bf16[2,4,2,2,2,2,8,1152]{7,6,5,4,3,2,1,0:T(8,128)(2,1)S(1)}, bf16[2,4,2,2,2,2,8,1152]{7,6,5,4,3,2,1,0:T(8,128)(2,1)S(1)}, u32[]{:S(2)}, u32[]{:S(2)}) %collective-permute-start) | collective-permute-done | bytes 2359328 | tf_op jit(solution)/shard_map/ppermute | solution.py:152
  10.2 0.9 multiply_convert_fusion
  11.0 37.6 %all_to_all.15 = f16[32,4,8,1152]{3,2,1,0:T(8,128)(2,1)S(1)} all-to-all(f16[32,4,8,1152]{3,2,1,0:T(8,128)(2,1)S(1)} %bitcast.59), channel_id=1, replica_groups=mesh['xh'=2,'y'=4,'xl'=2,'zh'=2,'zm'=2,'zl'=2,'c'=2] {'xh','y','xl','zl'}, dimensions={0} | all-to-all | bytes 4718592 | tf_op jit(solution)/shard_map/all_to_all | solution.py:133
  48.7 0.3 convert_reduce_fusion
  49.1 3.1 %collective-permute-start.1 = (f16[8,1152]{1,0:T(8,128)(2,1)S(1)}, f16[8,1152]{1,0:T(8,128)(2,1)S(1)}, u32[]{:S(2)}, u32[]{:S(2)}) collective-permute-start(f16[8,1152]{1,0:T(8,128)(2,1)S(1)} %get-tuple-element.26), channel_id=1, source_target_pairs={{0,4},{4,0},{8,12},{12,8},{1,5},{5,1},{9,13},{13,9},{2,6},{6,2},{1... | collective-permute-start | bytes 55304 | tf_op jit(solution)/shard_map/ppermute | solution.py:137
  52.1 4.2 %collective-permute-start.2 = (f16[8,1152]{1,0:T(8,128)(2,1)S(1)}, f16[8,1152]{1,0:T(8,128)(2,1)S(1)}, u32[]{:S(2)}, u32[]{:S(2)}) collective-permute-start(f16[8,1152]{1,0:T(8,128)(2,1)S(1)} %get-tuple-element.28), channel_id=1, source_target_pairs={{0,8},{4,12},{8,0},{12,4},{1,9},{5,13},{9,1},{13,5},{2,10},{6,14},... | collective-permute-start | bytes 55304 | tf_op jit(solution)/shard_map/ppermute | solution.py:137
  56.3 2.4 %collective-permute-done.2 = f16[8,1152]{1,0:T(8,128)(2,1)S(1)} collective-permute-done((f16[8,1152]{1,0:T(8,128)(2,1)S(1)}, f16[8,1152]{1,0:T(8,128)(2,1)S(1)}, u32[]{:S(2)}, u32[]{:S(2)}) %collective-permute-start.2) | collective-permute-done | bytes 18464 | tf_op jit(solution)/shard_map/ppermute | solution.py:137
  58.8 2.6 %collective-permute-done.3 = f16[8,1152]{1,0:T(8,128)(2,1)S(1)} collective-permute-done((f16[8,1152]{1,0:T(8,128)(2,1)S(1)}, f16[8,1152]{1,0:T(8,128)(2,1)S(1)}, u32[]{:S(2)}, u32[]{:S(2)}) %collective-permute-start.3) | collective-permute-done | bytes 18464 | tf_op jit(solution)/shard_map/ppermute | solution.py:137
  61.4 0.7 broadcast_in_dim.6
  62.2 3.4 %all-to-all-start.1 = ((f32[8,8,1152]{2,1,0:T(8,128)}), f32[8,8,1152]{2,1,0:T(8,128)S(1)}, u32[]{:S(2)}, u32[]{:S(2)}) async-start(f32[8,8,1152]{2,1,0:T(8,128)} %broadcast_in_dim.6), calls=%async_computation.1 | async-start | bytes 589824 | tf_op jit(solution)/shard_map/all_to_all | solution.py:162
  65.6 1.0 collective-permute-start.4
  66.6 1.8 %collective-permute-start.5 = (bf16[8,1152]{1,0:T(8,128)(2,1)S(1)}, bf16[8,1152]{1,0:T(8,128)(2,1)S(1)}, u32[]{:S(2)}, u32[]{:S(2)}) collective-permute-start(bf16[8,1152]{1,0:T(8,128)(2,1)S(1)} %get-tuple-element.23), channel_id=1, source_target_pairs={{0,8},{4,12},{8,0},{12,4},{1,9},{5,13},{9,1},{13,5},{2,10},{6,14},... | collective-permute-start | bytes 55304 | tf_op jit(solution)/shard_map/ppermute | solution.py:137
  68.3 3.0 %collective-permute-start.6 = (bf16[8,1152]{1,0:T(8,128)(2,1)S(1)}, bf16[8,1152]{1,0:T(8,128)(2,1)S(1)}, u32[]{:S(2)}, u32[]{:S(2)}) collective-permute-start(bf16[8,1152]{1,0:T(8,128)(2,1)S(1)} %get-tuple-element.23), channel_id=1, source_target_pairs={{0,12},{4,8},{8,4},{12,0},{1,13},{5,9},{9,5},{13,1},{2,14},{6,10},... | collective-permute-start | bytes 55304 | tf_op jit(solution)/shard_map/ppermute | solution.py:137
  71.3 1.9 %collective-permute-done.5 = bf16[8,1152]{1,0:T(8,128)(2,1)S(1)} collective-permute-done((bf16[8,1152]{1,0:T(8,128)(2,1)S(1)}, bf16[8,1152]{1,0:T(8,128)(2,1)S(1)}, u32[]{:S(2)}, u32[]{:S(2)}) %collective-permute-start.5) | collective-permute-done | bytes 18464 | tf_op jit(solution)/shard_map/ppermute | solution.py:137
  73.3 0.2 collective-permute-done.6
  73.7 33.8 %all_to_all.16 = bf16[32,4,8,1152]{3,2,1,0:T(8,128)(2,1)S(1)} all-to-all(bf16[32,4,8,1152]{3,2,1,0:T(8,128)(2,1)S(1)} %broadcast_in_dim.7), channel_id=1, replica_groups=mesh['xh'=2,'y'=4,'xl'=2,'zh'=2,'zm'=2,'zl'=2,'c'=2] {'xh','y','xl','zl'}, dimensions={0} | all-to-all | bytes 4718592 | tf_op jit(solution)/shard_map/all_to_all | solution.py:133
  107.5 5.7 %collective-permute-start.7 = (bf16[2,4,2,2,2,2,8,1152]{7,6,5,4,3,2,1,0:T(8,128)(2,1)S(1)}, bf16[2,4,2,2,2,2,8,1152]{7,6,5,4,3,2,1,0:T(8,128)(2,1)S(1)}, u32[]{:S(2)}, u32[]{:S(2)}) collective-permute-start(bf16[2,4,2,2,2,2,8,1152]{7,6,5,4,3,2,1,0:T(8,128)(2,1)S(1)} %bitcast.54), channel_id=1, source_target_pairs={{0,1},{1,0},{2,3},{3,2},{4,5},{5,4},{6,7},{7,6},{8,9},{9,8},{10,11... | collective-permute-start | bytes 7077896 | tf_op jit(solution)/shard_map/ppermute | solution.py:167
  113.2 1.7 %place_mine.1.refs_0_ = bf16[2,2,2,2,2,2,8,4608]{7,6,5,4,3,2,1,0:T(8,128)(2,1)} custom-call(bf16[2,4,2,2,2,2,8,1152]{7,6,5,4,3,2,1,0:T(8,128)(2,1)S(1)} %bitcast.55), custom_call_target="tpu_custom_call" | custom-call | bytes 4718592 | tf_op jit(solution)/shard_map/place_mine/pallas_call | solution.py:87
  114.9 1.0 new_states.1
  116.0 1.4 %collective-permute-done.7.refs_1_ = bf16[2,4,2,2,2,2,8,1152]{7,6,5,4,3,2,1,0:T(8,128)(2,1)S(1)} collective-permute-done((bf16[2,4,2,2,2,2,8,1152]{7,6,5,4,3,2,1,0:T(8,128)(2,1)S(1)}, bf16[2,4,2,2,2,2,8,1152]{7,6,5,4,3,2,1,0:T(8,128)(2,1)S(1)}, u32[]{:S(2)}, u32[]{:S(2)}) %collective-permute-start.7) | collective-permute-done | bytes 2359328 | tf_op jit(solution)/shard_map/ppermute | solution.py:167
  117.4 1.7 %place_theirs.1 = bf16[2,2,2,2,2,2,8,4608]{7,6,5,4,3,2,1,0:T(8,128)(2,1)} custom-call(bf16[2,2,2,2,2,2,8,4608]{7,6,5,4,3,2,1,0:T(8,128)(2,1)} %place_mine.1.refs_0_, bf16[2,4,2,2,2,2,8,1152]{7,6,5,4,3,2,1,0:T(8,128)(2,1)S(1)} %collective-permute-done.7.refs_1_), custom_call_target="tpu_custom_call", output_to_operand_aliasing={{}: (0, {})} | custom-call | bytes 4718592 | tf_op jit(solution)/shard_map/place_theirs/pallas_call | solution.py:87
  (15 shorter events, 0.3 us)
Async XLA Ops:
  2.7 7.5 %collective-permute-start = (bf16[2,4,2,2,2,2,8,1152]{7,6,5,4,3,2,1,0:T(8,128)(2,1)S(1)}, bf16[2,4,2,2,2,2,8,1152]{7,6,5,4,3,2,1,0:T(8,128)(2,1)S(1)}, u32[]{:S(2)}, u32[]{:S(2)}) collective-permute-start(bf16[2,4,2,2,2,2,8,1152]{7,6,5,4,3,2,1,0:T(8,128)(2,1)S(1)} %split_theirs.1), channel_id=1, source_target_pairs={{0,1},{1,0},{2,3},{3,2},{4,5},{5,4},{6,7},{7,6},{8,9},{9,8},{10,11... | collective-permute-start | bytes 7077896 | tf_op jit(solution)/shard_map/ppermute | solution.py:152
  49.1 7.3 %collective-permute-start.1 = (f16[8,1152]{1,0:T(8,128)(2,1)S(1)}, f16[8,1152]{1,0:T(8,128)(2,1)S(1)}, u32[]{:S(2)}, u32[]{:S(2)}) collective-permute-start(f16[8,1152]{1,0:T(8,128)(2,1)S(1)} %get-tuple-element.26), channel_id=1, source_target_pairs={{0,4},{4,0},{8,12},{12,8},{1,5},{5,1},{9,13},{13,9},{2,6},{6,2},{1... | collective-permute-start | bytes 55304 | tf_op jit(solution)/shard_map/ppermute | solution.py:137
  52.1 6.6 %collective-permute-start.2 = (f16[8,1152]{1,0:T(8,128)(2,1)S(1)}, f16[8,1152]{1,0:T(8,128)(2,1)S(1)}, u32[]{:S(2)}, u32[]{:S(2)}) collective-permute-start(f16[8,1152]{1,0:T(8,128)(2,1)S(1)} %get-tuple-element.28), channel_id=1, source_target_pairs={{0,8},{4,12},{8,0},{12,4},{1,9},{5,13},{9,1},{13,5},{2,10},{6,14},... | collective-permute-start | bytes 55304 | tf_op jit(solution)/shard_map/ppermute | solution.py:137
  56.3 5.0 %collective-permute-start.3 = (f16[8,1152]{1,0:T(8,128)(2,1)S(1)}, f16[8,1152]{1,0:T(8,128)(2,1)S(1)}, u32[]{:S(2)}, u32[]{:S(2)}) collective-permute-start(f16[8,1152]{1,0:T(8,128)(2,1)S(1)} %get-tuple-element.27), channel_id=1, source_target_pairs={{0,12},{4,8},{8,4},{12,0},{1,13},{5,9},{9,5},{13,1},{2,14},{6,10},... | collective-permute-start | bytes 55304 | tf_op jit(solution)/shard_map/ppermute | solution.py:137
  62.2 11.4 %all-to-all-start.1 = ((f32[8,8,1152]{2,1,0:T(8,128)}), f32[8,8,1152]{2,1,0:T(8,128)S(1)}, u32[]{:S(2)}, u32[]{:S(2)}) async-start(f32[8,8,1152]{2,1,0:T(8,128)} %broadcast_in_dim.6), calls=%async_computation.1 | async-start | bytes 589824 | tf_op jit(solution)/shard_map/all_to_all | solution.py:162
  65.6 5.7 %collective-permute-start.4 = (bf16[8,1152]{1,0:T(8,128)(2,1)S(1)}, bf16[8,1152]{1,0:T(8,128)(2,1)S(1)}, u32[]{:S(2)}, u32[]{:S(2)}) collective-permute-start(bf16[8,1152]{1,0:T(8,128)(2,1)S(1)} %get-tuple-element.23), channel_id=1, source_target_pairs={{0,4},{4,0},{8,12},{12,8},{1,5},{5,1},{9,13},{13,9},{2,6},{6,2},{1... | collective-permute-start | bytes 55304 | tf_op jit(solution)/shard_map/ppermute | solution.py:137
  66.6 6.7 %collective-permute-start.5 = (bf16[8,1152]{1,0:T(8,128)(2,1)S(1)}, bf16[8,1152]{1,0:T(8,128)(2,1)S(1)}, u32[]{:S(2)}, u32[]{:S(2)}) collective-permute-start(bf16[8,1152]{1,0:T(8,128)(2,1)S(1)} %get-tuple-element.23), channel_id=1, source_target_pairs={{0,8},{4,12},{8,0},{12,4},{1,9},{5,13},{9,1},{13,5},{2,10},{6,14},... | collective-permute-start | bytes 55304 | tf_op jit(solution)/shard_map/ppermute | solution.py:137
  68.3 5.2 %collective-permute-start.6 = (bf16[8,1152]{1,0:T(8,128)(2,1)S(1)}, bf16[8,1152]{1,0:T(8,128)(2,1)S(1)}, u32[]{:S(2)}, u32[]{:S(2)}) collective-permute-start(bf16[8,1152]{1,0:T(8,128)(2,1)S(1)} %get-tuple-element.23), channel_id=1, source_target_pairs={{0,12},{4,8},{8,4},{12,0},{1,13},{5,9},{9,5},{13,1},{2,14},{6,10},... | collective-permute-start | bytes 55304 | tf_op jit(solution)/shard_map/ppermute | solution.py:137
  107.5 7.4 %copy-start = (f32[16,4608]{1,0:T(8,128)S(1)}, f32[16,4608]{1,0:T(8,128)}, u32[]{:S(2)}) copy-start(f32[16,4608]{1,0:T(8,128)} %refs_0_.1) | copy-start | bytes 884740
  107.5 7.4 %copy-start.1 = (f32[16,4608]{1,0:T(8,128)S(1)}, f32[16,4608]{1,0:T(8,128)}, u32[]{:S(2)}) copy-start(f32[16,4608]{1,0:T(8,128)} %refs_1_.1) | copy-start | bytes 884740
  107.5 7.4 %copy-start.2 = (f32[16,4608]{1,0:T(8,128)S(1)}, f32[16,4608]{1,0:T(8,128)}, u32[]{:S(2)}) copy-start(f32[16,4608]{1,0:T(8,128)} %refs_2_.1) | copy-start | bytes 884740
  107.5 9.9 %collective-permute-start.7 = (bf16[2,4,2,2,2,2,8,1152]{7,6,5,4,3,2,1,0:T(8,128)(2,1)S(1)}, bf16[2,4,2,2,2,2,8,1152]{7,6,5,4,3,2,1,0:T(8,128)(2,1)S(1)}, u32[]{:S(2)}, u32[]{:S(2)}) collective-permute-start(bf16[2,4,2,2,2,2,8,1152]{7,6,5,4,3,2,1,0:T(8,128)(2,1)S(1)} %bitcast.54), channel_id=1, source_target_pairs={{0,1},{1,0},{2,3},{3,2},{4,5},{5,4},{6,7},{7,6},{8,9},{9,8},{10,11... | collective-permute-start | bytes 7077896 | tf_op jit(solution)/shard_map/ppermute | solution.py:167

commit v9 on v8

--- a/solution.py
+++ b/solution.py
@@ -15,6 +15,8 @@
 COPIES = XH * Y * ZH * ZM
 STATES = 3
 PAIR_SCALE, COLUMN_SCALE = 256.0, 8.0
+BLOCKS = ZH * ZM
+DEVICES = XH * Y * XL * ZL * ZH * ZM * CORES
 VMEM = pl.BlockSpec(memory_space=pltpu.VMEM)
 ANY = pl.BlockSpec(memory_space=pl.ANY)
 SMALL = pltpu.CompilerParams(vmem_limit_bytes=2 * 2**20)
@@ -39,41 +41,41 @@
         copy.wait()
 
 
-def split_theirs_kernel(whole, pieces, sems):
-    copy_all(views(whole, pieces, 1 - lax.axis_index("c")), sems)
-
-
-def split_mine_kernel(whole, master, moment1, moment2, pieces, olds, sems):
+def split_theirs_kernel(whole, master, moment1, moment2, pieces, olds, sems):
     rows = pl.ds(pl.multiple_of(lax.axis_index("xh") * LOW, LOW), LOW)
     cols = pl.ds(pl.multiple_of(lax.axis_index("y") * COLS, 128), COLS)
     states = [(state.at[rows, cols], olds.at[i]) for i, state in enumerate((master, moment1, moment2))]
-    copy_all(views(whole, pieces, lax.axis_index("c")) + states, sems)
-
-
-def split_theirs(whole):
+    copy_all(views(whole, pieces, 1 - lax.axis_index("c")) + states, sems)
+
+
+def split_mine_kernel(whole, pieces, sems):
+    copy_all(views(whole, pieces, lax.axis_index("c")), sems)
+
+
+def split_theirs(whole, *states):
     return pl.pallas_call(
         split_theirs_kernel,
+        out_shape=[pltpu.VMEM(SHAPE, whole.dtype), pltpu.VMEM((STATES, LOW, COLS), jnp.float32)],
+        in_specs=[ANY] * (1 + STATES),
+        out_specs=[ANY] * 2,
+        scratch_shapes=[pltpu.SemaphoreType.DMA((COPIES + STATES,))],
+        compiler_params=SMALL,
+        cost_estimate=pl.CostEstimate(flops=0, bytes_accessed=2 * whole.size, transcendentals=0),
+        name="split_theirs",
+    )(whole, *states)
+
+
+def split_mine(whole):
+    return pl.pallas_call(
+        split_mine_kernel,
         out_shape=pltpu.VMEM(SHAPE, whole.dtype),
         in_specs=[ANY],
         out_specs=ANY,
         scratch_shapes=[pltpu.SemaphoreType.DMA((COPIES,))],
         compiler_params=SMALL,
         cost_estimate=pl.CostEstimate(flops=0, bytes_accessed=2 * whole.size, transcendentals=0),
-        name="split_theirs",
+        name="split_mine",
     )(whole)
-
-
-def split_mine(whole, *states):
-    return pl.pallas_call(
-        split_mine_kernel,
-        out_shape=[pltpu.VMEM(SHAPE, whole.dtype), pltpu.VMEM((STATES, LOW, COLS), jnp.float32)],
-        in_specs=[ANY] * (1 + STATES),
-        out_specs=[ANY] * 2,
-        scratch_shapes=[pltpu.SemaphoreType.DMA((COPIES + STATES,))],
-        compiler_params=SMALL,
-        cost_estimate=pl.CostEstimate(flops=0, bytes_accessed=2 * whole.size, transcendentals=0),
-        name="split_mine",
-    )(whole, *states)
 
 
 def place_kernel(of_other, *refs):
@@ -129,12 +131,67 @@
     )(grads, *states)
 
 
+def blocks_kernel(*refs):
+    columns, olds, (params, grad) = refs[:BLOCKS], refs[BLOCKS : 2 * BLOCKS], refs[2 * BLOCKS :]
+    for s in range(BLOCKS):
+        near = columns[0][s] + columns[1][s ^ 1]
+        far = columns[2][s ^ 2] + columns[3][s ^ 3]
+        total = (near + far) / (COLUMN_SCALE * DEVICES)
+        if s == 0:
+            grad[...] = total
+        old = olds[s]
+        params[s] = adam(total, old[0], old[1], old[2])[0].astype(params.dtype)
+
+
+def blocks(columns, olds):
+    size = BLOCKS * LOW * COLS
+    return pl.pallas_call(
+        blocks_kernel,
+        out_shape=[
+            jax.ShapeDtypeStruct((BLOCKS, LOW, COLS), jnp.bfloat16),
+            jax.ShapeDtypeStruct((LOW, COLS), jnp.float32),
+        ],
+        in_specs=[VMEM] * (2 * BLOCKS),
+        out_specs=[VMEM] * 2,
+        compiler_params=pltpu.CompilerParams(vmem_limit_bytes=8 * 2**20),
+        cost_estimate=pl.CostEstimate(flops=20 * size, bytes_accessed=30 * size, transcendentals=size),
+        name="blocks",
+    )(*columns, *olds)
+
+
+def spread_kernel(mine, *refs):
+    theirs, out = refs[:-1], refs[-1]
+    core = lax.axis_index("c")
+    for s in range(BLOCKS):
+        block = mine[s]
+        if s:
+            block = jnp.where(core == 0, block.astype(jnp.float32), theirs[s - 1][...].astype(jnp.float32))
+            block = block.astype(out.dtype)
+        for p in range(out.shape[0]):
+            out[p, s] = block
+
+
+def spread(mine, theirs):
+    shape = (XH * Y * XL * ZL, BLOCKS, LOW, COLS)
+    return pl.pallas_call(
+        spread_kernel,
+        out_shape=pltpu.VMEM(shape, mine.dtype),
+        in_specs=[VMEM] * BLOCKS,
+        out_specs=VMEM,
+        compiler_params=pltpu.CompilerParams(vmem_limit_bytes=8 * 2**20),
+        cost_estimate=pl.CostEstimate(flops=0, bytes_accessed=64 * mine.size, transcendentals=0),
+        name="spread",
+    )(mine, *theirs)
+
+
 def exchange(chunks):
-    return lax.all_to_all(chunks.reshape(-1, ZH * ZM, LOW, COLS), BIG, 0, 0, tiled=True)
-
-
-def partner(a, m):
-    return lax.ppermute(a, ("zh", "zm"), [(i, i ^ m) for i in range(ZH * ZM)])
+    return lax.all_to_all(chunks.reshape(-1, BLOCKS, LOW, COLS), BIG, 0, 0, tiled=True)
+
+
+def partner(a, m, core=None):
+    cores = range(CORES) if core is None else (core,)
+    pairs = [(i * CORES + c, (i ^ m) * CORES + c) for i in range(BLOCKS) for c in cores]
+    return lax.ppermute(a, ("zh", "zm", "c"), pairs)
 
 
 def add(parts):
@@ -143,26 +200,28 @@
 
 def per_device(gradients, *states):
     rows, width = gradients.shape[2:]
-    big = XH * Y * XL * ZL
+    partners = range(1, BLOCKS)
 
     def in_hbm(a):
         return pltpu.with_memory_space_constraint(a, pltpu.HBM)
 
     whole = in_hbm(gradients.reshape(WHOLE))
-    came = lax.ppermute(split_theirs(whole), "c", SWAP)
-    pair, olds = split_mine(whole, *[in_hbm(state) for state in states])
-    pair = pair.astype(jnp.float32) + came.astype(jnp.float32)
-    column = add(exchange((PAIR_SCALE * pair).astype(jnp.float16))) * (COLUMN_SCALE / PAIR_SCALE)
-
-    came = [partner(column[m].astype(jnp.float16), m) for m in range(1, ZH * ZM)]
-    grad = sum((a.astype(jnp.float32) for a in came), column[0])
-    grad = grad / (COLUMN_SCALE * big * ZH * ZM * CORES)
-
-    part = adam(grad, *olds)[0].astype(jnp.bfloat16)
+    theirs, old = split_theirs(whole, *[in_hbm(state) for state in states])
+    came = lax.ppermute(theirs, "c", SWAP)
+    far = partner(old, 2, 0)
+    olds = [old, partner(old, 1, 0), far, partner(old, 3, 0)]
+    pair = split_mine(whole).astype(jnp.float32) + came.astype(jnp.float32)
+    pair, olds = lax.optimization_barrier(((PAIR_SCALE * pair).astype(jnp.float16), olds))
+
+    column = add(exchange(pair)) * (COLUMN_SCALE / PAIR_SCALE)
+    column = column.astype(jnp.float16)
+    columns = [column] + [partner(column, m) for m in partners]
+    mine, grad = blocks([a.astype(jnp.float32) for a in columns], olds)
+
     grads = lax.all_to_all(jnp.broadcast_to(grad, (XH * Y, LOW, COLS)), ("xh", "y"), 0, 0, tiled=True)
-    part = jnp.stack([part] + [partner(part, m) for m in range(1, ZH * ZM)])
-    part, grads = lax.optimization_barrier((part, grads))
-    part = exchange(jnp.broadcast_to(part, (big, *part.shape))).reshape(SHAPE)
+    theirs = [partner(mine[0], m, 1) for m in partners]
+    mine, theirs, grads = lax.optimization_barrier((mine, theirs, grads))
+    part = exchange(spread(mine, theirs)).reshape(SHAPE)
     part, grads = lax.optimization_barrier((part, grads))
     came = lax.ppermute(part, "c", SWAP)
     params = place(True, came, (place(False, part),))

time: 119 us -> 119 us (level)
  starting transfers between devices: 25.5 us -> 34.1 us
  blocking collectives: 71.4 us -> 63.4 us
    all_to_all x2, blocking collectives: 71.4 us -> 63.4 us  [exchange(): lax.all_to_all(chunks.reshape(-1, BLOCKS, LOW, COLS), BIG, 0, 0, tiled=True)]
    ppermute x7 -> x10, starting transfers between devices: 16.4 us -> 23.2 us  [the longest x9 19.8 us: partner(): return lax.ppermute(a, ('zh', 'zm', 'c'), pairs)]
    ppermute x1, starting transfers between devices: 5.73 us -> 7.49 us  [per_device(): came = lax.ppermute(part, 'c', SWAP)]
    ppermute x7 -> x10, waiting for transfers between devices: 9.31 us -> 8.31 us  [the longest x9 8.2 us: partner(): return lax.ppermute(a, ('zh', 'zm', 'c'), pairs)]
    pallas_call x2 -> x4, Pallas kernels: 4.06 us -> 4.41 us  [the longest x1 2.06 us: split_theirs(): pl.pallas_call(split_theirs_kernel, out_shape=[pltpu.VMEM(SHAPE, whole.dt...]
  transfers between devices with their start and end apart: 9 -> 12, of which waited for: 6 -> 6; matrix products, arithmetic and copies ran while one was open for 0% -> 1% of each run, Pallas kernels for 4% -> 4%
where the time goes in v9:
time: 119 us
  blocking collectives  63.4 us (53%)
  starting transfers between devices  34.1 us (29%)
  waiting for transfers between devices  9.72 us (8%)
  Pallas kernels  8.79 us (7%)
  other arithmetic  1.22 us (1%)
    all_to_all x2, blocking collectives, exchange(): lax.all_to_all(chunks.reshape(-1, BLOCKS, LOW, COLS), BIG, 0, 0, tiled=True)  63.4 us
    ppermute x9, starting transfers between devices, partner(): return lax.ppermute(a, ('zh', 'zm', 'c'), pairs)  19.8 us
    ppermute x9, waiting for transfers between devices, partner(): return lax.ppermute(a, ('zh', 'zm', 'c'), pairs)  8.2 us
    ppermute x1, starting transfers between devices, per_device(): came = lax.ppermute(part, 'c', SWAP)  7.49 us
    all_to_all x1, starting transfers between devices, per_device(): lax.all_to_all(jnp.broadcast_to(grad, (XH * Y, LOW, COLS)), ('xh', 'y'),...  3.42 us
    pallas_call x2, Pallas kernels, place(): pl.pallas_call(lambda *refs: place_kernel(of_other, *refs), out_shape=jax...  3.33 us
    ppermute x1, starting transfers between devices, per_device(): came = lax.ppermute(theirs, 'c', SWAP)  3.33 us
  transfers between devices with their start and end apart: 12, of which 6 were waited for; matrix products, arithmetic and copies ran while one was open for 1% of the time, Pallas kernels for 4%

profile of v9, /device:TPU:1, one launch (start us, length us, event | category | flops | bytes accessed | tf_op | source)
XLA Modules:
  0.0 118.8 jit_solution(8131528164780743181)
XLA Ops:
  0.6 2.1 %split_theirs.1 = (bf16[2,4,2,2,2,2,8,1152]{7,6,5,4,3,2,1,0:T(8,128)(2,1)S(1)}, f32[3,8,1152]{2,1,0:T(8,128)S(1)}) custom-call(bf16[2,2,2,2,2,2,8,4608]{7,6,5,4,3,2,1,0:T(8,128)(2,1)} %bitcast.8, f32[16,4608]{1,0:T(8,128)} %refs_0_.1, f32[16,4608]{1,0:T(8,128)} %refs_1_.1, f32[16,4608]{1,0:T(8,128)} %refs_2_.1), custom_call_target="tpu_custom_call" | custom-call | bytes 4718592 | tf_op jit(solution)/shard_map/split_theirs/pallas_call | solution.py:56
  2.7 3.3 %collective-permute-start = (bf16[2,4,2,2,2,2,8,1152]{7,6,5,4,3,2,1,0:T(8,128)(2,1)S(1)}, bf16[2,4,2,2,2,2,8,1152]{7,6,5,4,3,2,1,0:T(8,128)(2,1)S(1)}, u32[]{:S(2)}, u32[]{:S(2)}) collective-permute-start(bf16[2,4,2,2,2,2,8,1152]{7,6,5,4,3,2,1,0:T(8,128)(2,1)S(1)} %get-tuple-element.23), channel_id=1, source_target_pairs={{0,1},{1,0},{2,3},{3,2},{4,5},{5,4},{6,7},{7,6},{8,9},{9,8},{10,11... | collective-permute-start | bytes 7077896 | tf_op jit(solution)/shard_map/ppermute | solution.py:210
  6.0 0.7 collective-permute-start.1
  6.7 0.7 collective-permute-start.2
  7.4 0.7 collective-permute-start.3
  8.0 2.0 %split_mine.1 = bf16[2,4,2,2,2,2,8,1152]{7,6,5,4,3,2,1,0:T(8,128)(2,1)S(1)} custom-call(bf16[2,2,2,2,2,2,8,4608]{7,6,5,4,3,2,1,0:T(8,128)(2,1)} %bitcast.9), custom_call_target="tpu_custom_call" | custom-call | bytes 4718592 | tf_op jit(solution)/shard_map/split_mine/pallas_call | solution.py:69
  10.2 0.8 multiply_convert_fusion
  11.1 29.2 %all_to_all.15 = f16[32,4,8,1152]{3,2,1,0:T(8,128)(2,1)S(1)} all-to-all(f16[32,4,8,1152]{3,2,1,0:T(8,128)(2,1)S(1)} %bitcast.11), channel_id=1, replica_groups=mesh['xh'=2,'y'=4,'xl'=2,'zh'=2,'zm'=2,'zl'=2,'c'=2] {'xh','y','xl','zl'}, dimensions={0} | all-to-all | bytes 4718592 | tf_op jit(solution)/shard_map/all_to_all | solution.py:188
  40.6 1.5 %collective-permute-start.4 = (f16[4,8,1152]{2,1,0:T(8,128)(2,1)S(1)}, f16[4,8,1152]{2,1,0:T(8,128)(2,1)S(1)}, u32[]{:S(2)}, u32[]{:S(2)}) collective-permute-start(f16[4,8,1152]{2,1,0:T(8,128)(2,1)S(1)} %get-tuple-element.43), channel_id=1, source_target_pairs={{0,4},{1,5},{4,0},{5,1},{8,12},{9,13},{12,8},{13,9},{2,6},{3,7},{6... | collective-permute-start | bytes 221192 | tf_op jit(solution)/shard_map/ppermute | solution.py:194
  42.1 4.9 %collective-permute-start.5 = (f16[4,8,1152]{2,1,0:T(8,128)(2,1)S(1)}, f16[4,8,1152]{2,1,0:T(8,128)(2,1)S(1)}, u32[]{:S(2)}, u32[]{:S(2)}) collective-permute-start(f16[4,8,1152]{2,1,0:T(8,128)(2,1)S(1)} %get-tuple-element.43), channel_id=1, source_target_pairs={{0,8},{1,9},{4,12},{5,13},{8,0},{9,1},{12,4},{13,5},{2,10},{3,11},... | collective-permute-start | bytes 221192 | tf_op jit(solution)/shard_map/ppermute | solution.py:194
  47.1 4.2 %collective-permute-done.5 = f16[4,8,1152]{2,1,0:T(8,128)(2,1)S(1)} collective-permute-done((f16[4,8,1152]{2,1,0:T(8,128)(2,1)S(1)}, f16[4,8,1152]{2,1,0:T(8,128)(2,1)S(1)}, u32[]{:S(2)}, u32[]{:S(2)}) %collective-permute-start.5) | collective-permute-done | bytes 73760 | tf_op jit(solution)/shard_map/ppermute | solution.py:194
  51.3 2.2 %collective-permute-done.6 = f16[4,8,1152]{2,1,0:T(8,128)(2,1)S(1)} collective-permute-done((f16[4,8,1152]{2,1,0:T(8,128)(2,1)S(1)}, f16[4,8,1152]{2,1,0:T(8,128)(2,1)S(1)}, u32[]{:S(2)}, u32[]{:S(2)}) %collective-permute-start.6) | collective-permute-done | bytes 73760 | tf_op jit(solution)/shard_map/ppermute | solution.py:194
  53.7 0.7 broadcast_in_dim.3
  54.4 3.4 %all-to-all-start.1 = ((f32[8,8,1152]{2,1,0:T(8,128)}), f32[8,8,1152]{2,1,0:T(8,128)S(1)}, u32[]{:S(2)}, u32[]{:S(2)}) async-start(f32[8,8,1152]{2,1,0:T(8,128)} %broadcast_in_dim.3), calls=%async_computation.1 | async-start | bytes 589824 | tf_op jit(solution)/shard_map/all_to_all | solution.py:221
  57.8 3.1 %collective-permute-start.7 = (bf16[8,1152]{1,0:T(8,128)(2,1)S(1)}, bf16[8,1152]{1,0:T(8,128)(2,1)S(1)}, u32[]{:S(2)}, u32[]{:S(2)}) collective-permute-start(bf16[8,1152]{1,0:T(8,128)(2,1)S(1)} %slice_bitcast_fusion), channel_id=1, source_target_pairs={{1,5},{5,1},{9,13},{13,9},{3,7},{7,3},{11,15},{15,11},{17,21},{21,... | collective-permute-start | bytes 55304 | tf_op jit(solution)/shard_map/ppermute | solution.py:194
  61.0 3.4 %collective-permute-start.8 = (bf16[8,1152]{1,0:T(8,128)(2,1)S(1)}, bf16[8,1152]{1,0:T(8,128)(2,1)S(1)}, u32[]{:S(2)}, u32[]{:S(2)}) collective-permute-start(bf16[8,1152]{1,0:T(8,128)(2,1)S(1)} %slice_bitcast_fusion), channel_id=1, source_target_pairs={{1,9},{5,13},{9,1},{13,5},{3,11},{7,15},{11,3},{15,7},{17,25},{21,... | collective-permute-start | bytes 55304 | tf_op jit(solution)/shard_map/ppermute | solution.py:194
  64.4 4.8 %collective-permute-start.9 = (bf16[8,1152]{1,0:T(8,128)(2,1)S(1)}, bf16[8,1152]{1,0:T(8,128)(2,1)S(1)}, u32[]{:S(2)}, u32[]{:S(2)}) collective-permute-start(bf16[8,1152]{1,0:T(8,128)(2,1)S(1)} %slice_bitcast_fusion), channel_id=1, source_target_pairs={{1,13},{5,9},{9,5},{13,1},{3,15},{7,11},{11,7},{15,3},{17,29},{21,... | collective-permute-start | bytes 55304 | tf_op jit(solution)/shard_map/ppermute | solution.py:194
  69.4 1.6 %collective-permute-done.9.refs_2_ = bf16[8,1152]{1,0:T(8,128)(2,1)S(1)} collective-permute-done((bf16[8,1152]{1,0:T(8,128)(2,1)S(1)}, bf16[8,1152]{1,0:T(8,128)(2,1)S(1)}, u32[]{:S(2)}, u32[]{:S(2)}) %collective-permute-start.9) | collective-permute-done | bytes 18464 | tf_op jit(solution)/shard_map/ppermute | solution.py:194
  71.2 34.3 %all_to_all.16 = bf16[32,4,8,1152]{3,2,1,0:T(8,128)(2,1)S(1)} all-to-all(bf16[32,4,8,1152]{3,2,1,0:T(8,128)(2,1)S(1)} %spread.1), channel_id=1, replica_groups=mesh['xh'=2,'y'=4,'xl'=2,'zh'=2,'zm'=2,'zl'=2,'c'=2] {'xh','y','xl','zl'}, dimensions={0} | all-to-all | bytes 4718592 | tf_op jit(solution)/shard_map/all_to_all | solution.py:188
  105.5 7.5 %collective-permute-start.10 = (bf16[2,4,2,2,2,2,8,1152]{7,6,5,4,3,2,1,0:T(8,128)(2,1)S(1)}, bf16[2,4,2,2,2,2,8,1152]{7,6,5,4,3,2,1,0:T(8,128)(2,1)S(1)}, u32[]{:S(2)}, u32[]{:S(2)}) collective-permute-start(bf16[2,4,2,2,2,2,8,1152]{7,6,5,4,3,2,1,0:T(8,128)(2,1)S(1)} %bitcast.6), channel_id=1, source_target_pairs={{0,1},{1,0},{2,3},{3,2},{4,5},{5,4},{6,7},{7,6},{8,9},{9,8},{10,11... | collective-permute-start | bytes 7077896 | tf_op jit(solution)/shard_map/ppermute | solution.py:226
  113.0 1.7 %place_mine.1.refs_0_ = bf16[2,2,2,2,2,2,8,4608]{7,6,5,4,3,2,1,0:T(8,128)(2,1)} custom-call(bf16[2,4,2,2,2,2,8,1152]{7,6,5,4,3,2,1,0:T(8,128)(2,1)S(1)} %bitcast.7), custom_call_target="tpu_custom_call" | custom-call | bytes 4718592 | tf_op jit(solution)/shard_map/place_mine/pallas_call | solution.py:89
  114.7 1.0 new_states.1
  115.7 1.4 %collective-permute-done.10.refs_1_ = bf16[2,4,2,2,2,2,8,1152]{7,6,5,4,3,2,1,0:T(8,128)(2,1)S(1)} collective-permute-done((bf16[2,4,2,2,2,2,8,1152]{7,6,5,4,3,2,1,0:T(8,128)(2,1)S(1)}, bf16[2,4,2,2,2,2,8,1152]{7,6,5,4,3,2,1,0:T(8,128)(2,1)S(1)}, u32[]{:S(2)}, u32[]{:S(2)}) %collective-permute-start.10) | collective-permute-done | bytes 2359328 | tf_op jit(solution)/shard_map/ppermute | solution.py:226
  117.1 1.7 %place_theirs.1 = bf16[2,2,2,2,2,2,8,4608]{7,6,5,4,3,2,1,0:T(8,128)(2,1)} custom-call(bf16[2,2,2,2,2,2,8,4608]{7,6,5,4,3,2,1,0:T(8,128)(2,1)} %place_mine.1.refs_0_, bf16[2,4,2,2,2,2,8,1152]{7,6,5,4,3,2,1,0:T(8,128)(2,1)S(1)} %collective-permute-done.10.refs_1_), custom_call_target="tpu_custom_call", output_to_operand_aliasing={{}: (0, {})} | custom-call | bytes 4718592 | tf_op jit(solution)/shard_map/place_theirs/pallas_call | solution.py:89
  (23 shorter events, 1.0 us)
Async XLA Ops:
  2.7 7.5 %collective-permute-start = (bf16[2,4,2,2,2,2,8,1152]{7,6,5,4,3,2,1,0:T(8,128)(2,1)S(1)}, bf16[2,4,2,2,2,2,8,1152]{7,6,5,4,3,2,1,0:T(8,128)(2,1)S(1)}, u32[]{:S(2)}, u32[]{:S(2)}) collective-permute-start(bf16[2,4,2,2,2,2,8,1152]{7,6,5,4,3,2,1,0:T(8,128)(2,1)S(1)} %get-tuple-element.23), channel_id=1, source_target_pairs={{0,1},{1,0},{2,3},{3,2},{4,5},{5,4},{6,7},{7,6},{8,9},{9,8},{10,11... | collective-permute-start | bytes 7077896 | tf_op jit(solution)/shard_map/ppermute | solution.py:210
  6.0 5.0 %collective-permute-start.1 = (f32[3,8,1152]{2,1,0:T(8,128)S(1)}, f32[3,8,1152]{2,1,0:T(8,128)S(1)}, u32[]{:S(2)}, u32[]{:S(2)}) collective-permute-start(f32[3,8,1152]{2,1,0:T(8,128)S(1)} %get-tuple-element.26.refs_4_), channel_id=1, source_target_pairs={{0,4},{4,0},{8,12},{12,8},{2,6},{6,2},{10,14},{14,10},{16,20},{20,... | collective-permute-start | bytes 331784 | tf_op jit(solution)/shard_map/ppermute | solution.py:194
  6.7 4.4 %collective-permute-start.2 = (f32[3,8,1152]{2,1,0:T(8,128)S(1)}, f32[3,8,1152]{2,1,0:T(8,128)S(1)}, u32[]{:S(2)}, u32[]{:S(2)}) collective-permute-start(f32[3,8,1152]{2,1,0:T(8,128)S(1)} %get-tuple-element.26.refs_4_), channel_id=1, source_target_pairs={{0,8},{4,12},{8,0},{12,4},{2,10},{6,14},{10,2},{14,6},{16,24},{20,... | collective-permute-start | bytes 331784 | tf_op jit(solution)/shard_map/ppermute | solution.py:194
  7.4 3.7 %collective-permute-start.3 = (f32[3,8,1152]{2,1,0:T(8,128)S(1)}, f32[3,8,1152]{2,1,0:T(8,128)S(1)}, u32[]{:S(2)}, u32[]{:S(2)}) collective-permute-start(f32[3,8,1152]{2,1,0:T(8,128)S(1)} %get-tuple-element.26.refs_4_), channel_id=1, source_target_pairs={{0,12},{4,8},{8,4},{12,0},{2,14},{6,10},{10,6},{14,2},{16,28},{20,... | collective-permute-start | bytes 331784 | tf_op jit(solution)/shard_map/ppermute | solution.py:194
  40.6 6.5 %collective-permute-start.4 = (f16[4,8,1152]{2,1,0:T(8,128)(2,1)S(1)}, f16[4,8,1152]{2,1,0:T(8,128)(2,1)S(1)}, u32[]{:S(2)}, u32[]{:S(2)}) collective-permute-start(f16[4,8,1152]{2,1,0:T(8,128)(2,1)S(1)} %get-tuple-element.43), channel_id=1, source_target_pairs={{0,4},{1,5},{4,0},{5,1},{8,12},{9,13},{12,8},{13,9},{2,6},{3,7},{6... | collective-permute-start | bytes 221192 | tf_op jit(solution)/shard_map/ppermute | solution.py:194
  42.1 9.2 %collective-permute-start.5 = (f16[4,8,1152]{2,1,0:T(8,128)(2,1)S(1)}, f16[4,8,1152]{2,1,0:T(8,128)(2,1)S(1)}, u32[]{:S(2)}, u32[]{:S(2)}) collective-permute-start(f16[4,8,1152]{2,1,0:T(8,128)(2,1)S(1)} %get-tuple-element.43), channel_id=1, source_target_pairs={{0,8},{1,9},{4,12},{5,13},{8,0},{9,1},{12,4},{13,5},{2,10},{3,11},... | collective-permute-start | bytes 221192 | tf_op jit(solution)/shard_map/ppermute | solution.py:194
  47.0 6.5 %collective-permute-start.6 = (f16[4,8,1152]{2,1,0:T(8,128)(2,1)S(1)}, f16[4,8,1152]{2,1,0:T(8,128)(2,1)S(1)}, u32[]{:S(2)}, u32[]{:S(2)}) collective-permute-start(f16[4,8,1152]{2,1,0:T(8,128)(2,1)S(1)} %get-tuple-element.43), channel_id=1, source_target_pairs={{0,12},{1,13},{4,8},{5,9},{8,4},{9,5},{12,0},{13,1},{2,14},{3,15},... | collective-permute-start | bytes 221192 | tf_op jit(solution)/shard_map/ppermute | solution.py:194
  54.4 16.6 %all-to-all-start.1 = ((f32[8,8,1152]{2,1,0:T(8,128)}), f32[8,8,1152]{2,1,0:T(8,128)S(1)}, u32[]{:S(2)}, u32[]{:S(2)}) async-start(f32[8,8,1152]{2,1,0:T(8,128)} %broadcast_in_dim.3), calls=%async_computation.1 | async-start | bytes 589824 | tf_op jit(solution)/shard_map/all_to_all | solution.py:221
  57.8 11.4 %collective-permute-start.7 = (bf16[8,1152]{1,0:T(8,128)(2,1)S(1)}, bf16[8,1152]{1,0:T(8,128)(2,1)S(1)}, u32[]{:S(2)}, u32[]{:S(2)}) collective-permute-start(bf16[8,1152]{1,0:T(8,128)(2,1)S(1)} %slice_bitcast_fusion), channel_id=1, source_target_pairs={{1,5},{5,1},{9,13},{13,9},{3,7},{7,3},{11,15},{15,11},{17,21},{21,... | collective-permute-start | bytes 55304 | tf_op jit(solution)/shard_map/ppermute | solution.py:194
  61.0 8.4 %collective-permute-start.8 = (bf16[8,1152]{1,0:T(8,128)(2,1)S(1)}, bf16[8,1152]{1,0:T(8,128)(2,1)S(1)}, u32[]{:S(2)}, u32[]{:S(2)}) collective-permute-start(bf16[8,1152]{1,0:T(8,128)(2,1)S(1)} %slice_bitcast_fusion), channel_id=1, source_target_pairs={{1,9},{5,13},{9,1},{13,5},{3,11},{7,15},{11,3},{15,7},{17,25},{21,... | collective-permute-start | bytes 55304 | tf_op jit(solution)/shard_map/ppermute | solution.py:194
  64.4 6.6 %collective-permute-start.9 = (bf16[8,1152]{1,0:T(8,128)(2,1)S(1)}, bf16[8,1152]{1,0:T(8,128)(2,1)S(1)}, u32[]{:S(2)}, u32[]{:S(2)}) collective-permute-start(bf16[8,1152]{1,0:T(8,128)(2,1)S(1)} %slice_bitcast_fusion), channel_id=1, source_target_pairs={{1,13},{5,9},{9,5},{13,1},{3,15},{7,11},{11,7},{15,3},{17,29},{21,... | collective-permute-start | bytes 55304 | tf_op jit(solution)/shard_map/ppermute | solution.py:194
  105.5 9.2 %copy-start = (f32[16,4608]{1,0:T(8,128)S(1)}, f32[16,4608]{1,0:T(8,128)}, u32[]{:S(2)}) copy-start(f32[16,4608]{1,0:T(8,128)} %refs_0_.1) | copy-start | bytes 884740
  105.5 9.2 %copy-start.1 = (f32[16,4608]{1,0:T(8,128)S(1)}, f32[16,4608]{1,0:T(8,128)}, u32[]{:S(2)}) copy-start(f32[16,4608]{1,0:T(8,128)} %refs_1_.1) | copy-start | bytes 884740
  105.5 9.2 %copy-start.2 = (f32[16,4608]{1,0:T(8,128)S(1)}, f32[16,4608]{1,0:T(8,128)}, u32[]{:S(2)}) copy-start(f32[16,4608]{1,0:T(8,128)} %refs_2_.1) | copy-start | bytes 884740
  105.5 11.7 %collective-permute-start.10 = (bf16[2,4,2,2,2,2,8,1152]{7,6,5,4,3,2,1,0:T(8,128)(2,1)S(1)}, bf16[2,4,2,2,2,2,8,1152]{7,6,5,4,3,2,1,0:T(8,128)(2,1)S(1)}, u32[]{:S(2)}, u32[]{:S(2)}) collective-permute-start(bf16[2,4,2,2,2,2,8,1152]{7,6,5,4,3,2,1,0:T(8,128)(2,1)S(1)} %bitcast.6), channel_id=1, source_target_pairs={{0,1},{1,0},{2,3},{3,2},{4,5},{5,4},{6,7},{7,6},{8,9},{9,8},{10,11... | collective-permute-start | bytes 7077896 | tf_op jit(solution)/shard_map/ppermute | solution.py:226

commit v10 on v8

--- a/solution.py
+++ b/solution.py
@@ -12,7 +12,6 @@
 LOW, COLS = 8, 1152
 SHAPE = (XH, Y, XL, ZL, ZH, ZM, LOW, COLS)
 WHOLE = (XL, ZH, ZM, ZL, CORES, XH, LOW, Y * COLS)
-COPIES = XH * Y * ZH * ZM
 STATES = 3
 PAIR_SCALE, COLUMN_SCALE = 256.0, 8.0
 VMEM = pl.BlockSpec(memory_space=pltpu.VMEM)
@@ -31,23 +30,26 @@
     ]
 
 
-def copy_all(pairs, sems):
-    copies = [pltpu.make_async_copy(a, b, sems.at[k]) for k, (a, b) in enumerate(pairs)]
-    for copy in copies:
-        copy.start()
-    for copy in copies:
-        copy.wait()
+def copy_all(pairs, pieces, sem):
+    for source, target in pairs:
+        pltpu.make_async_copy(source, target, sem).start()
+    pltpu.make_async_copy(pieces, pieces, sem).wait()
 
 
-def split_theirs_kernel(whole, pieces, sems):
-    copy_all(views(whole, pieces, 1 - lax.axis_index("c")), sems)
+def split_theirs_kernel(whole, pieces, sem):
+    copy_all(views(whole, pieces, 1 - lax.axis_index("c")), pieces, sem)
 
 
-def split_mine_kernel(whole, master, moment1, moment2, pieces, olds, sems):
+def split_mine_kernel(whole, master, moment1, moment2, pieces, olds, sem, sems):
     rows = pl.ds(pl.multiple_of(lax.axis_index("xh") * LOW, LOW), LOW)
     cols = pl.ds(pl.multiple_of(lax.axis_index("y") * COLS, 128), COLS)
     states = [(state.at[rows, cols], olds.at[i]) for i, state in enumerate((master, moment1, moment2))]
-    copy_all(views(whole, pieces, lax.axis_index("c")) + states, sems)
+    copies = [pltpu.make_async_copy(a, b, sems.at[i]) for i, (a, b) in enumerate(states)]
+    for copy in copies:
+        copy.start()
+    copy_all(views(whole, pieces, lax.axis_index("c")), pieces, sem)
+    for copy in copies:
+        copy.wait()
 
 
 def split_theirs(whole):
@@ -56,7 +58,7 @@
         out_shape=pltpu.VMEM(SHAPE, whole.dtype),
         in_specs=[ANY],
         out_specs=ANY,
-        scratch_shapes=[pltpu.SemaphoreType.DMA((COPIES,))],
+        scratch_shapes=[pltpu.SemaphoreType.DMA],
         compiler_params=SMALL,
         cost_estimate=pl.CostEstimate(flops=0, bytes_accessed=2 * whole.size, transcendentals=0),
         name="split_theirs",
@@ -69,7 +71,7 @@
         out_shape=[pltpu.VMEM(SHAPE, whole.dtype), pltpu.VMEM((STATES, LOW, COLS), jnp.float32)],
         in_specs=[ANY] * (1 + STATES),
         out_specs=[ANY] * 2,
-        scratch_shapes=[pltpu.SemaphoreType.DMA((COPIES + STATES,))],
+        scratch_shapes=[pltpu.SemaphoreType.DMA, pltpu.SemaphoreType.DMA((STATES,))],
         compiler_params=SMALL,
         cost_estimate=pl.CostEstimate(flops=0, bytes_accessed=2 * whole.size, transcendentals=0),
         name="split_mine",
@@ -77,10 +79,10 @@
 
 
 def place_kernel(of_other, *refs):
-    pieces, out, sems = refs[-3:]
+    pieces, out, sem = refs[-3:]
     core = lax.axis_index("c")
     pairs = views(out, pieces, 1 - core if of_other else core)
-    copy_all([(b, a) for a, b in pairs], sems)
+    copy_all([(b, a) for a, b in pairs], pieces, sem)
 
 
 def place(of_other, pieces, half=()):
@@ -89,7 +91,7 @@
         out_shape=jax.ShapeDtypeStruct(WHOLE, pieces.dtype),
         in_specs=[ANY] * (len(half) + 1),
         out_specs=ANY,
-        scratch_shapes=[pltpu.SemaphoreType.DMA((COPIES,))],
+        scratch_shapes=[pltpu.SemaphoreType.DMA],
         input_output_aliases={0: 0} if half else {},
         compiler_params=SMALL,
         cost_estimate=pl.CostEstimate(flops=0, bytes_accessed=4 * pieces.size, transcendentals=0),

time: 119 us -> 119 us (level)
  no operation moved by 1% of the time
where the time goes in v10:
time: 119 us; the launch traced here: 118 us
  blocking collectives  71.4 us (60%)
  starting transfers between devices  25.5 us (21%)
  waiting for transfers between devices  11.3 us (9%)
  Pallas kernels  7.35 us (6%)
  other arithmetic  1.29 us (1%)
    all_to_all x2, blocking collectives, exchange(): lax.all_to_all(chunks.reshape(-1, ZH * ZM, LOW, COLS), BIG, 0, 0, tiled=T...  71.4 us
    ppermute x6, starting transfers between devices, partner(): return lax.ppermute(a, ('zh', 'zm'), [(i, i ^ m) for i in range(ZH * ZM)])  13 us
    ppermute x6, waiting for transfers between devices, partner(): return lax.ppermute(a, ('zh', 'zm'), [(i, i ^ m) for i in range(ZH * ZM)])  7.19 us
    ppermute x1, starting transfers between devices, per_device(): came = lax.ppermute(part, 'c', SWAP)  5.73 us
    all_to_all x1, starting transfers between devices, per_device(): lax.all_to_all(jnp.broadcast_to(grad, (XH * Y, LOW, COLS)), ('xh', 'y'),...  3.42 us
    ppermute x1, starting transfers between devices, per_device(): came = lax.ppermute(split_theirs(whole), 'c', SWAP)  3.33 us
    pallas_call x2, Pallas kernels, place(): pl.pallas_call(lambda *refs: place_kernel(of_other, *refs), out_shape=jax...  2.78 us
  transfers between devices with their start and end apart: 9, of which 6 were waited for; matrix products, arithmetic and copies ran while one was open for 0% of the time, Pallas kernels for 4%

profile of v10, /device:TPU:1, one launch (start us, length us, event | category | flops | bytes accessed | tf_op | source)
XLA Modules:
  0.0 118.5 jit_solution(12853795724406283831)
XLA Ops:
  0.6 1.8 %split_theirs.1 = bf16[2,4,2,2,2,2,8,1152]{7,6,5,4,3,2,1,0:T(8,128)(2,1)S(1)} custom-call(bf16[2,2,2,2,2,2,8,4608]{7,6,5,4,3,2,1,0:T(8,128)(2,1)} %bitcast.56), custom_call_target="tpu_custom_call" | custom-call | bytes 4718592 | tf_op jit(solution)/shard_map/split_theirs/pallas_call | solution.py:56
  2.4 3.3 %collective-permute-start = (bf16[2,4,2,2,2,2,8,1152]{7,6,5,4,3,2,1,0:T(8,128)(2,1)S(1)}, bf16[2,4,2,2,2,2,8,1152]{7,6,5,4,3,2,1,0:T(8,128)(2,1)S(1)}, u32[]{:S(2)}, u32[]{:S(2)}) collective-permute-start(bf16[2,4,2,2,2,2,8,1152]{7,6,5,4,3,2,1,0:T(8,128)(2,1)S(1)} %split_theirs.1), channel_id=1, source_target_pairs={{0,1},{1,0},{2,3},{3,2},{4,5},{5,4},{6,7},{7,6},{8,9},{9,8},{10,11... | collective-permute-start | bytes 7077896 | tf_op jit(solution)/shard_map/ppermute | solution.py:154
  5.7 1.8 %split_mine.1 = (bf16[2,4,2,2,2,2,8,1152]{7,6,5,4,3,2,1,0:T(8,128)(2,1)S(1)}, f32[3,8,1152]{2,1,0:T(8,128)S(1)}) custom-call(bf16[2,2,2,2,2,2,8,4608]{7,6,5,4,3,2,1,0:T(8,128)(2,1)} %bitcast.57, f32[16,4608]{1,0:T(8,128)} %refs_0_.1, f32[16,4608]{1,0:T(8,128)} %refs_1_.1, f32[16,4608]{1,0:T(8,128)} %refs_2_.1), custom_call_target="tpu_custom_call" | custom-call | bytes 4718592 | tf_op jit(solution)/shard_map/split_mine/pallas_call | solution.py:69
  7.5 2.4 %collective-permute-done = bf16[2,4,2,2,2,2,8,1152]{7,6,5,4,3,2,1,0:T(8,128)(2,1)S(1)} collective-permute-done((bf16[2,4,2,2,2,2,8,1152]{7,6,5,4,3,2,1,0:T(8,128)(2,1)S(1)}, bf16[2,4,2,2,2,2,8,1152]{7,6,5,4,3,2,1,0:T(8,128)(2,1)S(1)}, u32[]{:S(2)}, u32[]{:S(2)}) %collective-permute-start) | collective-permute-done | bytes 2359328 | tf_op jit(solution)/shard_map/ppermute | solution.py:154
  9.9 0.9 multiply_convert_fusion
  10.8 37.6 %all_to_all.15 = f16[32,4,8,1152]{3,2,1,0:T(8,128)(2,1)S(1)} all-to-all(f16[32,4,8,1152]{3,2,1,0:T(8,128)(2,1)S(1)} %bitcast.59), channel_id=1, replica_groups=mesh['xh'=2,'y'=4,'xl'=2,'zh'=2,'zm'=2,'zl'=2,'c'=2] {'xh','y','xl','zl'}, dimensions={0} | all-to-all | bytes 4718592 | tf_op jit(solution)/shard_map/all_to_all | solution.py:135
  48.4 0.3 convert_reduce_fusion
  48.8 3.1 %collective-permute-start.1 = (f16[8,1152]{1,0:T(8,128)(2,1)S(1)}, f16[8,1152]{1,0:T(8,128)(2,1)S(1)}, u32[]{:S(2)}, u32[]{:S(2)}) collective-permute-start(f16[8,1152]{1,0:T(8,128)(2,1)S(1)} %get-tuple-element.26), channel_id=1, source_target_pairs={{0,4},{4,0},{8,12},{12,8},{1,5},{5,1},{9,13},{13,9},{2,6},{6,2},{1... | collective-permute-start | bytes 55304 | tf_op jit(solution)/shard_map/ppermute | solution.py:139
  51.9 4.2 %collective-permute-start.2 = (f16[8,1152]{1,0:T(8,128)(2,1)S(1)}, f16[8,1152]{1,0:T(8,128)(2,1)S(1)}, u32[]{:S(2)}, u32[]{:S(2)}) collective-permute-start(f16[8,1152]{1,0:T(8,128)(2,1)S(1)} %get-tuple-element.28), channel_id=1, source_target_pairs={{0,8},{4,12},{8,0},{12,4},{1,9},{5,13},{9,1},{13,5},{2,10},{6,14},... | collective-permute-start | bytes 55304 | tf_op jit(solution)/shard_map/ppermute | solution.py:139
  56.1 2.4 %collective-permute-done.2 = f16[8,1152]{1,0:T(8,128)(2,1)S(1)} collective-permute-done((f16[8,1152]{1,0:T(8,128)(2,1)S(1)}, f16[8,1152]{1,0:T(8,128)(2,1)S(1)}, u32[]{:S(2)}, u32[]{:S(2)}) %collective-permute-start.2) | collective-permute-done | bytes 18464 | tf_op jit(solution)/shard_map/ppermute | solution.py:139
  58.5 2.6 %collective-permute-done.3 = f16[8,1152]{1,0:T(8,128)(2,1)S(1)} collective-permute-done((f16[8,1152]{1,0:T(8,128)(2,1)S(1)}, f16[8,1152]{1,0:T(8,128)(2,1)S(1)}, u32[]{:S(2)}, u32[]{:S(2)}) %collective-permute-start.3) | collective-permute-done | bytes 18464 | tf_op jit(solution)/shard_map/ppermute | solution.py:139
  61.2 0.7 broadcast_in_dim.6
  61.9 3.4 %all-to-all-start.1 = ((f32[8,8,1152]{2,1,0:T(8,128)}), f32[8,8,1152]{2,1,0:T(8,128)S(1)}, u32[]{:S(2)}, u32[]{:S(2)}) async-start(f32[8,8,1152]{2,1,0:T(8,128)} %broadcast_in_dim.6), calls=%async_computation.1 | async-start | bytes 589824 | tf_op jit(solution)/shard_map/all_to_all | solution.py:164
  65.3 1.0 collective-permute-start.4
  66.3 1.8 %collective-permute-start.5 = (bf16[8,1152]{1,0:T(8,128)(2,1)S(1)}, bf16[8,1152]{1,0:T(8,128)(2,1)S(1)}, u32[]{:S(2)}, u32[]{:S(2)}) collective-permute-start(bf16[8,1152]{1,0:T(8,128)(2,1)S(1)} %get-tuple-element.23), channel_id=1, source_target_pairs={{0,8},{4,12},{8,0},{12,4},{1,9},{5,13},{9,1},{13,5},{2,10},{6,14},... | collective-permute-start | bytes 55304 | tf_op jit(solution)/shard_map/ppermute | solution.py:139
  68.1 3.0 %collective-permute-start.6 = (bf16[8,1152]{1,0:T(8,128)(2,1)S(1)}, bf16[8,1152]{1,0:T(8,128)(2,1)S(1)}, u32[]{:S(2)}, u32[]{:S(2)}) collective-permute-start(bf16[8,1152]{1,0:T(8,128)(2,1)S(1)} %get-tuple-element.23), channel_id=1, source_target_pairs={{0,12},{4,8},{8,4},{12,0},{1,13},{5,9},{9,5},{13,1},{2,14},{6,10},... | collective-permute-start | bytes 55304 | tf_op jit(solution)/shard_map/ppermute | solution.py:139
  71.1 1.9 %collective-permute-done.5 = bf16[8,1152]{1,0:T(8,128)(2,1)S(1)} collective-permute-done((bf16[8,1152]{1,0:T(8,128)(2,1)S(1)}, bf16[8,1152]{1,0:T(8,128)(2,1)S(1)}, u32[]{:S(2)}, u32[]{:S(2)}) %collective-permute-start.5) | collective-permute-done | bytes 18464 | tf_op jit(solution)/shard_map/ppermute | solution.py:139
  73.0 0.2 collective-permute-done.6
  73.4 33.8 %all_to_all.16 = bf16[32,4,8,1152]{3,2,1,0:T(8,128)(2,1)S(1)} all-to-all(bf16[32,4,8,1152]{3,2,1,0:T(8,128)(2,1)S(1)} %broadcast_in_dim.7), channel_id=1, replica_groups=mesh['xh'=2,'y'=4,'xl'=2,'zh'=2,'zm'=2,'zl'=2,'c'=2] {'xh','y','xl','zl'}, dimensions={0} | all-to-all | bytes 4718592 | tf_op jit(solution)/shard_map/all_to_all | solution.py:135
  107.2 5.7 %collective-permute-start.7 = (bf16[2,4,2,2,2,2,8,1152]{7,6,5,4,3,2,1,0:T(8,128)(2,1)S(1)}, bf16[2,4,2,2,2,2,8,1152]{7,6,5,4,3,2,1,0:T(8,128)(2,1)S(1)}, u32[]{:S(2)}, u32[]{:S(2)}) collective-permute-start(bf16[2,4,2,2,2,2,8,1152]{7,6,5,4,3,2,1,0:T(8,128)(2,1)S(1)} %bitcast.54), channel_id=1, source_target_pairs={{0,1},{1,0},{2,3},{3,2},{4,5},{5,4},{6,7},{7,6},{8,9},{9,8},{10,11... | collective-permute-start | bytes 7077896 | tf_op jit(solution)/shard_map/ppermute | solution.py:169
  112.9 1.4 %place_mine.1.refs_0_ = bf16[2,2,2,2,2,2,8,4608]{7,6,5,4,3,2,1,0:T(8,128)(2,1)} custom-call(bf16[2,4,2,2,2,2,8,1152]{7,6,5,4,3,2,1,0:T(8,128)(2,1)S(1)} %bitcast.55), custom_call_target="tpu_custom_call" | custom-call | bytes 4718592 | tf_op jit(solution)/shard_map/place_mine/pallas_call | solution.py:89
  114.4 1.0 new_states.1
  115.4 1.7 %collective-permute-done.7.refs_1_ = bf16[2,4,2,2,2,2,8,1152]{7,6,5,4,3,2,1,0:T(8,128)(2,1)S(1)} collective-permute-done((bf16[2,4,2,2,2,2,8,1152]{7,6,5,4,3,2,1,0:T(8,128)(2,1)S(1)}, bf16[2,4,2,2,2,2,8,1152]{7,6,5,4,3,2,1,0:T(8,128)(2,1)S(1)}, u32[]{:S(2)}, u32[]{:S(2)}) %collective-permute-start.7) | collective-permute-done | bytes 2359328 | tf_op jit(solution)/shard_map/ppermute | solution.py:169
  117.1 1.4 %place_theirs.1 = bf16[2,2,2,2,2,2,8,4608]{7,6,5,4,3,2,1,0:T(8,128)(2,1)} custom-call(bf16[2,2,2,2,2,2,8,4608]{7,6,5,4,3,2,1,0:T(8,128)(2,1)} %place_mine.1.refs_0_, bf16[2,4,2,2,2,2,8,1152]{7,6,5,4,3,2,1,0:T(8,128)(2,1)S(1)} %collective-permute-done.7.refs_1_), custom_call_target="tpu_custom_call", output_to_operand_aliasing={{}: (0, {})} | custom-call | bytes 4718592 | tf_op jit(solution)/shard_map/place_theirs/pallas_call | solution.py:89
  (15 shorter events, 0.3 us)
Async XLA Ops:
  2.4 7.5 %collective-permute-start = (bf16[2,4,2,2,2,2,8,1152]{7,6,5,4,3,2,1,0:T(8,128)(2,1)S(1)}, bf16[2,4,2,2,2,2,8,1152]{7,6,5,4,3,2,1,0:T(8,128)(2,1)S(1)}, u32[]{:S(2)}, u32[]{:S(2)}) collective-permute-start(bf16[2,4,2,2,2,2,8,1152]{7,6,5,4,3,2,1,0:T(8,128)(2,1)S(1)} %split_theirs.1), channel_id=1, source_target_pairs={{0,1},{1,0},{2,3},{3,2},{4,5},{5,4},{6,7},{7,6},{8,9},{9,8},{10,11... | collective-permute-start | bytes 7077896 | tf_op jit(solution)/shard_map/ppermute | solution.py:154
  48.8 7.3 %collective-permute-start.1 = (f16[8,1152]{1,0:T(8,128)(2,1)S(1)}, f16[8,1152]{1,0:T(8,128)(2,1)S(1)}, u32[]{:S(2)}, u32[]{:S(2)}) collective-permute-start(f16[8,1152]{1,0:T(8,128)(2,1)S(1)} %get-tuple-element.26), channel_id=1, source_target_pairs={{0,4},{4,0},{8,12},{12,8},{1,5},{5,1},{9,13},{13,9},{2,6},{6,2},{1... | collective-permute-start | bytes 55304 | tf_op jit(solution)/shard_map/ppermute | solution.py:139
  51.9 6.6 %collective-permute-start.2 = (f16[8,1152]{1,0:T(8,128)(2,1)S(1)}, f16[8,1152]{1,0:T(8,128)(2,1)S(1)}, u32[]{:S(2)}, u32[]{:S(2)}) collective-permute-start(f16[8,1152]{1,0:T(8,128)(2,1)S(1)} %get-tuple-element.28), channel_id=1, source_target_pairs={{0,8},{4,12},{8,0},{12,4},{1,9},{5,13},{9,1},{13,5},{2,10},{6,14},... | collective-permute-start | bytes 55304 | tf_op jit(solution)/shard_map/ppermute | solution.py:139
  56.1 5.0 %collective-permute-start.3 = (f16[8,1152]{1,0:T(8,128)(2,1)S(1)}, f16[8,1152]{1,0:T(8,128)(2,1)S(1)}, u32[]{:S(2)}, u32[]{:S(2)}) collective-permute-start(f16[8,1152]{1,0:T(8,128)(2,1)S(1)} %get-tuple-element.27), channel_id=1, source_target_pairs={{0,12},{4,8},{8,4},{12,0},{1,13},{5,9},{9,5},{13,1},{2,14},{6,10},... | collective-permute-start | bytes 55304 | tf_op jit(solution)/shard_map/ppermute | solution.py:139
  61.9 11.4 %all-to-all-start.1 = ((f32[8,8,1152]{2,1,0:T(8,128)}), f32[8,8,1152]{2,1,0:T(8,128)S(1)}, u32[]{:S(2)}, u32[]{:S(2)}) async-start(f32[8,8,1152]{2,1,0:T(8,128)} %broadcast_in_dim.6), calls=%async_computation.1 | async-start | bytes 589824 | tf_op jit(solution)/shard_map/all_to_all | solution.py:164
  65.3 5.7 %collective-permute-start.4 = (bf16[8,1152]{1,0:T(8,128)(2,1)S(1)}, bf16[8,1152]{1,0:T(8,128)(2,1)S(1)}, u32[]{:S(2)}, u32[]{:S(2)}) collective-permute-start(bf16[8,1152]{1,0:T(8,128)(2,1)S(1)} %get-tuple-element.23), channel_id=1, source_target_pairs={{0,4},{4,0},{8,12},{12,8},{1,5},{5,1},{9,13},{13,9},{2,6},{6,2},{1... | collective-permute-start | bytes 55304 | tf_op jit(solution)/shard_map/ppermute | solution.py:139
  66.3 6.7 %collective-permute-start.5 = (bf16[8,1152]{1,0:T(8,128)(2,1)S(1)}, bf16[8,1152]{1,0:T(8,128)(2,1)S(1)}, u32[]{:S(2)}, u32[]{:S(2)}) collective-permute-start(bf16[8,1152]{1,0:T(8,128)(2,1)S(1)} %get-tuple-element.23), channel_id=1, source_target_pairs={{0,8},{4,12},{8,0},{12,4},{1,9},{5,13},{9,1},{13,5},{2,10},{6,14},... | collective-permute-start | bytes 55304 | tf_op jit(solution)/shard_map/ppermute | solution.py:139
  68.1 5.2 %collective-permute-start.6 = (bf16[8,1152]{1,0:T(8,128)(2,1)S(1)}, bf16[8,1152]{1,0:T(8,128)(2,1)S(1)}, u32[]{:S(2)}, u32[]{:S(2)}) collective-permute-start(bf16[8,1152]{1,0:T(8,128)(2,1)S(1)} %get-tuple-element.23), channel_id=1, source_target_pairs={{0,12},{4,8},{8,4},{12,0},{1,13},{5,9},{9,5},{13,1},{2,14},{6,10},... | collective-permute-start | bytes 55304 | tf_op jit(solution)/shard_map/ppermute | solution.py:139
  107.2 7.1 %copy-start = (f32[16,4608]{1,0:T(8,128)S(1)}, f32[16,4608]{1,0:T(8,128)}, u32[]{:S(2)}) copy-start(f32[16,4608]{1,0:T(8,128)} %refs_0_.1) | copy-start | bytes 884740
  107.2 7.1 %copy-start.1 = (f32[16,4608]{1,0:T(8,128)S(1)}, f32[16,4608]{1,0:T(8,128)}, u32[]{:S(2)}) copy-start(f32[16,4608]{1,0:T(8,128)} %refs_1_.1) | copy-start | bytes 884740
  107.2 7.2 %copy-start.2 = (f32[16,4608]{1,0:T(8,128)S(1)}, f32[16,4608]{1,0:T(8,128)}, u32[]{:S(2)}) copy-start(f32[16,4608]{1,0:T(8,128)} %refs_2_.1) | copy-start | bytes 884740
  107.2 9.9 %collective-permute-start.7 = (bf16[2,4,2,2,2,2,8,1152]{7,6,5,4,3,2,1,0:T(8,128)(2,1)S(1)}, bf16[2,4,2,2,2,2,8,1152]{7,6,5,4,3,2,1,0:T(8,128)(2,1)S(1)}, u32[]{:S(2)}, u32[]{:S(2)}) collective-permute-start(bf16[2,4,2,2,2,2,8,1152]{7,6,5,4,3,2,1,0:T(8,128)(2,1)S(1)} %bitcast.54), channel_id=1, source_target_pairs={{0,1},{1,0},{2,3},{3,2},{4,5},{5,4},{6,7},{7,6},{8,9},{9,8},{10,11... | collective-permute-start | bytes 7077896 | tf_op jit(solution)/shard_map/ppermute | solution.py:169
